TPU v7x, 32 devices: a whole 2x2x4 slice. The times are simulated.
32 devices in a mesh: fsdp: 8 (over y, x, core), replica: 4 (over z).
Axes of the slice: x: 2, y: 2, z: 4, core: 2. Of those that a mesh axis runs over, the one named last changes fastest.
Arguments:
- tokens: bfloat16 [6144, 2048], P(('fsdp', 'replica')), may hold values from -6 to 6
- cotangent: bfloat16 [6144, 2048], P(('fsdp', 'replica')), may hold values from -6 to 6
- w_qkv: bfloat16 [2048, 4096], P('fsdp'), may hold values from -0.125 to 0.125
- w_out: bfloat16 [2048, 2048], P('fsdp'), may hold values from -0.375 to 0.375
- w_gate: bfloat16 [2048, 6144], P('fsdp'), may hold values from -0.125 to 0.125
- w_up: bfloat16 [2048, 6144], P('fsdp'), may hold values from -0.125 to 0.125
- w_down_t: bfloat16 [2048, 6144], P('fsdp'), may hold values from -0.078125 to 0.078125
- gain_attn: float32 [2048], replicated, may hold values from 0.5 to 1.5
- gain_mlp: float32 [2048], replicated, may hold values from 0.5 to 1.5
- gain_query: float32 [128], replicated, may hold values from 0.25 to 1.75
- gain_key: float32 [128], replicated, may hold values from 0.25 to 1.75
- dealt_lens: int32 [8, 4, 4], P('fsdp'), may hold values from 1 to 96, 192 in all within a row
- seq_order: int32 [8, 16], P('fsdp'), may hold values from 0 to 15, each once within a row
Outputs:
- output: bfloat16 [6144, 2048], P(('fsdp', 'replica'))
- input_grad: bfloat16 [6144, 2048], P(('fsdp', 'replica'))
- grad_qkv: float32 [2048, 4096], P('fsdp')
- grad_out: float32 [2048, 2048], P('fsdp')
- grad_gate: float32 [2048, 6144], P('fsdp')
- grad_up: float32 [2048, 6144], P('fsdp')
- grad_down_t: float32 [2048, 6144], P('fsdp')
- grad_gain_attn: float32 [2048], replicated
- grad_gain_mlp: float32 [2048], replicated
- grad_gain_query: float32 [128], replicated
- grad_gain_key: float32 [128], replicated
Inputs may be any that keep to these rules, and one draw needn't show every extreme that they name: Each row dealt_lens[f, r, :] sums to 192: the sequences that device r of group f receives, in its order. The longest sequence of every device has exactly 96 tokens. Each row seq_order[f, :] is a permutation; entry r * 4 + s is the place in the group's initial order of device r's s-th sequence.
All inputs are finite; a program needn't handle non-finite values.
Results may differ from a plain program's by a relative error of at most 0.02.
Values may be sent and summed in bfloat16 or wider, within the bound.
A program may use at most 640 MiB of HBM per device.

v0:
```python
import jax
import jax.numpy as jnp
from jax import lax
from jax.sharding import PartitionSpec as P

QUERY_HEADS = 16
KEY_VALUE_HEADS = 8
HEAD_WIDTH = 128


EPSILON = 1e-06
ROPE_BASE = 1000000.0
NEG_FILL = -1e30


def dot_rows(left, right):
    return lax.dot_general(
        left, right, (((0,), (0,)), ((), ())), preferred_element_type=jnp.float32
    )


def dot_cols(left, right):
    return lax.dot_general(
        left, right, (((1,), (1,)), ((), ())), preferred_element_type=jnp.float32
    )


def rope_tables(positions, head_size):
    half_size = head_size // 2
    steps_up = jnp.arange(half_size, dtype=jnp.float32)
    inverse = ROPE_BASE ** (-(2.0 * steps_up) / head_size)
    angles = positions.astype(jnp.float32)[:, None] * inverse[None, :]
    return (jnp.cos(angles)[:, None, :], jnp.sin(angles)[:, None, :])


def rotate(values, cosine, sine):
    half_size = values.shape[-1] // 2
    first = values[..., :half_size]
    second = values[..., half_size:]
    return jnp.concatenate(
        [first * cosine - second * sine, second * cosine + first * sine], axis=-1
    )


def rotate_back(grads, cosine, sine):
    half_size = grads.shape[-1] // 2
    first = grads[..., :half_size]
    second = grads[..., half_size:]
    return jnp.concatenate(
        [first * cosine + second * sine, second * cosine - first * sine], axis=-1
    )


def dealt_index(own_lens, own_starts, token_count):
    local_end = jnp.cumsum(own_lens)
    local_start = local_end - own_lens
    row_index = jnp.arange(token_count, dtype=jnp.int32)
    segment_index = jnp.sum((row_index[:, None] >= local_end[None, :]).astype(jnp.int32), axis=1)
    one_hot = (
        segment_index[:, None] == jnp.arange(own_lens.shape[0], dtype=jnp.int32)[None, :]
    ).astype(jnp.int32)
    positions = row_index - jnp.sum(one_hot * local_start[None, :], axis=1)
    source = jnp.sum(one_hot * own_starts[None, :], axis=1) + positions
    return (segment_index, positions, source)


def group_starts(flat_lens, ranks):
    earlier = (ranks[:, None] < ranks[None, :]).astype(jnp.int32)
    return jnp.sum(flat_lens[:, None] * earlier, axis=0)


def masked_scores(query_grouped, key_reduced, key_mask):
    scores = jnp.einsum(
        "qkgd,tkd->kgqt", query_grouped, key_reduced, preferred_element_type=jnp.float32
    ) * HEAD_WIDTH ** (-0.5)
    return jnp.where(key_mask, scores, NEG_FILL)


def norm_back(d_normed, normed, rms):
    return rms * (d_normed - normed * jnp.mean(d_normed * normed, axis=-1, keepdims=True))


def per_device(
    tokens,
    cotangent,
    w_qkv,
    w_out,
    w_gate,
    w_up,
    w_down_t,
    gain_attn,
    gain_mlp,
    gain_query,
    gain_key,
    dealt_lens,
    seq_order,
):
    token_count = tokens.shape[0]
    model_width = tokens.shape[1]
    per_dev = dealt_lens.shape[2]
    query_group_width = QUERY_HEADS // KEY_VALUE_HEADS
    device = lax.axis_index("replica")
    flat_lens = dealt_lens[0].reshape(-1)
    starts = group_starts(flat_lens, seq_order[0])
    own_lens = lax.dynamic_slice_in_dim(flat_lens, device * per_dev, per_dev)
    own_starts = lax.dynamic_slice_in_dim(starts, device * per_dev, per_dev)
    segment_index, positions, source = dealt_index(own_lens, own_starts, token_count)
    group_tokens, group_cot = (
        lax.all_gather(tokens, "replica", axis=0, tiled=True),
        lax.all_gather(cotangent, "replica", axis=0, tiled=True),
    )
    inputs = jnp.take(group_tokens, source, axis=0).astype(jnp.float32)
    grad_rows = jnp.take(group_cot, source, axis=0).astype(jnp.float32)
    wqkv_full, wout_full = (
        lax.all_gather(w_qkv, "fsdp", axis=0, tiled=True),
        lax.all_gather(w_out, "fsdp", axis=0, tiled=True),
    )
    gate_full, up_full, down_full = (
        lax.all_gather(w_gate, "fsdp", axis=0, tiled=True),
        lax.all_gather(w_up, "fsdp", axis=0, tiled=True),
        lax.all_gather(w_down_t, "fsdp", axis=0, tiled=True),
    )
    rms_one = lax.rsqrt(jnp.mean(inputs * inputs, axis=1, keepdims=True) + EPSILON)
    normed_one = inputs * rms_one
    n1_low = (normed_one * gain_attn).astype(jnp.bfloat16)
    projected_rows = jnp.dot(n1_low, wqkv_full, preferred_element_type=jnp.float32)
    query_width = QUERY_HEADS * HEAD_WIDTH
    key_width = KEY_VALUE_HEADS * HEAD_WIDTH
    query_rows = projected_rows[:, :query_width].reshape(token_count, QUERY_HEADS, HEAD_WIDTH)
    key_rows_unnormed = projected_rows[:, query_width : query_width + key_width].reshape(
        token_count, KEY_VALUE_HEADS, HEAD_WIDTH
    )
    value_rows_unnormed = projected_rows[:, query_width + key_width :].reshape(
        token_count, KEY_VALUE_HEADS, HEAD_WIDTH
    )
    rms_q = lax.rsqrt(jnp.mean(query_rows * query_rows, axis=2, keepdims=True) + EPSILON)
    q_hat = query_rows * rms_q
    rms_k = lax.rsqrt(
        jnp.mean(key_rows_unnormed * key_rows_unnormed, axis=2, keepdims=True) + EPSILON
    )
    k_hat = key_rows_unnormed * rms_k
    cosine, sine = rope_tables(positions, HEAD_WIDTH)
    query_reduced = rotate(q_hat * gain_query, cosine, sine).astype(jnp.bfloat16)
    key_reduced = rotate(k_hat * gain_key, cosine, sine).astype(jnp.bfloat16)
    value_reduced = value_rows_unnormed.astype(jnp.bfloat16)
    query_grouped = query_reduced.reshape(
        token_count, KEY_VALUE_HEADS, query_group_width, HEAD_WIDTH
    )
    row_index = jnp.arange(token_count, dtype=jnp.int32)
    key_mask = (segment_index[:, None] == segment_index[None, :]) & (
        row_index[None, :] <= row_index[:, None]
    )
    scores = masked_scores(query_grouped, key_reduced, key_mask)
    row_top = jnp.max(scores, axis=3, keepdims=True)
    exp_terms = jnp.exp(scores - row_top)
    row_total = jnp.sum(exp_terms, axis=3, keepdims=True)
    log_total = row_top + jnp.log(row_total)
    probs_low = (exp_terms / row_total).astype(jnp.bfloat16)
    context_rows = jnp.einsum(
        "kgqt,tkd->qkgd", probs_low, value_reduced, preferred_element_type=jnp.float32
    )
    ctx_low = context_rows.reshape(token_count, QUERY_HEADS * HEAD_WIDTH).astype(jnp.bfloat16)
    resid = inputs + jnp.dot(ctx_low, wout_full, preferred_element_type=jnp.float32)
    rms_two = lax.rsqrt(jnp.mean(resid * resid, axis=1, keepdims=True) + EPSILON)
    normed_two = resid * rms_two
    n2_low = (normed_two * gain_mlp).astype(jnp.bfloat16)
    gate_proj = jnp.dot(n2_low, gate_full, preferred_element_type=jnp.float32)
    up_proj = jnp.dot(n2_low, up_full, preferred_element_type=jnp.float32)
    sigmoid_gate = jax.nn.sigmoid(gate_proj)
    silu_gate = gate_proj * sigmoid_gate
    act_low = (silu_gate * up_proj).astype(jnp.bfloat16)
    output = resid + dot_cols(act_low, down_full)
    gate_back, up_back, down_back = (
        lax.all_gather(w_gate, "fsdp", axis=0, tiled=True),
        lax.all_gather(w_up, "fsdp", axis=0, tiled=True),
        lax.all_gather(w_down_t, "fsdp", axis=0, tiled=True),
    )
    dm_low = grad_rows.astype(jnp.bfloat16)
    d_act = jnp.dot(dm_low, down_back, preferred_element_type=jnp.float32)
    d_gate_low = (d_act * up_proj * sigmoid_gate * (1.0 + gate_proj * (1.0 - sigmoid_gate))).astype(
        jnp.bfloat16
    )
    d_up_low = (d_act * silu_gate).astype(jnp.bfloat16)
    mlp_shard = lax.psum_scatter(
        jnp.concatenate(
            [dot_rows(n2_low, d_gate_low), dot_rows(n2_low, d_up_low), dot_rows(dm_low, act_low)],
            axis=1,
        ).astype(jnp.bfloat16),
        "fsdp",
        scatter_dimension=0,
        tiled=True,
    )
    d_n2 = dot_cols(d_gate_low, gate_back) + dot_cols(d_up_low, up_back)
    d_gain_mlp = jnp.sum(d_n2 * normed_two, axis=0)
    d_resid = grad_rows + norm_back(d_n2 * gain_mlp, normed_two, rms_two)
    wqkv_back, wout_back = (
        lax.all_gather(w_qkv, "fsdp", axis=0, tiled=True),
        lax.all_gather(w_out, "fsdp", axis=0, tiled=True),
    )
    do_low = d_resid.astype(jnp.bfloat16)
    context_grad_reduced = dot_cols(do_low, wout_back).astype(jnp.bfloat16)
    context_grad_grouped = context_grad_reduced.reshape(
        token_count, KEY_VALUE_HEADS, query_group_width, HEAD_WIDTH
    )
    probs_back = jnp.exp(masked_scores(query_grouped, key_reduced, key_mask) - log_total)
    probs_back_low = probs_back.astype(jnp.bfloat16)
    d_value = jnp.einsum(
        "kgqt,qkgd->tkd", probs_back_low, context_grad_grouped, preferred_element_type=jnp.float32
    )
    d_probs = jnp.einsum(
        "qkgd,tkd->kgqt", context_grad_grouped, value_reduced, preferred_element_type=jnp.float32
    )
    delta = jnp.sum(probs_back * d_probs, axis=3, keepdims=True)
    d_scores_low = (probs_back * (d_probs - delta)).astype(jnp.bfloat16)
    d_query = jnp.einsum(
        "kgqt,tkd->qkgd", d_scores_low, key_reduced, preferred_element_type=jnp.float32
    ).reshape(token_count, QUERY_HEADS, HEAD_WIDTH) * HEAD_WIDTH ** (-0.5)
    d_key = jnp.einsum(
        "kgqt,qkgd->tkd", d_scores_low, query_grouped, preferred_element_type=jnp.float32
    ) * HEAD_WIDTH ** (-0.5)
    dq_gained = rotate_back(d_query, cosine, sine)
    dk_gained = rotate_back(d_key, cosine, sine)
    d_gain_query = jnp.sum(dq_gained * q_hat, axis=(0, 1))
    d_gain_key = jnp.sum(dk_gained * k_hat, axis=(0, 1))
    d_queries = norm_back(dq_gained * gain_query, q_hat, rms_q)
    d_keys = norm_back(dk_gained * gain_key, k_hat, rms_k)
    d_qkv_low = jnp.concatenate(
        [
            d_queries.reshape(token_count, query_width),
            d_keys.reshape(token_count, key_width),
            d_value.reshape(token_count, key_width),
        ],
        axis=1,
    ).astype(jnp.bfloat16)
    attn_shard = lax.psum_scatter(
        jnp.concatenate([dot_rows(n1_low, d_qkv_low), dot_rows(ctx_low, do_low)], axis=1).astype(
            jnp.bfloat16
        ),
        "fsdp",
        scatter_dimension=0,
        tiled=True,
    )
    d_n1 = dot_cols(d_qkv_low, wqkv_back)
    d_gain_attn = jnp.sum(d_n1 * normed_one, axis=0)
    d_inputs = d_resid + norm_back(d_n1 * gain_attn, normed_one, rms_one)
    attn_sum, mlp_sum = (
        lax.psum(attn_shard, "replica").astype(jnp.float32),
        lax.psum(mlp_shard, "replica").astype(jnp.float32),
    )
    gain_attn_sum, gain_mlp_sum, gain_query_sum, gain_key_sum = lax.psum(
        (d_gain_attn, d_gain_mlp, d_gain_query, d_gain_key), ("fsdp", "replica")
    )
    rows_total = group_tokens.shape[0]
    blank = jnp.zeros((rows_total, model_width), jnp.float32)
    back_out = blank.at[source].set(output)
    back_grad = blank.at[source].set(d_inputs)
    own_out, own_grad = (
        lax.psum_scatter(
            back_out.astype(jnp.bfloat16), "replica", scatter_dimension=0, tiled=True
        ).astype(jnp.float32),
        lax.psum_scatter(
            back_grad.astype(jnp.bfloat16), "replica", scatter_dimension=0, tiled=True
        ).astype(jnp.float32),
    )
    out_low = own_out.astype(jnp.bfloat16)
    grad_low = own_grad.astype(jnp.bfloat16)
    qkv_width = wqkv_full.shape[1]
    ff_width = gate_full.shape[1]
    return (
        out_low,
        grad_low,
        attn_sum[:, :qkv_width],
        attn_sum[:, qkv_width:],
        mlp_sum[:, :ff_width],
        mlp_sum[:, ff_width : 2 * ff_width],
        mlp_sum[:, 2 * ff_width :],
        gain_attn_sum,
        gain_mlp_sum,
        gain_query_sum,
        gain_key_sum,
    )


def solution(mesh):
    return jax.shard_map(
        per_device,
        mesh=mesh,
        in_specs=(
            P(("fsdp", "replica"), None),
            P(("fsdp", "replica"), None),
            P("fsdp", None),
            P("fsdp", None),
            P("fsdp", None),
            P("fsdp", None),
            P("fsdp", None),
            P(),
            P(),
            P(),
            P(),
            P("fsdp", None, None),
            P("fsdp", None),
        ),
        out_specs=(
            P(("fsdp", "replica"), None),
            P(("fsdp", "replica"), None),
            P("fsdp", None),
            P("fsdp", None),
            P("fsdp", None),
            P("fsdp", None),
            P("fsdp", None),
            P(),
            P(),
            P(),
            P(),
        ),
        check_vma=False,
    )
```

profile of v0, /device:TPU:0, one launch (start us, length us, event | category | flops | bytes accessed | tf_op | source)
XLA Modules:
  0.0 1930.8 jit_solution(11148136693560359899)
XLA Ops:
  15.2 60.6 %all-gather.8.cloned.1.call-done = bf16[768,2048]{1,0:T(8,128)(2,1)} async-done(((bf16[192,2048]{1,0:T(8,128)(2,1)}), bf16[768,2048]{1,0:T(8,128)(2,1)}) %all-gather.8.cloned.1.call-update) | async-done | bytes 3145744 | tf_op jit(solution)/shard_map/all_gather | solution.py:109
  75.8 4.2 gather_fusion
  80.0 59.5 %all-gather.20.cloned.1.call-done = bf16[768,2048]{1,0:T(8,128)(2,1)} async-done(((bf16[192,2048]{1,0:T(8,128)(2,1)}), bf16[768,2048]{1,0:T(8,128)(2,1)}) %all-gather.20.cloned.1.call-update) | async-done | bytes 3145744 | tf_op jit(solution)/shard_map/all_gather | solution.py:110
  139.6 5.1 gather_fusion.1
  145.0 85.0 %all-gather.10.cloned.1.call-done = bf16[2048,4096]{1,0:T(8,128)(2,1)} async-done(((bf16[256,4096]{1,0:T(8,128)(2,1)}), bf16[2048,4096]{1,0:T(8,128)(2,1)}) %all-gather.10.cloned.1.call-update) | async-done | bytes 16777232 | tf_op jit(solution)/shard_map/all_gather | solution.py:115
  230.0 7.9 fusion.63
  245.6 2.6 fusion.75
  250.1 1.7 copy.118
  251.8 3.4 convert_element_type.92
  255.2 31.0 %all-gather.12.cloned.1.call-done = bf16[2048,2048]{1,0:T(8,128)(2,1)} async-done(((bf16[256,2048]{1,0:T(8,128)(2,1)}), bf16[2048,2048]{1,0:T(8,128)(2,1)}) %all-gather.12.cloned.1.call-update) | async-done | bytes 8388624 | tf_op jit(solution)/shard_map/all_gather | solution.py:116
  286.2 5.7 multiply_reduce_fusion.3
  294.1 119.1 %all-gather.16.cloned.1.call-done = bf16[2048,6144]{1,0:T(8,128)(2,1)} async-done(((bf16[256,6144]{1,0:T(8,128)(2,1)}), bf16[2048,6144]{1,0:T(8,128)(2,1)}) %all-gather.16.cloned.1.call-update) | async-done | bytes 25165840 | tf_op jit(solution)/shard_map/all_gather | solution.py:120
  413.3 12.7 fusion.77
  426.0 114.4 %all-gather.14.cloned.1.call-done = bf16[2048,6144]{1,0:T(8,128)(2,1)} async-done(((bf16[256,6144]{1,0:T(8,128)(2,1)}), bf16[2048,6144]{1,0:T(8,128)(2,1)}) %all-gather.14.cloned.1.call-update) | async-done | bytes 25165840 | tf_op jit(solution)/shard_map/all_gather | solution.py:119
  540.4 12.4 fusion.76
  552.8 114.8 %all-gather.18.cloned.1.call-done = bf16[2048,6144]{1,0:T(8,128)(2,1)} async-done(((bf16[256,6144]{1,0:T(8,128)(2,1)}), bf16[2048,6144]{1,0:T(8,128)(2,1)}) %all-gather.18.cloned.1.call-update) | async-done | bytes 25165840 | tf_op jit(solution)/shard_map/all_gather | solution.py:121
  667.6 16.5 multiply_convert_fusion
  684.2 15.2 fusion.78
  699.3 16.4 multiply_reduce_fusion
  716.4 2.6 multiply_add_fusion.1
  720.1 7.2 convolution_convert_fusion.5
  727.3 3.4 reshape.252
  730.7 2.0 fusion.41
  737.6 5.7 convolution_convert_fusion.4
  746.6 1.9 multiply_add_fusion
  753.7 3.0 fusion.27
  756.7 9.5 convolution_convert_fusion.3
  766.3 17.1 pad_maximum_fusion.1
  784.5 18.9 convolution_convert_fusion.1
  803.4 16.9 convolution_convert_fusion.2
  820.3 14.4 convolution_convert_fusion
  834.8 51.6 %pad_maximum_fusion = bf16[2048,18432]{1,0:T(8,128)(2,1)} fusion(bf16[2048,6144]{1,0:T(8,128)(2,1)} %convolution_convert_fusion, bf16[2048,6144]{1,0:T(8,128)(2,1)} %convolution_convert_fusion.1, bf16[2048,6144]{1,0:T(8,128)(2,1)} %convolution_convert_fusion.2), kind=kLoop, calls=%fused_computation.4 | loop fusion | flops 226492416 | bytes 150994944 | tf_op jit(solution)/shard_map/concatenate | solution.py:185
  886.4 54.0 %reduce-scatter.9.cloned.1.call-done = bf16[256,6144]{1,0:T(8,128)(2,1)} async-done(((bf16[2048,6144]{1,0:T(8,128)(2,1)}), bf16[256,6144]{1,0:T(8,128)(2,1)}) %reduce-scatter.9.cloned.1.call-update) | async-done | bytes 3145744 | tf_op jit(solution)/shard_map/reduce_scatter | solution.py:235
  940.4 427.5 %reduce-scatter.11.cloned.1.call-done = bf16[256,18432]{1,0:T(8,128)(2,1)} async-done(((bf16[2048,18432]{1,0:T(8,128)(2,1)}), bf16[256,18432]{1,0:T(8,128)(2,1)}) %reduce-scatter.11.cloned.1.call-update) | async-done | bytes 9437200 | tf_op jit(solution)/shard_map/reduce_scatter | solution.py:184
  1369.4 13.4 fusion.20
  1383.4 6.1 scatter_custom_fusion.1
  1389.6 4.9 convert_element_type.103
  1395.9 14.0 convolution_add_fusion.2
  1409.9 4.9 scatter_custom_fusion
  1414.8 4.9 convert_element_type.95
  1420.4 47.3 %all-reduce = (f32[2048]{0:T(1024)}, f32[2048]{0:T(1024)}, f32[128]{0:T(128)}, f32[128]{0:T(128)}) all-reduce(f32[2048]{0:T(1024)S(1)} %copy-done.54, f32[2048]{0:T(1024)S(1)} %copy-done.53, f32[128]{0:T(128)S(1)} %bitcast_reduce_fusion, f32[128]{0:T(128)S(1)} %bitcast_reduce_fusion.1), channel_id=1, replica_groups=mesh['fsdp'=8,'replica'=4] {'fsdp','replica'}, use_global_device_ids=true, to_apply=%region_25.27 | all-reduce | flops 4352 | bytes 34816 | tf_op jit(solution)/shard_map/psum | solution.py:250
  1467.7 330.7 %all-reduce.4.cloned.1.call-done = (bf16[256,6144]{1,0:T(8,128)(2,1)}, bf16[256,18432]{1,0:T(8,128)(2,1)}) async-done(((bf16[256,6144]{1,0:T(8,128)(2,1)}, bf16[256,18432]{1,0:T(8,128)(2,1)}), (bf16[256,6144]{1,0:T(8,128)(2,1)}, bf16[256,18432]{1,0:T(8,128)(2,1)})) %all-reduce.4.cloned.1.call-update) | async-done | bytes 12582928 | tf_op jit(solution)/shard_map/psum | solution.py:247
  1798.4 2.9 slice.81
  1801.3 2.6 slice.80
  1803.9 1.7 copy-done
  1805.6 6.9 fusion.73
  1812.5 48.1 %reduce-scatter.7.cloned.1.call-done = bf16[192,2048]{1,0:T(8,128)(2,1)} async-done(((bf16[768,2048]{1,0:T(8,128)(2,1)}), bf16[192,2048]{1,0:T(8,128)(2,1)}) %reduce-scatter.7.cloned.1.call-update) | async-done | bytes 786448 | tf_op jit(solution)/shard_map/reduce_scatter | solution.py:261
  1860.6 63.1 %reduce-scatter.5.cloned.1.call-done = bf16[192,2048]{1,0:T(8,128)(2,1)} async-done(((bf16[768,2048]{1,0:T(8,128)(2,1)}), bf16[192,2048]{1,0:T(8,128)(2,1)}) %reduce-scatter.5.cloned.1.call-update) | async-done | bytes 786448 | tf_op jit(solution)/shard_map/reduce_scatter | solution.py:258
  (208 shorter events, 40.2 us)
Async XLA Ops:
  7.2 68.6 %all-gather.8.cloned.1.call-start = ((), (), s32[]{:S(2)}) async-start(), calls=%async_computation.4 | async-start | bytes 3932160 | tf_op jit(solution)/shard_map/all_gather | solution.py:109
  7.9 131.7 %all-gather.20.cloned.1.call-start = ((), (), s32[]{:S(2)}) async-start(), calls=%async_computation.11 | async-start | bytes 3932160 | tf_op jit(solution)/shard_map/all_gather | solution.py:110
  8.7 221.3 %all-gather.10.cloned.1.call-start = ((), (), s32[]{:S(2)}) async-start(), calls=%async_computation.5 | async-start | bytes 18874368 | tf_op jit(solution)/shard_map/all_gather | solution.py:115
  9.4 276.8 %all-gather.12.cloned.1.call-start = ((), (), s32[]{:S(2)}) async-start(), calls=%async_computation.6 | async-start | bytes 9437184 | tf_op jit(solution)/shard_map/all_gather | solution.py:116
  10.0 403.3 %all-gather.16.cloned.1.call-start = ((), (), s32[]{:S(2)}) async-start(), calls=%async_computation.8 | async-start | bytes 28311552 | tf_op jit(solution)/shard_map/all_gather | solution.py:120
  10.6 529.8 %all-gather.14.cloned.1.call-start = ((), (), s32[]{:S(2)}) async-start(), calls=%async_computation.7 | async-start | bytes 28311552 | tf_op jit(solution)/shard_map/all_gather | solution.py:119
  11.2 1.7 copy-start.55
  11.2 2.3 copy-start.57
  11.2 656.4 %all-gather.18.cloned.1.call-start = ((), (), s32[]{:S(2)}) async-start(), calls=%async_computation.9 | async-start | bytes 28311552 | tf_op jit(solution)/shard_map/all_gather | solution.py:121
  11.9 928.5 %reduce-scatter.9.cloned.1.call-start = ((), (), s32[]{:S(2)}) async-start(), calls=%async_computation.13 | async-start | bytes 28311552 | tf_op jit(solution)/shard_map/reduce_scatter | solution.py:235
  12.8 2.0 copy-start.51
  12.8 217.2 %copy-start.39 = (pred[192]{0:T(512)(128)(4,1)}, pred[192]{0:T(512)(128)(4,1)S(1)}, u32[]{:S(2)}) copy-start(pred[192]{0:T(512)(128)(4,1)S(1)} %get-tuple-element.26) | copy-start | bytes 580
  15.2 230.0 %copy-start.24 = (f32[192,64]{1,0:T(8,128)}, f32[192,64]{1,0:T(8,128)S(1)}, u32[]{:S(2)}) copy-start(f32[192,64]{1,0:T(8,128)S(1)} %get-tuple-element.52) | copy-start | bytes 147460
  15.2 230.0 %copy-start.26 = (f32[192,64]{1,0:T(8,128)}, f32[192,64]{1,0:T(8,128)S(1)}, u32[]{:S(2)}) copy-start(f32[192,64]{1,0:T(8,128)S(1)} %get-tuple-element.53) | copy-start | bytes 147460
  80.0 150.0 %copy-start.5 = (bf16[192,2048]{1,0:T(8,128)(2,1)}, bf16[192,2048]{1,0:T(8,128)(2,1)S(1)}, u32[]{:S(2)}) copy-start(bf16[192,2048]{1,0:T(8,128)(2,1)S(1)} %gather_fusion) | copy-start | bytes 2359300
  80.0 150.0 %copy-start.42 = (f32[2048]{0:T(1024)S(1)}, f32[2048]{0:T(1024)}, u32[]{:S(2)}) copy-start(f32[2048]{0:T(1024)} %param.22) | copy-start | bytes 24580
  145.0 92.9 %copy-start.46 = (f32[192]{0:T(256)}, f32[192]{0:T(256)S(1)}, u32[]{:S(2)}) copy-start(f32[192]{0:T(256)S(1)} %add_rsqrt_fusion.3) | copy-start | bytes 2308
  237.9 5.5 copy-start.9
  243.6 1.9 copy-start.11
  244.1 1.5 copy-start.35
  245.5 2.7 copy-start.19
  248.2 1.9 copy-start.33
  286.2 5.8 copy-start.34
  286.2 5.8 copy-start.38
  286.2 6.9 copy-start.41
  730.7 2.0 copy-start.13
  730.7 2.0 copy-start.29
  736.0 1.4 copy-start.4
  736.0 1.6 copy-start.18
  737.6 6.5 copy-start.25
  737.6 6.5 copy-start.27
  746.6 1.9 copy-start.2
  746.6 1.9 copy-start.31
  746.6 1.9 copy-start.58
  748.6 1.9 copy-start.10
  748.6 1.9 copy-start.48
  753.6 3.1 copy-start.6
  753.6 3.1 copy-start.40
  753.7 3.1 copy-start.43
  753.7 3.1 copy-start.47
  756.7 9.5 copy-start.21
  783.4 584.5 %reduce-scatter.11.cloned.1.call-start = ((), (), s32[]{:S(2)}) async-start(), calls=%async_computation.14 | async-start | bytes 84934656 | tf_op jit(solution)/shard_map/reduce_scatter | solution.py:184
  886.4 912.0 %all-reduce.4.cloned.1.call-start = ((), (), s32[]{:S(2)}) async-start(), calls=%async_computation.15 | async-start | bytes 25165824 | tf_op jit(solution)/shard_map/psum | solution.py:247
  1367.9 1.5 copy-start.22
  1367.9 492.7 %reduce-scatter.7.cloned.1.call-start = ((), (), s32[]{:S(2)}) async-start(), calls=%async_computation.12 | async-start | bytes 3932160 | tf_op jit(solution)/shard_map/reduce_scatter | solution.py:261
  1394.5 529.2 %reduce-scatter.5.cloned.1.call-start = ((), (), s32[]{:S(2)}) async-start(), calls=%async_computation.10 | async-start | bytes 3932160 | tf_op jit(solution)/shard_map/reduce_scatter | solution.py:258
  1798.4 2.9 copy-start.7
  1798.4 7.2 copy-start
  (25 other events, 27.0 us)
Sparse Core Ops, SparseCore 0:
  9.6 66.1 all-gather.7
  77.4 62.1 all-gather.19
  141.5 88.4 all-gather.9
  231.7 54.3 all-gather.11
  287.9 125.3 all-gather.15
  415.0 125.3 all-gather.13
  542.2 125.3 all-gather.17
  783.5 156.8 reduce-scatter.8
  944.1 423.7 reduce-scatter.10
  1370.5 427.8 all-reduce.3
  1801.4 59.1 reduce-scatter.6
  1863.4 60.2 reduce-scatter.4
where the time goes:
time: 1940 us; the launch traced here: 1930 us
  waiting for transfers between devices  1510 us (78%)
  matrix products  195 us (10%)
  other arithmetic  106 us (5%)
  local copies, waits for them, and re-layouts  54.3 us (3%)
  blocking collectives  47.3 us (2%)
    reduce_scatter x1, waiting for transfers between devices, per_device(): lax.psum_scatter(jnp.concatenate([dot_rows(n2_low, d_gate_low), dot_rows(...  427 us
    psum x1, waiting for transfers between devices, per_device(): lax.psum(attn_shard, 'replica').astype(jnp.float32)  331 us
    all_gather x1, waiting for transfers between devices, per_device(): lax.all_gather(w_up, 'fsdp', axis=0, tiled=True)  119 us
    all_gather x1, waiting for transfers between devices, per_device(): lax.all_gather(w_down_t, 'fsdp', axis=0, tiled=True)  115 us
    all_gather x1, waiting for transfers between devices, per_device(): lax.all_gather(w_gate, 'fsdp', axis=0, tiled=True)  114 us
    all_gather x1, waiting for transfers between devices, per_device(): lax.all_gather(w_qkv, 'fsdp', axis=0, tiled=True)  85 us
    dot_general x5, matrix products, dot_cols(): lax.dot_general(left, right, (((1,), (1,)), ((), ())), preferred_element_...  66.1 us
    dot_general x5, matrix products, dot_rows(): lax.dot_general(left, right, (((0,), (0,)), ((), ())), preferred_element_...  65.4 us
  transfers between devices with their start and end apart: 12, of which 12 were waited for; matrix products, arithmetic and copies ran while one was open for 12% of the time, Pallas kernels for 0%

commit v1 on v0

v1 whole, which is shorter than its diff:
```python
import jax
import jax.numpy as jnp
from jax import lax
from jax.sharding import PartitionSpec as P

QUERY_HEADS = 16
KEY_VALUE_HEADS = 8
HEAD_WIDTH = 128
LMAX = 96

EPSILON = 1e-06
ROPE_BASE = 1000000.0
NEG_FILL = -1e30
BF = jnp.bfloat16
F32 = jnp.float32


def dot(left, right):
    return jnp.dot(left, right, preferred_element_type=F32)


def dot_rows(left, right):
    return lax.dot_general(left, right, (((0,), (0,)), ((), ())), preferred_element_type=F32)


def dot_cols(left, right):
    return lax.dot_general(left, right, (((1,), (1,)), ((), ())), preferred_element_type=F32)


def rope_tables(positions):
    half_size = HEAD_WIDTH // 2
    steps_up = jnp.arange(half_size, dtype=F32)
    inverse = ROPE_BASE ** (-(2.0 * steps_up) / HEAD_WIDTH)
    angles = positions.astype(F32)[:, None] * inverse[None, :]
    return jnp.cos(angles), jnp.sin(angles)


def rotate(values, cosine, sine):
    half_size = HEAD_WIDTH // 2
    first, second = values[..., :half_size], values[..., half_size:]
    return jnp.concatenate([first * cosine - second * sine, second * cosine + first * sine], axis=-1)


def norm_back(d_normed, normed, rms):
    return rms * (d_normed - normed * jnp.mean(d_normed * normed, axis=-1, keepdims=True))


def row_positions(flat_lens, ranks, first_row, count):
    earlier = (ranks[:, None] < ranks[None, :]).astype(jnp.int32)
    starts = jnp.sum(flat_lens[:, None] * earlier, axis=0)
    rows = first_row + jnp.arange(count, dtype=jnp.int32)
    begun = jnp.where(starts[None, :] <= rows[:, None], starts[None, :], 0)
    return rows - jnp.max(begun, axis=1)


def per_device(
    n_replica, tokens, cotangent, w_qkv, w_out, w_gate, w_up, w_down_t,
    gain_attn, gain_mlp, gain_query, gain_key, dealt_lens, seq_order,
):
    rows, width = tokens.shape
    n_fsdp = width // w_qkv.shape[0]
    q_w = QUERY_HEADS * HEAD_WIDTH
    k_w = KEY_VALUE_HEADS * HEAD_WIDTH
    replica = lax.axis_index("replica")
    shared = n_fsdp // KEY_VALUE_HEADS
    heads = QUERY_HEADS // n_fsdp
    qw = heads * HEAD_WIDTH

    pos = row_positions(dealt_lens[0].reshape(-1), seq_order[0], replica * rows, rows)
    pos_all = lax.all_gather(pos, "fsdp", axis=0, tiled=True)

    def scatter_cols(w):
        return lax.all_to_all(w, "fsdp", split_axis=1, concat_axis=0, tiled=True)

    depth = w_qkv.shape[0]
    wq = w_qkv[:, :q_w].reshape(depth, n_fsdp, qw)
    wk = jnp.repeat(w_qkv[:, q_w:q_w + k_w].reshape(depth, KEY_VALUE_HEADS, HEAD_WIDTH), shared, axis=1)
    wv = jnp.repeat(w_qkv[:, q_w + k_w:].reshape(depth, KEY_VALUE_HEADS, HEAD_WIDTH), shared, axis=1)
    w_qkv_c = scatter_cols(jnp.concatenate([wq, wk, wv], axis=2).reshape(depth, -1))
    gate_c, up_c, down_c = scatter_cols(w_gate), scatter_cols(w_up), scatter_cols(w_down_t)

    def gather(a):
        return lax.all_gather(a, "fsdp", axis=0, tiled=True)

    def scatter_sum(a):
        return lax.psum_scatter(a.astype(BF), "fsdp", scatter_dimension=0, tiled=True).astype(F32)

    x = tokens.astype(F32)
    g = cotangent.astype(F32)
    r1 = lax.rsqrt(jnp.mean(x * x, axis=1, keepdims=True) + EPSILON)
    u1 = x * r1
    n1 = gather((u1 * gain_attn).astype(BF))
    g_all = gather(cotangent)
    total = n1.shape[0]

    proj = dot(n1, w_qkv_c)
    q_rows = proj[:, :qw].reshape(total, heads, HEAD_WIDTH)
    k_rows = proj[:, qw:qw + HEAD_WIDTH]
    v_low = proj[:, qw + HEAD_WIDTH:].astype(BF)
    rq = lax.rsqrt(jnp.mean(q_rows * q_rows, axis=2, keepdims=True) + EPSILON)
    q_hat = q_rows * rq
    rk = lax.rsqrt(jnp.mean(k_rows * k_rows, axis=1, keepdims=True) + EPSILON)
    k_hat = k_rows * rk
    cosine, sine = rope_tables(pos_all)
    q_low = rotate(q_hat * gain_query, cosine[:, None], sine[:, None]).astype(BF)
    k_low = rotate(k_hat * gain_key, cosine, sine).astype(BF)

    groups = n_fsdp
    halo = LMAX
    kv = jnp.concatenate([k_low, v_low], axis=1).reshape(groups, rows, 2 * HEAD_WIDTH)
    up_pairs = [(i, i + 1) for i in range(n_replica - 1)]
    down_pairs = [(i + 1, i) for i in range(n_replica - 1)]
    kv_before = lax.ppermute(kv[:, rows - halo:], "replica", up_pairs)
    kv_window = jnp.concatenate([kv_before, kv], axis=1)
    k_win, v_win = kv_window[..., :HEAD_WIDTH], kv_window[..., HEAD_WIDTH:]
    q_grp = q_low.reshape(groups, rows, heads, HEAD_WIDTH)
    pos_grp = pos_all.reshape(groups, rows)
    i_at = halo + jnp.arange(rows, dtype=jnp.int32)
    j_at = jnp.arange(halo + rows, dtype=jnp.int32)
    mask = (j_at[None, None, :] <= i_at[None, :, None]) & (
        j_at[None, None, :] >= i_at[None, :, None] - pos_grp[:, :, None])
    mask = mask[:, None]
    scale = HEAD_WIDTH ** (-0.5)
    scores = jnp.einsum("gqhd,gkd->ghqk", q_grp, k_win, preferred_element_type=F32) * scale
    scores = jnp.where(mask, scores, NEG_FILL)
    top = jnp.max(scores, axis=3, keepdims=True)
    terms = jnp.exp(scores - top)
    probs = terms / jnp.sum(terms, axis=3, keepdims=True)
    probs_low = probs.astype(BF)
    ctx = jnp.einsum("ghqk,gkd->gqhd", probs_low, v_win, preferred_element_type=F32)
    ctx_low = ctx.reshape(total, qw).astype(BF)
    h = x + scatter_sum(dot(ctx_low, w_out))

    r2 = lax.rsqrt(jnp.mean(h * h, axis=1, keepdims=True) + EPSILON)
    u2 = h * r2
    n2 = gather((u2 * gain_mlp).astype(BF))
    gate = dot(n2, gate_c)
    up = dot(n2, up_c)
    sg = jax.nn.sigmoid(gate)
    silu = gate * sg
    act = (silu * up).astype(BF)
    output = (h + scatter_sum(dot_cols(act, down_c))).astype(BF)

    d_act = dot(g_all, down_c)
    d_gate = (d_act * up * sg * (1.0 + gate * (1.0 - sg))).astype(BF)
    d_up = (d_act * silu).astype(BF)

    d_n2 = scatter_sum(dot_cols(d_gate, gate_c) + dot_cols(d_up, up_c))
    d_gain_mlp = jnp.sum(d_n2 * u2, axis=0)
    d_h = g + norm_back(d_n2 * gain_mlp, u2, r2)
    dh_all = gather(d_h.astype(BF))
    d_ctx = dot_cols(dh_all, w_out).astype(BF).reshape(groups, rows, heads, HEAD_WIDTH)
    d_v = jnp.einsum("ghqk,gqhd->gkd", probs_low, d_ctx, preferred_element_type=F32)
    d_p = jnp.einsum("gqhd,gkd->ghqk", d_ctx, v_win, preferred_element_type=F32)
    delta = jnp.sum(probs * d_p, axis=3, keepdims=True)
    d_s = (probs * (d_p - delta)).astype(BF)
    d_q = jnp.einsum("ghqk,gkd->gqhd", d_s, k_win, preferred_element_type=F32) * scale
    d_k = jnp.einsum("ghqk,gqhd->gkd", d_s, q_grp, preferred_element_type=F32) * scale
    d_kv = jnp.concatenate([d_k, d_v], axis=2)
    d_kv_after = lax.ppermute(d_kv[:, :halo].astype(BF), "replica", down_pairs).astype(F32)
    d_kv = d_kv[:, halo:]
    d_kv = jnp.concatenate([d_kv[:, :rows - halo], d_kv[:, rows - halo:] + d_kv_after], axis=1)
    d_k = d_kv[..., :HEAD_WIDTH].reshape(total, HEAD_WIDTH)
    d_v = d_kv[..., HEAD_WIDTH:].reshape(total, HEAD_WIDTH)
    d_q = d_q.reshape(total, heads, HEAD_WIDTH)
    dq_g = rotate(d_q, cosine[:, None], -sine[:, None])
    dk_g = rotate(d_k, cosine, -sine)
    d_gain_query = jnp.sum(dq_g * q_hat, axis=(0, 1))
    d_gain_key = jnp.sum(dk_g * k_hat, axis=0)
    dq = norm_back(dq_g * gain_query, q_hat, rq)
    dk = norm_back(dk_g * gain_key, k_hat, rk)
    d_proj = jnp.concatenate([dq.reshape(total, qw), dk, d_v], axis=1).astype(BF)
    d_n1 = scatter_sum(dot_cols(d_proj, w_qkv_c))
    d_gain_attn = jnp.sum(d_n1 * u1, axis=0)
    input_grad = (d_h + norm_back(d_n1 * gain_attn, u1, r1)).astype(BF)

    def reduce_cols(grad):
        share = grad.shape[1]
        low = grad.astype(BF).reshape(n_fsdp, n_replica, width // n_fsdp // n_replica, share)
        low = low.transpose(1, 0, 2, 3).reshape(width, share)
        part = lax.psum_scatter(low, "replica", scatter_dimension=0, tiled=True)
        part = lax.all_to_all(part.reshape(n_fsdp, -1, share), "fsdp", split_axis=0, concat_axis=1)
        whole = lax.all_gather(part, "replica", axis=0, tiled=True)
        return whole.astype(F32)

    def reduce_rows(grad):
        low = lax.psum_scatter(grad.astype(BF), "replica", scatter_dimension=0, tiled=True)
        return lax.all_gather(low, "replica", axis=0, tiled=True).astype(F32)

    g_down = reduce_cols(dot_rows(g_all, act)).reshape(depth, -1)
    g_gate = reduce_cols(dot_rows(n2, d_gate)).reshape(depth, -1)
    g_up = reduce_cols(dot_rows(n2, d_up)).reshape(depth, -1)
    g_out = reduce_rows(dot_rows(ctx_low, dh_all))
    g_qkv = reduce_cols(dot_rows(n1, d_proj))

    def of_key_heads(part):
        return jnp.sum(part.reshape(depth, KEY_VALUE_HEADS, shared, HEAD_WIDTH), axis=2).reshape(depth, k_w)

    g_qkv = jnp.concatenate([
        g_qkv[:, :, :qw].reshape(depth, q_w),
        of_key_heads(g_qkv[:, :, qw:qw + HEAD_WIDTH]),
        of_key_heads(g_qkv[:, :, qw + HEAD_WIDTH:])], axis=1)
    sums = lax.psum((d_gain_attn, d_gain_mlp, d_gain_query, d_gain_key), ("fsdp", "replica"))
    return (output, input_grad, g_qkv, g_out, g_gate, g_up, g_down) + tuple(sums)


def solution(mesh):
    n_replica = mesh.shape["replica"]

    def program(*args):
        return per_device(n_replica, *args)

    rows = P(("fsdp", "replica"), None)
    weight = P("fsdp", None)
    return jax.shard_map(
        program,
        mesh=mesh,
        in_specs=(rows, rows) + (weight,) * 5 + (P(),) * 4 + (P("fsdp", None, None), P("fsdp", None)),
        out_specs=(rows, rows) + (weight,) * 5 + (P(),) * 4,
        check_vma=False,
    )
```

time: 1940 us -> 1200 us (0.62)
  waiting for transfers between devices: 1510 us -> 690 us
  blocking collectives: 47.3 us -> 137 us
  local copies, waits for them, and re-layouts: 54.3 us -> 128 us
  matrix products: 195 us -> 127 us
  other arithmetic: 106 us -> 68.2 us
  starting transfers between devices: 0.64 us -> 26 us
    all_gather x7 -> x9, waiting for transfers between devices: 584 us -> 202 us  [the longest x4 172 us: reduce_cols(): whole = lax.all_gather(part, 'replica', axis=0, tiled=True)]
    psum x1 -> x0, waiting for transfers between devices: 331 us -> none  [per_device(): lax.psum(attn_shard, 'replica').astype(jnp.float32)]
    reduce_scatter x4 -> x9, waiting for transfers between devices: 593 us -> 343 us  [the longest x4 195 us: scatter_sum(): lax.psum_scatter(a.astype(BF), 'fsdp', scatter_dimension=0, tiled=True)]
    all_to_all x0 -> x4, waiting for transfers between devices: none -> 132 us  [scatter_cols(): return lax.all_to_all(w, 'fsdp', split_axis=1, concat_axis=0, tiled=True)]
    all_to_all x0 -> x4, blocking collectives: none -> 63 us  [reduce_cols(): lax.all_to_all(part.reshape(n_fsdp, -1, share), 'fsdp', split_axis=0, con...]
    concatenate x2 -> x5, other arithmetic: 68.7 us -> 7.28 us  [the longest x1 2.5 us: per_device(): jnp.concatenate([wq, wk, wv], axis=2).reshape(depth, -1)]
    unnamed x129 -> x126, local copies, waits for them, and re-layouts: 12.5 us -> 51.4 us
    unnamed x0 -> x1, blocking collectives: none -> 33.9 us
  transfers between devices with their start and end apart: 12 -> 24, of which waited for: 12 -> 19; matrix products, arithmetic and copies ran while one was open for 12% -> 21% of each run, Pallas kernels for 0% -> 0%
where the time goes in v1:
time: 1200 us; the launch traced here: 1190 us
  waiting for transfers between devices  690 us (58%)
  blocking collectives  137 us (11%)
  local copies, waits for them, and re-layouts  128 us (11%)
  matrix products  127 us (11%)
  other arithmetic  68.2 us (6%)
  starting transfers between devices  26 us (2%)
  between operations  16 us (1%)
    reduce_scatter x4, waiting for transfers between devices, scatter_sum(): lax.psum_scatter(a.astype(BF), 'fsdp', scatter_dimension=0, tiled=True)  195 us
    all_gather x4, waiting for transfers between devices, reduce_cols(): whole = lax.all_gather(part, 'replica', axis=0, tiled=True)  172 us
    reduce_scatter x4, waiting for transfers between devices, reduce_cols(): part = lax.psum_scatter(low, 'replica', scatter_dimension=0, tiled=True)  135 us
    all_to_all x4, waiting for transfers between devices, scatter_cols(): return lax.all_to_all(w, 'fsdp', split_axis=1, concat_axis=0, tiled=True)  132 us
    all_to_all x4, blocking collectives, reduce_cols(): lax.all_to_all(part.reshape(n_fsdp, -1, share), 'fsdp', split_axis=0, con...  63 us
    unnamed x126, local copies, waits for them, and re-layouts  51.4 us
    dot_general x5, matrix products, dot(): return jnp.dot(left, right, preferred_element_type=F32)  40 us
    psum x1, blocking collectives, per_device(): lax.psum((d_gain_attn, d_gain_mlp, d_gain_query, d_gain_key), ('fsdp', 'r...  40 us
  transfers between devices with their start and end apart: 24, of which 19 were waited for; matrix products, arithmetic and copies ran while one was open for 21% of the time, Pallas kernels for 0%

profile of v1, /device:TPU:0, one launch (start us, length us, event | category | flops | bytes accessed | tf_op | source)
XLA Modules:
  0.0 1191.7 jit_solution(7250412797753550780)
XLA Ops:
  17.5 5.3 all-to-all-start
  24.5 33.9 %all-reduce = s32[1536]{0:T(1024)S(1)} all-reduce(s32[1536]{0:T(1024)S(1)} %subtract_dynamic-update-slice_fusion), channel_id=1, replica_groups=mesh['fsdp'=8,'replica'=4] {'fsdp'}, use_global_device_ids=true, to_apply=%add | all-reduce | flops 1536 | bytes 12288
  63.8 13.4 %all-gather.14.cloned.1.call-done = bf16[1536,2048]{1,0:T(8,128)(2,1)} async-done(((bf16[192,2048]{1,0:T(8,128)(2,1)}), bf16[1536,2048]{1,0:T(8,128)(2,1)}) %all-gather.14.cloned.1.call-update) | async-done | bytes 6291472 | tf_op jit(solution)/shard_map/all_gather | solution.py:83
  77.2 6.3 fusion.87
  117.0 61.3 %reduce-scatter.10.cloned.1.call-done = bf16[192,2048]{1,0:T(8,128)(2,1)} async-done(((bf16[1536,2048]{1,0:T(8,128)(2,1)}), bf16[192,2048]{1,0:T(8,128)(2,1)}) %reduce-scatter.10.cloned.1.call-update) | async-done | bytes 786448 | tf_op jit(solution)/shard_map/reduce_scatter | solution.py:86
  196.5 49.9 %all-to-all-done.1 = bf16[256,8,768]{0,2,1:T(8,128)(2,1)} async-done(((bf16[256,8,768]{0,2,1:T(8,128)(2,1)}), bf16[256,8,768]{0,2,1:T(8,128)(2,1)}, u32[]{:S(2)}, u32[]{:S(2)}) %all-to-all-start.1) | async-done | bytes 3145760 | tf_op jit(solution)/shard_map/all_to_all | solution.py:73
  255.5 41.7 %all-to-all-done.2 = bf16[256,8,768]{0,2,1:T(8,128)(2,1)} async-done(((bf16[256,8,768]{0,2,1:T(8,128)(2,1)}), bf16[256,8,768]{0,2,1:T(8,128)(2,1)}, u32[]{:S(2)}, u32[]{:S(2)}) %all-to-all-start.2) | async-done | bytes 3145760 | tf_op jit(solution)/shard_map/all_to_all | solution.py:73
  311.3 40.3 %all-to-all-done.3 = bf16[256,8,768]{0,2,1:T(8,128)(2,1)} async-done(((bf16[256,8,768]{0,2,1:T(8,128)(2,1)}), bf16[256,8,768]{0,2,1:T(8,128)(2,1)}, u32[]{:S(2)}, u32[]{:S(2)}) %all-to-all-start.3) | async-done | bytes 3145760 | tf_op jit(solution)/shard_map/all_to_all | solution.py:73
  356.2 9.6 fusion.89
  365.8 6.6 fusion.88
  372.4 13.0 %multiply_convert_fusion = (bf16[1536,768]{1,0:T(8,128)(2,1)}, bf16[1536,768]{1,0:T(8,128)(2,1)S(1)}, bf16[1536,768]{1,0:T(8,128)(2,1)}) fusion(f32[1536,768]{1,0:T(8,128)} %fusion.88, f32[1536,768]{1,0:T(8,128)} %fusion.89, bf16[1536,2048]{1,0:T(8,128)(2,1)} %all-gather.18.cloned.1.call-done, bf16[2048,768]{1,0:T(8,128)(2,1)} %bitcast.216), kind=kOutput, calls=%fused_computation.11 | convolution fusion | flops 4849532928 | bytes 25952256 | tf_op jit(solution)/shard_map/dot_general | solution.py:19
  385.5 5.1 fusion.90
  390.6 9.4 add_convert_fusion
  400.1 61.0 %reduce-scatter.14.cloned.1.call-done = bf16[192,2048]{1,0:T(8,128)(2,1)} async-done(((bf16[1536,2048]{1,0:T(8,128)(2,1)}), bf16[192,2048]{1,0:T(8,128)(2,1)}) %reduce-scatter.14.cloned.1.call-update) | async-done | bytes 786448 | tf_op jit(solution)/shard_map/reduce_scatter | solution.py:86
  464.8 9.1 fusion.6
  482.5 8.0 convolution_convert_fusion.4
  492.7 8.2 convolution_convert_fusion.5
  505.2 5.3 all-gather.20.cloned.1.call-done
  510.4 5.5 convolution_convert_fusion.8
  540.2 5.6 convolution_convert_fusion.7
  549.1 12.0 %collective-permute-done.1 = bf16[8,96,256]{2,1,0:T(8,128)(2,1)} collective-permute-done((bf16[8,96,256]{2,1,0:T(8,128)(2,1)}, bf16[8,96,256]{2,1,0:T(8,128)(2,1)}, u32[]{:S(2)}, u32[]{:S(2)}) %collective-permute-start.1) | collective-permute-done | bytes 393248 | tf_op jit(solution)/shard_map/ppermute | solution.py:160
  572.5 7.5 convolution_convert_fusion.6
  581.6 17.2 %all_to_all.133 = bf16[8,64,1,768]{3,1,2,0:T(8,128)(2,1)S(1)} all-to-all(bf16[8,64,1,768]{3,1,2,0:T(8,128)(2,1)} %bitcast.236), channel_id=1, replica_groups=mesh['fsdp'=8,'replica'=4] {'fsdp'}, dimensions={0} | all-to-all | bytes 1572864 | tf_op jit(solution)/shard_map/all_to_all | solution.py:182
  600.2 44.4 %reduce-scatter.24.cloned.1.call-done = bf16[512,768]{1,0:T(8,128)(2,1)} async-done(((bf16[2048,768]{1,0:T(8,128)(2,1)}), bf16[512,768]{1,0:T(8,128)(2,1)}) %reduce-scatter.24.cloned.1.call-update) | async-done | bytes 786448 | tf_op jit(solution)/shard_map/reduce_scatter | solution.py:181
  644.6 16.2 %all_to_all.134 = bf16[8,64,1,768]{3,1,2,0:T(8,128)(2,1)S(1)} all-to-all(bf16[8,64,1,768]{3,1,2,0:T(8,128)(2,1)} %bitcast.235), channel_id=1, replica_groups=mesh['fsdp'=8,'replica'=4] {'fsdp'}, dimensions={0} | all-to-all | bytes 1572864 | tf_op jit(solution)/shard_map/all_to_all | solution.py:182
  662.2 45.6 %reduce-scatter.22.cloned.1.call-done = bf16[512,768]{1,0:T(8,128)(2,1)} async-done(((bf16[2048,768]{1,0:T(8,128)(2,1)}), bf16[512,768]{1,0:T(8,128)(2,1)}) %reduce-scatter.22.cloned.1.call-update) | async-done | bytes 786448 | tf_op jit(solution)/shard_map/reduce_scatter | solution.py:181
  707.8 16.2 %all_to_all.135 = bf16[8,64,1,768]{3,1,2,0:T(8,128)(2,1)S(1)} all-to-all(bf16[8,64,1,768]{3,1,2,0:T(8,128)(2,1)} %bitcast.234), channel_id=1, replica_groups=mesh['fsdp'=8,'replica'=4] {'fsdp'}, dimensions={0} | all-to-all | bytes 1572864 | tf_op jit(solution)/shard_map/all_to_all | solution.py:182
  725.3 12.3 %reduce-scatter.20.cloned.1.call-done = bf16[64,2048]{1,0:T(8,128)(2,1)} async-done(((bf16[256,2048]{1,0:T(8,128)(2,1)}), bf16[64,2048]{1,0:T(8,128)(2,1)}) %reduce-scatter.20.cloned.1.call-update) | async-done | bytes 262160 | tf_op jit(solution)/shard_map/reduce_scatter | solution.py:187
  737.7 45.4 %reduce-scatter.18.cloned.1.call-done = bf16[512,512]{1,0:T(8,128)(2,1)} async-done(((bf16[2048,512]{1,0:T(8,128)(2,1)}), bf16[512,512]{1,0:T(8,128)(2,1)}) %reduce-scatter.18.cloned.1.call-update) | async-done | bytes 524304 | tf_op jit(solution)/shard_map/reduce_scatter | solution.py:181
  783.2 13.4 %all_to_all.136 = bf16[8,64,1,512]{3,1,2,0:T(8,128)(2,1)S(1)} all-to-all(bf16[8,64,1,512]{3,1,2,0:T(8,128)(2,1)} %bitcast.237), channel_id=1, replica_groups=mesh['fsdp'=8,'replica'=4] {'fsdp'}, dimensions={0} | all-to-all | bytes 1048576 | tf_op jit(solution)/shard_map/all_to_all | solution.py:182
  797.9 7.9 convolution_convert_fusion.2
  806.0 9.2 convolution_convert_fusion
  815.2 32.2 %all-gather.30.cloned.1.call-done = bf16[1,256,8,1,768]{4,2,3,0,1:T(8,128)(2,1)} async-done(((bf16[1,64,8,1,768]{4,2,3,0,1:T(8,128)(2,1)}), bf16[1,256,8,1,768]{4,2,3,0,1:T(8,128)(2,1)}) %all-gather.30.cloned.1.call-update) | async-done | bytes 3145744 | tf_op jit(solution)/shard_map/all_gather | solution.py:183
  847.5 4.9 copy.246
  852.3 5.1 bitcast_convert_fusion
  857.4 6.6 copy.250
  864.0 47.7 %all-gather.28.cloned.1.call-done = bf16[1,256,8,1,768]{4,2,3,0,1:T(8,128)(2,1)} async-done(((bf16[1,64,8,1,768]{4,2,3,0,1:T(8,128)(2,1)}), bf16[1,256,8,1,768]{4,2,3,0,1:T(8,128)(2,1)}) %all-gather.28.cloned.1.call-update) | async-done | bytes 3145744 | tf_op jit(solution)/shard_map/all_gather | solution.py:183
  916.7 5.1 bitcast_convert_fusion.1
  921.8 6.6 copy.249
  928.3 47.6 %all-gather.26.cloned.1.call-done = bf16[1,256,8,1,768]{4,2,3,0,1:T(8,128)(2,1)} async-done(((bf16[1,64,8,1,768]{4,2,3,0,1:T(8,128)(2,1)}), bf16[1,256,8,1,768]{4,2,3,0,1:T(8,128)(2,1)}) %all-gather.26.cloned.1.call-update) | async-done | bytes 3145744 | tf_op jit(solution)/shard_map/all_gather | solution.py:183
  980.9 5.0 bitcast_convert_fusion.2
  985.9 6.6 copy.248
  992.5 11.5 all-gather.22.cloned.1.call-done
  1006.8 44.1 %all-gather.24.cloned.1.call-done = bf16[1,256,8,1,512]{4,2,3,0,1:T(8,128)(2,1)} async-done(((bf16[1,64,8,1,512]{4,2,3,0,1:T(8,128)(2,1)}), bf16[1,256,8,1,512]{4,2,3,0,1:T(8,128)(2,1)}) %all-gather.24.cloned.1.call-update) | async-done | bytes 2097168 | tf_op jit(solution)/shard_map/all_gather | solution.py:183
  1059.6 6.3 copy.247
  1065.9 48.7 %reduce-scatter.16.cloned.1.call-done = bf16[192,2048]{1,0:T(8,128)(2,1)} async-done(((bf16[1536,2048]{1,0:T(8,128)(2,1)}), bf16[192,2048]{1,0:T(8,128)(2,1)}) %reduce-scatter.16.cloned.1.call-update) | async-done | bytes 786448 | tf_op jit(solution)/shard_map/reduce_scatter | solution.py:86
  1116.4 40.0 %all-reduce.1 = (f32[2048]{0:T(1024)}, f32[2048]{0:T(1024)}, f32[128]{0:T(128)}, f32[128]{0:T(128)}) all-reduce(f32[2048]{0:T(1024)S(1)} %get-tuple-element.59, f32[2048]{0:T(1024)S(1)} %get-tuple-element.57, f32[128]{0:T(128)S(1)} %bitcast_reduce_fusion, ...), channel_id=1, replica_groups=mesh['fsdp'=8,'replica'=4] {'fsdp','replica'}, use_global_device_ids=true, to_apply=%region_23.24 | all-reduce | flops 4352 | bytes 34816 | tf_op jit(solution)/shard_map/psum | solution.py:203
  1156.4 24.2 %reduce-scatter.12.cloned.1.call-done = bf16[192,2048]{1,0:T(8,128)(2,1)} async-done(((bf16[1536,2048]{1,0:T(8,128)(2,1)}), bf16[192,2048]{1,0:T(8,128)(2,1)}) %reduce-scatter.12.cloned.1.call-update) | async-done | bytes 786448 | tf_op jit(solution)/shard_map/reduce_scatter | solution.py:86
  (265 shorter events, 187.5 us)
Async XLA Ops:
  7.2 105.2 %copy-start = (bf16[256,2048]{1,0:T(8,128)(2,1)S(1)}, bf16[256,2048]{1,0:T(8,128)(2,1)}, u32[]{:S(2)}) copy-start(bf16[256,2048]{1,0:T(8,128)(2,1)} %param.16) | copy-start | bytes 3145732
  7.2 70.0 %all-gather.14.cloned.1.call-start = ((), (), s32[]{:S(2)}) async-start(), calls=%async_computation.17 | async-start | bytes 7077888 | tf_op jit(solution)/shard_map/all_gather | solution.py:83
  17.5 5.4 copy-start.46
  17.5 5.5 copy-start.52
  17.5 6.7 copy-start.47
  17.5 42.3 %all-to-all-start = ((bf16[256,8,512]{0,2,1:T(8,128)(2,1)}), bf16[256,8,512]{0,2,1:T(8,128)(2,1)}, u32[]{:S(2)}, u32[]{:S(2)}) async-start(bf16[256,8,512]{0,2,1:T(8,128)(2,1)} %pad_maximum_fusion.1), calls=%async_computation | async-start | bytes 4194304 | tf_op jit(solution)/shard_map/all_to_all | solution.py:73
  22.8 155.5 %reduce-scatter.10.cloned.1.call-start = ((), (), s32[]{:S(2)}) async-start(), calls=%async_computation.18 | async-start | bytes 7077888 | tf_op jit(solution)/shard_map/reduce_scatter | solution.py:86
  58.5 26.8 %copy-start.40 = (f32[1536]{0:T(1024)}, f32[1536]{0:T(1024)S(1)}, u32[]{:S(2)}) copy-start(f32[1536]{0:T(1024)S(1)} %convert_element_type.114) | copy-start | bytes 18436
  58.5 26.7 %copy-start.49 = (f32[64]{0:T(128)}, f32[64]{0:T(128)S(1)}, u32[]{:S(2)}) copy-start(f32[64]{0:T(128)S(1)} %multiply_power_fusion) | copy-start | bytes 772
  85.1 16.2 %copy-start.34 = (f32[1536,2]{0,1:T(2,128)}, f32[1536,2]{0,1:T(2,128)S(1)}, u32[]{:S(2)}) copy-start(f32[1536,2]{0,1:T(2,128)S(1)} %add_rsqrt_fusion) | copy-start | bytes 36868
  88.7 11.0 slice-start
  90.2 19.2 %copy-start.7 = (bf16[1536,256]{1,0:T(8,128)(2,1)}, bf16[1536,256]{1,0:T(8,128)(2,1)S(1)}, u32[]{:S(2)}) copy-start(bf16[1536,256]{1,0:T(8,128)(2,1)S(1)} %copy.204) | copy-start | bytes 2359300
  91.0 12.9 %collective-permute-start = (bf16[8,96,256]{2,1,0:T(8,128)(2,1)}, bf16[8,96,256]{2,1,0:T(8,128)(2,1)}, u32[]{:S(2)}, u32[]{:S(2)}) collective-permute-start(bf16[8,96,256]{2,1,0:T(8,128)(2,1)} %slice.110), channel_id=1, source_target_pairs={{0,1},{1,2},{2,3},{4,5},{5,6},{6,7},{8,9},{9,10},{10,11},{12,13},{... | collective-permute-start | bytes 1179656 | tf_op jit(solution)/shard_map/ppermute | solution.py:113
  116.9 61.4 %copy-start.2 = (bf16[192,2048]{1,0:T(8,128)(2,1)S(1)}, bf16[192,2048]{1,0:T(8,128)(2,1)}, u32[]{:S(2)}) copy-start(bf16[192,2048]{1,0:T(8,128)(2,1)} %param.13) | copy-start | bytes 2359300
  116.9 62.9 %copy-start.36 = (f32[2048]{0:T(1024)S(1)}, f32[2048]{0:T(1024)}, u32[]{:S(2)}) copy-start(f32[2048]{0:T(1024)} %param.21) | copy-start | bytes 24580
  117.0 239.2 %all-gather.16.cloned.1.call-start = ((), (), s32[]{:S(2)}) async-start(), calls=%async_computation.19 | async-start | bytes 7077888 | tf_op jit(solution)/shard_map/all_gather | solution.py:83
  182.1 190.3 %all-gather.18.cloned.1.call-start = ((), (), s32[]{:S(2)}) async-start(), calls=%async_computation.21 | async-start | bytes 7077888 | tf_op jit(solution)/shard_map/all_gather | solution.py:83
  187.3 59.0 %all-to-all-start.1 = ((bf16[256,8,768]{0,2,1:T(8,128)(2,1)}), bf16[256,8,768]{0,2,1:T(8,128)(2,1)}, u32[]{:S(2)}, u32[]{:S(2)}) async-start(bf16[256,8,768]{0,2,1:T(8,128)(2,1)} %bitcast.197), calls=%async_computation.2 | async-start | bytes 6291456 | tf_op jit(solution)/shard_map/all_to_all | solution.py:73
  246.4 50.8 %all-to-all-start.2 = ((bf16[256,8,768]{0,2,1:T(8,128)(2,1)}), bf16[256,8,768]{0,2,1:T(8,128)(2,1)}, u32[]{:S(2)}, u32[]{:S(2)}) async-start(bf16[256,8,768]{0,2,1:T(8,128)(2,1)} %bitcast.196), calls=%async_computation.3 | async-start | bytes 6291456 | tf_op jit(solution)/shard_map/all_to_all | solution.py:73
  297.2 54.3 %all-to-all-start.3 = ((bf16[256,8,768]{0,2,1:T(8,128)(2,1)}), bf16[256,8,768]{0,2,1:T(8,128)(2,1)}, u32[]{:S(2)}, u32[]{:S(2)}) async-start(bf16[256,8,768]{0,2,1:T(8,128)(2,1)} %bitcast.195), calls=%async_computation.4 | async-start | bytes 6291456 | tf_op jit(solution)/shard_map/all_to_all | solution.py:73
  301.7 159.4 %reduce-scatter.14.cloned.1.call-start = ((), (), s32[]{:S(2)}) async-start(), calls=%async_computation.22 | async-start | bytes 7077888 | tf_op jit(solution)/shard_map/reduce_scatter | solution.py:86
  356.2 9.6 copy-start.23
  356.2 9.6 copy-start.51
  372.4 13.0 %copy-start.24 = (bf16[8,256,768]{2,1,0:T(8,128)(2,1)S(1)}, bf16[8,256,768]{2,1,0:T(8,128)(2,1)}, u32[]{:S(2)}) copy-start(bf16[8,256,768]{2,1,0:T(8,128)(2,1)} %copy.215) | copy-start | bytes 9437188
  385.5 5.1 copy-start.25
  400.0 61.1 %copy-start.5 = (bf16[192,2048]{1,0:T(8,128)(2,1)S(1)}, bf16[192,2048]{1,0:T(8,128)(2,1)}, u32[]{:S(2)}) copy-start(bf16[192,2048]{1,0:T(8,128)(2,1)} %reduce-scatter.10.cloned.1.call-done) | copy-start | bytes 2359300
  400.0 110.4 %all-gather.20.cloned.1.call-start = ((), (), s32[]{:S(2)}) async-start(), calls=%async_computation.23 | async-start | bytes 7077888 | tf_op jit(solution)/shard_map/all_gather | solution.py:83
  464.8 116.8 %reduce-scatter.26.cloned.1.call-start = ((), (), s32[]{:S(2)}) async-start(), calls=%async_computation.30 | async-start | bytes 3932160 | tf_op jit(solution)/shard_map/reduce_scatter | solution.py:181
  482.5 162.1 %reduce-scatter.24.cloned.1.call-start = ((), (), s32[]{:S(2)}) async-start(), calls=%async_computation.29 | async-start | bytes 3932160 | tf_op jit(solution)/shard_map/reduce_scatter | solution.py:181
  492.6 215.1 %reduce-scatter.22.cloned.1.call-start = ((), (), s32[]{:S(2)}) async-start(), calls=%async_computation.28 | async-start | bytes 3932160 | tf_op jit(solution)/shard_map/reduce_scatter | solution.py:181
  502.9 234.7 %reduce-scatter.20.cloned.1.call-start = ((), (), s32[]{:S(2)}) async-start(), calls=%async_computation.26 | async-start | bytes 1310720 | tf_op jit(solution)/shard_map/reduce_scatter | solution.py:187
  531.9 29.3 %collective-permute-start.1 = (bf16[8,96,256]{2,1,0:T(8,128)(2,1)}, bf16[8,96,256]{2,1,0:T(8,128)(2,1)}, u32[]{:S(2)}, u32[]{:S(2)}) collective-permute-start(bf16[8,96,256]{2,1,0:T(8,128)(2,1)} %fusion.44), channel_id=1, source_target_pairs={{1,0},{2,1},{3,2},{5,4},{6,5},{7,6},{9,8},{10,9},{11,10},{13,12},{... | collective-permute-start | bytes 1179656 | tf_op jit(solution)/shard_map/ppermute | solution.py:160
  545.8 237.3 %reduce-scatter.18.cloned.1.call-start = ((), (), s32[]{:S(2)}) async-start(), calls=%async_computation.25 | async-start | bytes 2621440 | tf_op jit(solution)/shard_map/reduce_scatter | solution.py:181
  564.9 6.1 copy-start.38
  564.9 6.1 copy-start.45
  572.5 7.5 copy-start.33
  581.5 266.0 %all-gather.30.cloned.1.call-start = ((), (), s32[]{:S(2)}) async-start(), calls=%async_computation.34 | async-start | bytes 3932160 | tf_op jit(solution)/shard_map/all_gather | solution.py:183
  600.1 311.7 %all-gather.28.cloned.1.call-start = ((), (), s32[]{:S(2)}) async-start(), calls=%async_computation.33 | async-start | bytes 3932160 | tf_op jit(solution)/shard_map/all_gather | solution.py:183
  662.1 313.9 %all-gather.26.cloned.1.call-start = ((), (), s32[]{:S(2)}) async-start(), calls=%async_computation.32 | async-start | bytes 3932160 | tf_op jit(solution)/shard_map/all_gather | solution.py:183
  725.3 72.7 %copy-start.32 = (bf16[1536,128]{0,1:T(8,128)(2,1)S(1)}, bf16[1536,128]{0,1:T(8,128)(2,1)}, u32[]{:S(2)}) copy-start(bf16[1536,128]{0,1:T(8,128)(2,1)} %copy.229) | copy-start | bytes 1179652
  725.3 278.7 %all-gather.22.cloned.1.call-start = ((), (), s32[]{:S(2)}) async-start(), calls=%async_computation.27 | async-start | bytes 1310720 | tf_op jit(solution)/shard_map/all_gather | solution.py:188
  737.7 313.2 %all-gather.24.cloned.1.call-start = ((), (), s32[]{:S(2)}) async-start(), calls=%async_computation.31 | async-start | bytes 2621440 | tf_op jit(solution)/shard_map/all_gather | solution.py:183
  797.7 316.9 %reduce-scatter.16.cloned.1.call-start = ((), (), s32[]{:S(2)}) async-start(), calls=%async_computation.24 | async-start | bytes 7077888 | tf_op jit(solution)/shard_map/reduce_scatter | solution.py:86
  805.9 374.7 %reduce-scatter.12.cloned.1.call-start = ((), (), s32[]{:S(2)}) async-start(), calls=%async_computation.20 | async-start | bytes 7077888 | tf_op jit(solution)/shard_map/reduce_scatter | solution.py:86
  1059.6 55.0 %copy-start.39 = (f32[2048]{0:T(1024)S(1)}, f32[2048]{0:T(1024)}, u32[]{:S(2)}) copy-start(f32[2048]{0:T(1024)} %param.20) | copy-start | bytes 24580
  1059.6 55.0 %copy-start.43 = (f32[192]{0:T(256)S(1)}, f32[192]{0:T(256)}, u32[]{:S(2)}) copy-start(f32[192]{0:T(256)} %copy-done.42) | copy-start | bytes 2308
  1059.6 121.0 %copy-start.10 = (bf16[192,2048]{1,0:T(8,128)(2,1)S(1)}, bf16[192,2048]{1,0:T(8,128)(2,1)}, u32[]{:S(2)}) copy-start(bf16[192,2048]{1,0:T(8,128)(2,1)} %param.14) | copy-start | bytes 2359300
  1156.4 28.2 %copy-start.1 = (bf16[256,2048]{1,0:T(8,128)(2,1)S(1)}, bf16[256,2048]{1,0:T(8,128)(2,1)}, u32[]{:S(2)}) copy-start(bf16[256,2048]{1,0:T(8,128)(2,1)} %param.16) | copy-start | bytes 3145732
  (34 other events, 88.7 us)
Sparse Core Ops, SparseCore 0:
  11.2 65.9 all-gather.13
  117.1 61.1 reduce-scatter.9
  182.3 71.5 all-gather.15
  255.8 83.4 all-gather.17
  400.2 60.8 reduce-scatter.13
  464.9 45.4 all-gather.19
  512.7 68.5 reduce-scatter.25
  584.2 60.2 reduce-scatter.23
  647.4 60.2 reduce-scatter.21
  710.5 27.1 reduce-scatter.19
  740.6 42.4 reduce-scatter.17
  784.6 62.8 all-gather.29
  849.6 62.1 all-gather.27
  913.8 62.1 all-gather.25
  977.4 26.5 all-gather.21
  1005.4 45.3 all-gather.23
  1054.1 60.4 reduce-scatter.15
  1118.2 62.3 reduce-scatter.11

commit v2 on v1

--- a/solution.py
+++ b/solution.py
@@ -1,6 +1,10 @@
+import functools
+
 import jax
 import jax.numpy as jnp
 from jax import lax
+from jax.experimental import pallas as pl
+from jax.experimental.pallas import tpu as pltpu
 from jax.sharding import PartitionSpec as P
 
 QUERY_HEADS = 16
@@ -13,6 +17,317 @@
 NEG_FILL = -1e30
 BF = jnp.bfloat16
 F32 = jnp.float32
+
+
+MESH = pl.DeviceIdType.MESH
+ANY = pl.BlockSpec(memory_space=pl.ANY)
+VMEM = pl.BlockSpec(memory_space=pltpu.VMEM)
+DMA = pltpu.SemaphoreType.DMA
+STRIP = 16
+LAG = 3
+
+
+class Place:
+    def __init__(self, n, n_z):
+        self.n, self.chips, self.n_z = n, n // 2, n_z
+        self.f = lax.axis_index("fsdp")
+        self.chip, self.core = self.f // 2, lax.rem(self.f, 2)
+        self.sib = self.f + 1 - 2 * self.core
+        self.z = lax.axis_index("replica")
+        low = (self.z < n_z // 2).astype(jnp.int32)
+        self.inner = self.z - 1 + 2 * low
+        self.outer = self.z + 1 - 2 * low
+        self.mid = (self.z == n_z // 2 - 1) | (self.z == n_z // 2)
+        self.has_outer = (self.z > 0) & (self.z < n_z - 1)
+
+    def to(self, k):
+        return lax.rem(self.f + k, self.n)
+
+    def chip_at(self, k):
+        return lax.rem(self.chip + k, self.chips)
+
+    def greet(self, line):
+        barrier = pltpu.get_barrier_semaphore()
+        for k in range(1, self.n):
+            pl.semaphore_signal(barrier, inc=1, device_id={"fsdp": self.to(k)}, device_id_type=MESH)
+        if line:
+            pl.semaphore_signal(barrier, inc=1, device_id={"replica": self.inner}, device_id_type=MESH)
+
+            @pl.when(self.has_outer)
+            def _():
+                pl.semaphore_signal(barrier, inc=1, device_id={"replica": self.outer}, device_id_type=MESH)
+                pl.semaphore_wait(barrier, 1)
+
+        pl.semaphore_wait(barrier, self.n - 1 + int(line))
+
+
+def remote(src, dst, send, recv, axis, index):
+    return pltpu.make_async_remote_copy(
+        src_ref=src, dst_ref=dst, send_sem=send, recv_sem=recv, device_id={axis: index}, device_id_type=MESH)
+
+
+def strips(rows, body):
+    def step(i, carry):
+        body(pl.ds(pl.multiple_of(i * STRIP, STRIP), STRIP))
+        return carry
+
+    lax.fori_loop(0, rows // STRIP, step, 0)
+
+
+class Exchange:
+    def __init__(self, at, pieces, send, recv):
+        self.copies, self.local = [], []
+        for i, (src, dst) in enumerate(pieces):
+            self.local.append(pltpu.make_async_copy(src(at.f), dst(at.f), recv.at[i, 0]))
+            for k in range(1, at.n):
+                self.copies.append(remote(src(at.to(k)), dst(at.f), send.at[i, k], recv.at[i, k], "fsdp", at.to(k)))
+
+    def start(self):
+        for c in self.copies + self.local:
+            c.start()
+
+    def wait(self):
+        for c in self.copies + self.local:
+            c.wait()
+
+
+class Gather:
+    def __init__(self, at, own, whole, sem):
+        rows = own.shape[0]
+
+        def block(i):
+            return whole.at[pl.ds(pl.multiple_of(i * rows, rows), rows)]
+
+        self.local = pltpu.make_async_copy(own, block(at.f), sem.at[0, 0])
+        self.across = [remote(own, block(at.f), sem.at[0, 1], sem.at[1, 0], "fsdp", at.sib)]
+        self.far, self.on = [], []
+        for k in range(1, at.chips):
+            to = 2 * at.chip_at(k) + at.core
+            self.far.append(remote(own, block(at.f), sem.at[2, k], sem.at[3, k], "fsdp", to))
+            came = 2 * at.chip_at(at.chips - k) + at.core
+            self.on.append(remote(block(came), block(came), sem.at[4, k], sem.at[5, k], "fsdp", at.sib))
+
+    def start(self):
+        for c in self.far + self.across + [self.local]:
+            c.start()
+
+    def forward(self):
+        for far, on in zip(self.far, self.on):
+            far.wait_recv()
+            on.start()
+
+    def wait(self):
+        for c in self.far:
+            c.wait_send()
+        for c in self.across + self.on + [self.local]:
+            c.wait()
+
+
+class ScatterSum:
+    def __init__(self, at, part, near, own, far, sem):
+        self.at, self.near, self.own, self.far = at, near, own, far
+        rows = own.shape[1]
+        self.rows = rows
+
+        def block(i):
+            return part.at[pl.ds(pl.multiple_of(i * rows, rows), rows)]
+
+        self.across, self.load, self.send = [], [], []
+        for k in range(at.chips):
+            q = at.chip_at(k)
+            self.across.append(remote(block(2 * q + 1 - at.core), near.at[k], sem.at[0, k], sem.at[1, k], "fsdp", at.sib))
+            self.load.append(pltpu.make_async_copy(block(2 * q + at.core), own.at[k], sem.at[2, k]))
+            if k:
+                self.send.append(
+                    remote(own.at[k], far.at[k - 1], sem.at[3, k], sem.at[4, k], "fsdp", 2 * q + at.core))
+
+    def start(self):
+        for k in list(range(1, self.at.chips)) + [0]:
+            self.across[k].start()
+            self.load[k].start()
+
+    def forward(self):
+        for k in list(range(1, self.at.chips)) + [0]:
+            self.across[k].wait()
+            self.load[k].wait()
+
+            def add(at, k=k):
+                self.own[k, at] = (self.own[k, at].astype(F32) + self.near[k, at].astype(F32)).astype(BF)
+
+            strips(self.rows, add)
+            if k:
+                self.send[k - 1].start()
+
+    def wait(self):
+        for c in self.send:
+            c.wait()
+
+    def total(self, at):
+        out = self.own[0, at].astype(F32)
+        for k in range(self.at.chips - 1):
+            out += self.far[k, at].astype(F32)
+        return out
+
+
+class LineSum:
+    def __init__(self, at, chunk, came, arrive, send, recv, out, out_sem):
+        self.at, self.chunk, self.came, self.arrive = at, chunk, came, arrive
+        self.send, self.recv, self.out, self.out_sem = send, recv, out, out_sem
+        self.count = chunk.shape[0]
+        self.kind = at.mid.astype(jnp.int32)
+
+    def inward(self, j):
+        return remote(self.chunk.at[j], self.came.at[self.kind, j], self.send.at[0, j], self.recv.at[self.kind, j],
+                      "replica", self.at.inner)
+
+    def outward(self, j, src):
+        return remote(src, self.came.at[1, j], self.send.at[1, j], self.recv.at[1, j], "replica", self.at.outer)
+
+    def here(self, kind, j):
+        return pltpu.make_async_copy(self.came.at[kind, j], self.came.at[kind, j], self.recv.at[kind, j])
+
+    def up(self, j):
+        pltpu.make_async_copy(self.chunk.at[j], self.chunk.at[j], self.arrive.at[j]).wait()
+
+        @pl.when(self.at.has_outer)
+        def _():
+            self.here(0, j).wait()
+            self.chunk[j] = (self.chunk[j].astype(F32) + self.came[0, j].astype(F32)).astype(BF)
+
+        self.inward(j).start()
+
+    def down(self, j):
+        self.here(1, j).wait()
+
+        @pl.when(self.at.mid)
+        def _():
+            self.came[1, j] = (self.chunk[j].astype(F32) + self.came[1, j].astype(F32)).astype(BF)
+
+        @pl.when(self.at.has_outer)
+        def _():
+            self.outward(j, self.came.at[1, j]).start()
+
+        pltpu.make_async_copy(self.came.at[1, j], self.out(j), self.out_sem.at[j]).start()
+
+    def settle(self):
+        def step(j, carry):
+            self.inward(j).wait_send()
+
+            @pl.when(self.at.has_outer)
+            def _():
+                self.outward(j, self.came.at[1, j]).wait_send()
+
+            pltpu.make_async_copy(self.came.at[1, j], self.out(j), self.out_sem.at[j]).wait()
+            return carry
+
+        lax.fori_loop(0, self.count, step, 0)
+
+
+def run_line(line, first, last):
+    lag = min(LAG, last - first)
+
+    def head(j, carry):
+        line.up(j)
+        return carry
+
+    def body(j, carry):
+        line.up(j)
+        line.down(j - lag)
+        return carry
+
+    def tail(j, carry):
+        line.down(j)
+        return carry
+
+    lax.fori_loop(first, first + lag, head, 0)
+    lax.fori_loop(first + lag, last, body, 0)
+    lax.fori_loop(last - lag, last, tail, 0)
+
+
+def rms_of(values):
+    return lax.rsqrt(jnp.mean(values * values, axis=-1, keepdims=True) + EPSILON)
+
+
+def qkv_pieces(at, w, wc, qw):
+    q_w, k_w = QUERY_HEADS * HEAD_WIDTH, KEY_VALUE_HEADS * HEAD_WIDTH
+    shared = at.n // KEY_VALUE_HEADS
+    depth = w.shape[0]
+
+    def cols(start, width):
+        return pl.ds(pl.multiple_of(start, HEAD_WIDTH), width)
+
+    def rows(s):
+        return pl.ds(pl.multiple_of(s * depth, depth), depth)
+
+    return [
+        (lambda t: w.at[:, cols(t * qw, qw)], lambda s: wc.at[rows(s), pl.ds(0, qw)]),
+        (lambda t: w.at[:, cols(q_w + t // shared * HEAD_WIDTH, HEAD_WIDTH)],
+         lambda s: wc.at[rows(s), pl.ds(qw, HEAD_WIDTH)]),
+        (lambda t: w.at[:, cols(q_w + k_w + t // shared * HEAD_WIDTH, HEAD_WIDTH)],
+         lambda s: wc.at[rows(s), pl.ds(qw + HEAD_WIDTH, HEAD_WIDTH)]),
+    ]
+
+
+def col_piece(w, wc, share):
+    depth = w.shape[0]
+    return (lambda t: w.at[:, pl.ds(pl.multiple_of(t * share, HEAD_WIDTH), share)],
+            lambda s: wc.at[pl.ds(pl.multiple_of(s * depth, depth), depth)])
+
+
+def begin_kernel(n, n_z, x_ref, gain_ref, place_ref, wqkv_ref, n1_ref, wc_ref, places_ref,
+                 own, s_x, r_x, s_g, s_p, r_p):
+    at = Place(n, n_z)
+    rows = x_ref.shape[0]
+    at.greet(False)
+    weights = Exchange(at, qkv_pieces(at, wqkv_ref, wc_ref, QUERY_HEADS * HEAD_WIDTH // n), s_x, r_x)
+    place = Exchange(at, [(lambda t: place_ref, lambda s: places_ref.at[s])], s_p, r_p)
+    place.start()
+    weights.start()
+
+    def norm(strip):
+        x = x_ref[strip].astype(F32)
+        own[strip] = (x * rms_of(x) * gain_ref[...]).astype(BF)
+
+    strips(rows, norm)
+    gather = Gather(at, own, n1_ref, s_g)
+    gather.start()
+    gather.forward()
+    gather.wait()
+    place.wait()
+    weights.wait()
+
+
+def middle_kernel(n, n_z, part_ref, x_ref, gain_ref, g_ref, gate_ref, up_ref, down_ref,
+                  h_ref, n2_ref, gall_ref, gate_c, up_c, down_c,
+                  near, mine, far, own, s_r, s_a, s_b, s_x, r_x, s_y, r_y):
+    at = Place(n, n_z)
+    share = gate_c.shape[1]
+    at.greet(False)
+    total = ScatterSum(at, part_ref, near, mine, far, s_r)
+    total.start()
+    total.forward()
+    first = Exchange(at, [col_piece(gate_ref, gate_c, share), col_piece(up_ref, up_c, share)], s_x, r_x)
+    second = Exchange(at, [col_piece(down_ref, down_c, share)], s_y, r_y)
+    first.start()
+    total.wait()
+
+    def norm(strip):
+        h = x_ref[strip].astype(F32) + total.total(strip)
+        h_ref[strip] = h
+        own[strip] = (h * rms_of(h) * gain_ref[...]).astype(BF)
+
+    strips(x_ref.shape[0], norm)
+    n2 = Gather(at, own, n2_ref, s_a)
+    g_all = Gather(at, g_ref, gall_ref, s_b)
+    n2.start()
+    g_all.start()
+    second.start()
+    n2.forward()
+    g_all.forward()
+    n2.wait()
+    g_all.wait()
+    first.wait()
+    second.wait()
 
 
 def dot(left, right):
@@ -43,6 +358,48 @@
 
 def norm_back(d_normed, normed, rms):
     return rms * (d_normed - normed * jnp.mean(d_normed * normed, axis=-1, keepdims=True))
+
+
+def begin(n, n_z, x, gain, place, w_qkv):
+    rows, width = x.shape
+    total, wide = n * rows, (QUERY_HEADS // n + 2) * HEAD_WIDTH
+    return pl.pallas_call(
+        functools.partial(begin_kernel, n, n_z),
+        out_shape=(
+            jax.ShapeDtypeStruct((total, width), BF),
+            jax.ShapeDtypeStruct((width, wide), BF),
+            jax.ShapeDtypeStruct((n,) + place.shape, place.dtype),
+        ),
+        in_specs=[VMEM, VMEM, ANY, ANY],
+        out_specs=(ANY, ANY, ANY),
+        scratch_shapes=[
+            pltpu.VMEM((rows, width), BF), DMA((3, n)), DMA((3, n)), DMA((6, n)), DMA((1, n)), DMA((1, n))],
+        compiler_params=pltpu.CompilerParams(collective_id=0, has_side_effects=True, vmem_limit_bytes=32 << 20),
+        name="begin",
+    )(x, gain, place, w_qkv)
+
+
+def middle(n, n_z, part, x, gain, g, gate, up, down):
+    rows, width = x.shape
+    total, share, chips = n * rows, gate.shape[1] // n, n // 2
+    columns = jax.ShapeDtypeStruct((width, share), BF)
+    return pl.pallas_call(
+        functools.partial(middle_kernel, n, n_z),
+        out_shape=(
+            jax.ShapeDtypeStruct((rows, width), F32),
+            jax.ShapeDtypeStruct((total, width), BF),
+            jax.ShapeDtypeStruct((total, width), BF),
+            columns, columns, columns,
+        ),
+        in_specs=[ANY, VMEM, VMEM, ANY, ANY, ANY, ANY],
+        out_specs=(VMEM, ANY, ANY, ANY, ANY, ANY),
+        scratch_shapes=[
+            pltpu.VMEM((chips, rows, width), BF), pltpu.VMEM((chips, rows, width), BF),
+            pltpu.VMEM((chips - 1, rows, width), BF), pltpu.VMEM((rows, width), BF),
+            DMA((5, n)), DMA((6, n)), DMA((6, n)), DMA((2, n)), DMA((2, n)), DMA((1, n)), DMA((1, n))],
+        compiler_params=pltpu.CompilerParams(collective_id=1, has_side_effects=True, vmem_limit_bytes=48 << 20),
+        name="middle",
+    )(part, x, gain, g, gate, up, down)
 
 
 def row_positions(flat_lens, ranks, first_row, count):
@@ -67,17 +424,10 @@
     qw = heads * HEAD_WIDTH
 
     pos = row_positions(dealt_lens[0].reshape(-1), seq_order[0], replica * rows, rows)
-    pos_all = lax.all_gather(pos, "fsdp", axis=0, tiled=True)
-
-    def scatter_cols(w):
-        return lax.all_to_all(w, "fsdp", split_axis=1, concat_axis=0, tiled=True)
-
     depth = w_qkv.shape[0]
-    wq = w_qkv[:, :q_w].reshape(depth, n_fsdp, qw)
-    wk = jnp.repeat(w_qkv[:, q_w:q_w + k_w].reshape(depth, KEY_VALUE_HEADS, HEAD_WIDTH), shared, axis=1)
-    wv = jnp.repeat(w_qkv[:, q_w + k_w:].reshape(depth, KEY_VALUE_HEADS, HEAD_WIDTH), shared, axis=1)
-    w_qkv_c = scatter_cols(jnp.concatenate([wq, wk, wv], axis=2).reshape(depth, -1))
-    gate_c, up_c, down_c = scatter_cols(w_gate), scatter_cols(w_up), scatter_cols(w_down_t)
+    place = jnp.zeros((8, HEAD_WIDTH), jnp.int32).reshape(-1).at[:rows].set(pos).reshape(8, HEAD_WIDTH)
+    n1, w_qkv_c, places = begin(n_fsdp, n_replica, tokens, gain_attn[None], place, w_qkv)
+    pos_all = places.reshape(n_fsdp, -1)[:, :rows].reshape(-1)
 
     def gather(a):
         return lax.all_gather(a, "fsdp", axis=0, tiled=True)
@@ -89,8 +439,6 @@
     g = cotangent.astype(F32)
     r1 = lax.rsqrt(jnp.mean(x * x, axis=1, keepdims=True) + EPSILON)
     u1 = x * r1
-    n1 = gather((u1 * gain_attn).astype(BF))
-    g_all = gather(cotangent)
     total = n1.shape[0]
 
     proj = dot(n1, w_qkv_c)
@@ -129,11 +477,11 @@
     probs_low = probs.astype(BF)
     ctx = jnp.einsum("ghqk,gkd->gqhd", probs_low, v_win, preferred_element_type=F32)
     ctx_low = ctx.reshape(total, qw).astype(BF)
-    h = x + scatter_sum(dot(ctx_low, w_out))
+    h, n2, g_all, gate_c, up_c, down_c = middle(
+        n_fsdp, n_replica, dot(ctx_low, w_out).astype(BF), tokens, gain_mlp[None], cotangent, w_gate, w_up, w_down_t)
 
     r2 = lax.rsqrt(jnp.mean(h * h, axis=1, keepdims=True) + EPSILON)
     u2 = h * r2
-    n2 = gather((u2 * gain_mlp).astype(BF))
     gate = dot(n2, gate_c)
     up = dot(n2, up_c)
     sg = jax.nn.sigmoid(gate)

time: 1200 us -> 1050 us (0.88)
  waiting for transfers between devices: 690 us -> 370 us
  Pallas kernels: 0 us -> 276 us
  local copies, waits for them, and re-layouts: 128 us -> 88.7 us
  blocking collectives: 137 us -> 101 us
  starting transfers between devices: 26 us -> 7.05 us
    pallas_call x0 -> x2, Pallas kernels: none -> 276 us  [the longest x1 210 us: middle(): pl.pallas_call(functools.partial(middle_kernel, n, n_z), out_shape=(jax.S...]
    reduce_scatter x4 -> x3, waiting for transfers between devices: 195 us -> 61.7 us  [scatter_sum(): lax.psum_scatter(a.astype(BF), 'fsdp', scatter_dimension=0, tiled=True)]
    all_to_all x4 -> x0, waiting for transfers between devices: 132 us -> none  [scatter_cols(): return lax.all_to_all(w, 'fsdp', split_axis=1, concat_axis=0, tiled=True)]
    unnamed x1 -> x0, blocking collectives: 33.9 us -> none
    reduce_scatter x4, waiting for transfers between devices: 135 us -> 102 us  [reduce_cols(): part = lax.psum_scatter(low, 'replica', scatter_dimension=0, tiled=True)]
    all_to_all x4 -> x0, starting transfers between devices: 18.8 us -> none  [scatter_cols(): return lax.all_to_all(w, 'fsdp', split_axis=1, concat_axis=0, tiled=True)]
    all_to_all x4 -> x0, local copies, waits for them, and re-layouts: 17.9 us -> none  [scatter_cols(): return lax.all_to_all(w, 'fsdp', split_axis=1, concat_axis=0, tiled=True)]
    ppermute x1, waiting for transfers between devices: 12 us -> 0.01 us  [per_device(): lax.ppermute(d_kv[:, :halo].astype(BF), 'replica', down_pairs).astype(F32)]
  transfers between devices with their start and end apart: 24 -> 16, of which waited for: 19 -> 11; matrix products, arithmetic and copies ran while one was open for 21% -> 18% of each run, Pallas kernels for 0% -> 0%
where the time goes in v2:
time: 1050 us; the launch traced here: 1040 us
  waiting for transfers between devices  370 us (35%)
  Pallas kernels  276 us (26%)
  matrix products  123 us (12%)
  blocking collectives  101 us (10%)
  local copies, waits for them, and re-layouts  88.7 us (8%)
  other arithmetic  60.4 us (6%)
  between operations  16.4 us (2%)
    pallas_call x1, Pallas kernels, middle(): pl.pallas_call(functools.partial(middle_kernel, n, n_z), out_shape=(jax.S...  210 us
    all_gather x4, waiting for transfers between devices, reduce_cols(): whole = lax.all_gather(part, 'replica', axis=0, tiled=True)  169 us
    reduce_scatter x4, waiting for transfers between devices, reduce_cols(): part = lax.psum_scatter(low, 'replica', scatter_dimension=0, tiled=True)  102 us
    pallas_call x1, Pallas kernels, begin(): pl.pallas_call(functools.partial(begin_kernel, n, n_z), out_shape=(jax.Sh...  66.1 us
    all_to_all x4, blocking collectives, reduce_cols(): lax.all_to_all(part.reshape(n_fsdp, -1, share), 'fsdp', split_axis=0, con...  61.8 us
    reduce_scatter x3, waiting for transfers between devices, scatter_sum(): lax.psum_scatter(a.astype(BF), 'fsdp', scatter_dimension=0, tiled=True)  61.7 us
    dot_general x5, matrix products, dot_cols(): lax.dot_general(left, right, (((1,), (1,)), ((), ())), preferred_element_...  41 us
    psum x1, blocking collectives, per_device(): lax.psum((d_gain_attn, d_gain_mlp, d_gain_query, d_gain_key), ('fsdp', 'r...  39.5 us
  transfers between devices with their start and end apart: 16, of which 11 were waited for; matrix products, arithmetic and copies ran while one was open for 18% of the time, Pallas kernels for 0%

profile of v2, /device:TPU:0, one launch (start us, length us, event | category | flops | bytes accessed | tf_op | source)
XLA Modules:
  0.0 1042.5 jit_solution(1935531709703093786)
XLA Ops:
  13.3 66.1 %begin.1 = (bf16[1536,2048]{1,0:T(8,128)(2,1)S(1)}, bf16[2048,512]{1,0:T(8,128)(2,1)S(1)}, s32[8,8,128]{2,1,0:T(8,128)S(1)}) custom-call(bf16[192,2048]{1,0:T(8,128)(2,1)S(1)} %copy-done.2, f32[1,2048]{1,0:T(1,128)S(1)} %bitcast.180, s32[8,128]{1,0:T(8,128)S(1)} %pad_bitcast_fusion.place_ref, bf16[256,4096]{1,0:T(8,128)(2,1)S(1)} %copy-done.6), custom_call_target="tpu_custom_call" | custom-call | tf_op jit(solution)/shard_map/begin/pallas_call | solution.py:366
  79.4 3.6 fusion.82
  90.4 4.3 collective-permute-start
  113.9 4.5 convolution_convert_fusion.1.part_ref
  118.4 209.6 %middle.1 = (f32[192,2048]{1,0:T(8,128)S(1)}, bf16[1536,2048]{1,0:T(8,128)(2,1)}, bf16[1536,2048]{1,0:T(8,128)(2,1)}, bf16[2048,768]{1,0:T(8,128)(2,1)}, bf16[20...) custom-call(bf16[1536,2048]{1,0:T(8,128)(2,1)} %convolution_convert_fusion.1.part_ref, bf16[192,2048]{1,0:T(8,128)(2,1)S(1)} %copy-done.3, ...), custom_call_target="tpu_custom_call" | custom-call | tf_op jit(solution)/shard_map/middle/pallas_call | solution.py:386
  328.1 8.2 fusion.83
  336.4 6.7 fusion.84
  343.1 9.9 multiply_convert_fusion
  353.0 8.4 fusion.85
  361.4 9.9 add_convert_fusion
  371.5 61.7 %reduce-scatter.11.cloned.1.call-done = bf16[192,2048]{1,0:T(8,128)(2,1)} async-done(((bf16[1536,2048]{1,0:T(8,128)(2,1)}), bf16[192,2048]{1,0:T(8,128)(2,1)}) %reduce-scatter.11.cloned.1.call-update) | async-done | bytes 786448 | tf_op jit(solution)/shard_map/reduce_scatter | solution.py:436
  436.6 8.0 convolution_convert_fusion.3
  446.8 8.0 convolution_convert_fusion.4
  456.9 8.2 convolution_convert_fusion.5
  469.3 12.9 %all-gather.11.cloned.1.call-done = bf16[1536,2048]{1,0:T(8,128)(2,1)} async-done(((bf16[192,2048]{1,0:T(8,128)(2,1)}), bf16[1536,2048]{1,0:T(8,128)(2,1)}) %all-gather.11.cloned.1.call-update) | async-done | bytes 6291472 | tf_op jit(solution)/shard_map/all_gather | solution.py:433
  482.2 5.6 convolution_convert_fusion.8
  489.8 3.6 fusion.1
  493.4 3.7 fusion.3
  511.5 5.6 convolution_convert_fusion.7
  531.6 7.5 convolution_convert_fusion.6
  540.7 16.0 %all_to_all.60 = bf16[8,64,1,768]{3,1,2,0:T(8,128)(2,1)S(1)} all-to-all(bf16[8,64,1,768]{3,1,2,0:T(8,128)(2,1)} %bitcast.216), channel_id=1, replica_groups=mesh['fsdp'=8,'replica'=4] {'fsdp'}, dimensions={0} | all-to-all | bytes 1572864 | tf_op jit(solution)/shard_map/all_to_all | solution.py:530
  558.1 11.5 %reduce-scatter.21.cloned.1.call-done = bf16[512,768]{1,0:T(8,128)(2,1)} async-done(((bf16[2048,768]{1,0:T(8,128)(2,1)}), bf16[512,768]{1,0:T(8,128)(2,1)}) %reduce-scatter.21.cloned.1.call-update) | async-done | bytes 786448 | tf_op jit(solution)/shard_map/reduce_scatter | solution.py:529
  569.6 16.2 %all_to_all.61 = bf16[8,64,1,768]{3,1,2,0:T(8,128)(2,1)S(1)} all-to-all(bf16[8,64,1,768]{3,1,2,0:T(8,128)(2,1)} %bitcast.215), channel_id=1, replica_groups=mesh['fsdp'=8,'replica'=4] {'fsdp'}, dimensions={0} | all-to-all | bytes 1572864 | tf_op jit(solution)/shard_map/all_to_all | solution.py:530
  587.2 45.5 %reduce-scatter.19.cloned.1.call-done = bf16[512,768]{1,0:T(8,128)(2,1)} async-done(((bf16[2048,768]{1,0:T(8,128)(2,1)}), bf16[512,768]{1,0:T(8,128)(2,1)}) %reduce-scatter.19.cloned.1.call-update) | async-done | bytes 786448 | tf_op jit(solution)/shard_map/reduce_scatter | solution.py:529
  632.7 16.2 %all_to_all.62 = bf16[8,64,1,768]{3,1,2,0:T(8,128)(2,1)S(1)} all-to-all(bf16[8,64,1,768]{3,1,2,0:T(8,128)(2,1)} %bitcast.214), channel_id=1, replica_groups=mesh['fsdp'=8,'replica'=4] {'fsdp'}, dimensions={0} | all-to-all | bytes 1572864 | tf_op jit(solution)/shard_map/all_to_all | solution.py:530
  650.3 12.5 %reduce-scatter.17.cloned.1.call-done = bf16[64,2048]{1,0:T(8,128)(2,1)} async-done(((bf16[256,2048]{1,0:T(8,128)(2,1)}), bf16[64,2048]{1,0:T(8,128)(2,1)}) %reduce-scatter.17.cloned.1.call-update) | async-done | bytes 262160 | tf_op jit(solution)/shard_map/reduce_scatter | solution.py:535
  662.8 44.9 %reduce-scatter.15.cloned.1.call-done = bf16[512,512]{1,0:T(8,128)(2,1)} async-done(((bf16[2048,512]{1,0:T(8,128)(2,1)}), bf16[512,512]{1,0:T(8,128)(2,1)}) %reduce-scatter.15.cloned.1.call-update) | async-done | bytes 524304 | tf_op jit(solution)/shard_map/reduce_scatter | solution.py:529
  707.7 13.4 %all_to_all.63 = bf16[8,64,1,512]{3,1,2,0:T(8,128)(2,1)S(1)} all-to-all(bf16[8,64,1,512]{3,1,2,0:T(8,128)(2,1)} %bitcast.217), channel_id=1, replica_groups=mesh['fsdp'=8,'replica'=4] {'fsdp'}, dimensions={0} | all-to-all | bytes 1048576 | tf_op jit(solution)/shard_map/all_to_all | solution.py:530
  722.5 7.9 convolution_convert_fusion.2
  730.5 9.2 convolution_convert_fusion
  741.2 31.4 %all-gather.21.cloned.1.call-done = bf16[1,256,8,1,768]{4,2,3,0,1:T(8,128)(2,1)} async-done(((bf16[1,64,8,1,768]{4,2,3,0,1:T(8,128)(2,1)}), bf16[1,256,8,1,768]{4,2,3,0,1:T(8,128)(2,1)}) %all-gather.21.cloned.1.call-update) | async-done | bytes 3145744 | tf_op jit(solution)/shard_map/all_gather | solution.py:531
  772.6 4.9 copy.201
  777.4 5.3 bitcast_convert_fusion
  782.8 6.6 copy.205
  789.4 47.3 %all-gather.19.cloned.1.call-done = bf16[1,256,8,1,768]{4,2,3,0,1:T(8,128)(2,1)} async-done(((bf16[1,64,8,1,768]{4,2,3,0,1:T(8,128)(2,1)}), bf16[1,256,8,1,768]{4,2,3,0,1:T(8,128)(2,1)}) %all-gather.19.cloned.1.call-update) | async-done | bytes 3145744 | tf_op jit(solution)/shard_map/all_gather | solution.py:531
  836.7 4.9 copy.197
  841.6 5.6 bitcast_convert_fusion.1
  847.2 6.6 copy.204
  853.8 47.0 %all-gather.17.cloned.1.call-done = bf16[1,256,8,1,768]{4,2,3,0,1:T(8,128)(2,1)} async-done(((bf16[1,64,8,1,768]{4,2,3,0,1:T(8,128)(2,1)}), bf16[1,256,8,1,768]{4,2,3,0,1:T(8,128)(2,1)}) %all-gather.17.cloned.1.call-update) | async-done | bytes 3145744 | tf_op jit(solution)/shard_map/all_gather | solution.py:531
  900.8 4.9 copy.193
  905.7 5.0 bitcast_convert_fusion.2
  910.7 6.6 copy.203
  917.3 11.6 %all-gather.13.cloned.1.call-done = bf16[256,2048]{1,0:T(8,128)(2,1)} async-done(((bf16[64,2048]{1,0:T(8,128)(2,1)}), bf16[256,2048]{1,0:T(8,128)(2,1)}) %all-gather.13.cloned.1.call-update) | async-done | bytes 1048592 | tf_op jit(solution)/shard_map/all_gather | solution.py:536
  931.6 43.9 %all-gather.15.cloned.1.call-done = bf16[1,256,8,1,512]{4,2,3,0,1:T(8,128)(2,1)} async-done(((bf16[1,64,8,1,512]{4,2,3,0,1:T(8,128)(2,1)}), bf16[1,256,8,1,512]{4,2,3,0,1:T(8,128)(2,1)}) %all-gather.15.cloned.1.call-update) | async-done | bytes 2097168 | tf_op jit(solution)/shard_map/all_gather | solution.py:531
  975.5 4.3 copy.189
  984.3 5.6 copy.202
  991.7 39.5 %all-reduce.1 = (f32[2048]{0:T(1024)}, f32[2048]{0:T(1024)}, f32[128]{0:T(128)}, f32[128]{0:T(128)}) all-reduce(f32[2048]{0:T(1024)S(1)} %get-tuple-element.89, f32[2048]{0:T(1024)S(1)} %get-tuple-element.87, f32[128]{0:T(128)S(1)} %bitcast_reduce_fusion, ...), channel_id=1, replica_groups=mesh['fsdp'=8,'replica'=4] {'fsdp','replica'}, use_global_device_ids=true, to_apply=%region_22.23 | all-reduce | flops 4352 | bytes 34816 | tf_op jit(solution)/shard_map/psum | solution.py:551
  1031.2 4.0 fusion.17
  (231 shorter events, 91.9 us)
Async XLA Ops:
  8.0 105.9 %copy-start = (bf16[256,2048]{1,0:T(8,128)(2,1)S(1)}, bf16[256,2048]{1,0:T(8,128)(2,1)}, u32[]{:S(2)}) copy-start(bf16[256,2048]{1,0:T(8,128)(2,1)} %param.18) | copy-start | bytes 3145732
  8.0 425.3 %reduce-scatter.11.cloned.1.call-start = ((), (), s32[]{:S(2)}) async-start(), calls=%async_computation.13 | async-start | bytes 7077888 | tf_op jit(solution)/shard_map/reduce_scatter | solution.py:436
  8.1 78.6 %copy-start.45 = (f32[64]{0:T(128)}, f32[64]{0:T(128)S(1)}, u32[]{:S(2)}) copy-start(f32[64]{0:T(128)S(1)} %multiply_power_fusion) | copy-start | bytes 772
  79.4 6.0 copy-start.42
  84.8 4.4 copy-start.40
  89.5 21.3 %copy-start.17 = (bf16[1536,256]{1,0:T(8,128)(2,1)}, bf16[1536,256]{1,0:T(8,128)(2,1)S(1)}, u32[]{:S(2)}) copy-start(bf16[1536,256]{1,0:T(8,128)(2,1)S(1)} %copy.166) | copy-start | bytes 2359300
  90.4 15.1 %collective-permute-start = (bf16[8,96,256]{2,1,0:T(8,128)(2,1)}, bf16[8,96,256]{2,1,0:T(8,128)(2,1)}, u32[]{:S(2)}, u32[]{:S(2)}) collective-permute-start(bf16[8,96,256]{2,1,0:T(8,128)(2,1)} %slice.114), channel_id=1, source_target_pairs={{0,1},{1,2},{2,3},{4,5},{5,6},{6,7},{8,9},{9,10},{10,11},{12,13},{... | collective-permute-start | bytes 1179656 | tf_op jit(solution)/shard_map/ppermute | solution.py:461
  96.2 4.5 slice-start
  98.5 3.8 copy-start.44
  113.9 4.6 copy-start.15
  113.9 4.6 copy-start.3
  113.9 4.5 copy-start.5
  113.9 4.5 copy-start.7
  328.1 8.3 copy-start.47
  328.1 8.3 copy-start.49
  328.1 15.0 %slice-start.3 = ((s8[6291456]{0:T(1024)(128)(4,1)}), s8[4194304]{0:T(1024)(128)(4,1)S(1)}, s32[]{:S(2)}) async-start(s8[6291456]{0:T(1024)(128)(4,1)} %bitcast.220), calls=%async_computation.29 | async-start | bytes 8388608
  336.3 6.7 slice-start.4
  336.4 6.7 copy-start.48
  343.1 9.9 copy-start.50
  352.9 8.4 copy-start.51
  352.9 8.4 copy-start.52
  371.3 110.9 %all-gather.11.cloned.1.call-start = ((), (), s32[]{:S(2)}) async-start(), calls=%async_computation.14 | async-start | bytes 7077888 | tf_op jit(solution)/shard_map/all_gather | solution.py:433
  436.5 104.2 %reduce-scatter.23.cloned.1.call-start = ((), (), s32[]{:S(2)}) async-start(), calls=%async_computation.21 | async-start | bytes 3932160 | tf_op jit(solution)/shard_map/reduce_scatter | solution.py:529
  446.7 122.9 %reduce-scatter.21.cloned.1.call-start = ((), (), s32[]{:S(2)}) async-start(), calls=%async_computation.20 | async-start | bytes 3932160 | tf_op jit(solution)/shard_map/reduce_scatter | solution.py:529
  456.9 175.8 %reduce-scatter.19.cloned.1.call-start = ((), (), s32[]{:S(2)}) async-start(), calls=%async_computation.19 | async-start | bytes 3932160 | tf_op jit(solution)/shard_map/reduce_scatter | solution.py:529
  467.2 195.6 %reduce-scatter.17.cloned.1.call-start = ((), (), s32[]{:S(2)}) async-start(), calls=%async_computation.17 | async-start | bytes 1310720 | tf_op jit(solution)/shard_map/reduce_scatter | solution.py:535
  469.3 20.5 %copy-start.18 = (bf16[1536,256]{1,0:T(8,128)(2,1)S(1)}, bf16[1536,256]{1,0:T(8,128)(2,1)}, u32[]{:S(2)}) copy-start(bf16[1536,256]{1,0:T(8,128)(2,1)} %copy-done.17) | copy-start | bytes 2359300
  497.1 4.4 slice-start.1
  502.8 17.5 %collective-permute-start.1 = (bf16[8,96,256]{2,1,0:T(8,128)(2,1)S(1)}, bf16[8,96,256]{2,1,0:T(8,128)(2,1)S(1)}, u32[]{:S(2)}, u32[]{:S(2)}) collective-permute-start(bf16[8,96,256]{2,1,0:T(8,128)(2,1)S(1)} %fusion.39), channel_id=1, source_target_pairs={{1,0},{2,1},{3,2},{5,4},{6,5},{7,6},{9,8},{10,9},{11,10},{13,12},{... | collective-permute-start | bytes 1179656 | tf_op jit(solution)/shard_map/ppermute | solution.py:508
  517.0 190.7 %reduce-scatter.15.cloned.1.call-start = ((), (), s32[]{:S(2)}) async-start(), calls=%async_computation.16 | async-start | bytes 2621440 | tf_op jit(solution)/shard_map/reduce_scatter | solution.py:529
  522.9 4.3 copy-start.41
  522.9 4.3 copy-start.46
  524.0 6.0 copy-start.39
  524.0 6.0 copy-start.43
  527.2 4.2 copy-start.13
  527.2 4.4 copy-start.32
  527.2 4.4 copy-start.35
  531.6 7.5 copy-start.37
  540.6 231.9 %all-gather.21.cloned.1.call-start = ((), (), s32[]{:S(2)}) async-start(), calls=%async_computation.25 | async-start | bytes 3932160 | tf_op jit(solution)/shard_map/all_gather | solution.py:531
  558.1 278.6 %all-gather.19.cloned.1.call-start = ((), (), s32[]{:S(2)}) async-start(), calls=%async_computation.24 | async-start | bytes 3932160 | tf_op jit(solution)/shard_map/all_gather | solution.py:531
  587.1 313.6 %all-gather.17.cloned.1.call-start = ((), (), s32[]{:S(2)}) async-start(), calls=%async_computation.23 | async-start | bytes 3932160 | tf_op jit(solution)/shard_map/all_gather | solution.py:531
  650.2 72.3 %copy-start.36 = (bf16[1536,128]{0,1:T(8,128)(2,1)S(1)}, bf16[1536,128]{0,1:T(8,128)(2,1)}, u32[]{:S(2)}) copy-start(bf16[1536,128]{0,1:T(8,128)(2,1)} %copy.185) | copy-start | bytes 1179652
  650.2 278.6 %all-gather.13.cloned.1.call-start = ((), (), s32[]{:S(2)}) async-start(), calls=%async_computation.18 | async-start | bytes 1310720 | tf_op jit(solution)/shard_map/all_gather | solution.py:536
  662.8 312.7 %all-gather.15.cloned.1.call-start = ((), (), s32[]{:S(2)}) async-start(), calls=%async_computation.22 | async-start | bytes 2621440 | tf_op jit(solution)/shard_map/all_gather | solution.py:531
  722.2 267.6 %reduce-scatter.13.cloned.1.call-start = ((), (), s32[]{:S(2)}) async-start(), calls=%async_computation.15 | async-start | bytes 7077888 | tf_op jit(solution)/shard_map/reduce_scatter | solution.py:436
  730.4 300.8 %reduce-scatter.9.cloned.1.call-start = ((), (), s32[]{:S(2)}) async-start(), calls=%async_computation.12 | async-start | bytes 7077888 | tf_op jit(solution)/shard_map/reduce_scatter | solution.py:436
  984.3 5.6 copy-start.9
  1031.2 4.0 copy-start.1
  (26 other events, 46.8 us)
Sparse Core Ops, SparseCore 0:
  371.4 61.8 reduce-scatter.10
  436.6 45.5 all-gather.10
  730.5 59.1 reduce-scatter.12
  793.0 61.7 reduce-scatter.8
Sparse Core Ops, SparseCore 1:
  446.8 60.2 reduce-scatter.22
  509.4 60.2 reduce-scatter.20
  572.4 60.2 reduce-scatter.18
  635.7 27.1 reduce-scatter.16
  665.7 42.0 reduce-scatter.14
  710.0 62.5 all-gather.20
  774.6 62.0 all-gather.18
  838.8 62.0 all-gather.16
  902.3 26.5 all-gather.12
  930.5 44.9 all-gather.14

commit v3 on v2

--- a/solution.py
+++ b/solution.py
@@ -24,7 +24,8 @@
 VMEM = pl.BlockSpec(memory_space=pltpu.VMEM)
 DMA = pltpu.SemaphoreType.DMA
 STRIP = 16
-LAG = 3
+LAG_MID = 2
+LAG_END = 6
 
 
 class Place:
@@ -43,6 +44,15 @@
     def to(self, k):
         return lax.rem(self.f + k, self.n)
 
+    def near(self, j):
+        return 2 * lax.rem(self.chip + j // 2, self.chips) + lax.rem(self.core + lax.rem(j, 2), 2)
+
+    def near_from(self, j):
+        return 2 * lax.rem(self.chip + self.chips - j // 2, self.chips) + lax.rem(self.core + lax.rem(j, 2), 2)
+
+    def plane(self, k):
+        return lax.rem(self.z + k, self.n_z)
+
     def chip_at(self, k):
         return lax.rem(self.chip + k, self.chips)
 
@@ -51,14 +61,10 @@
         for k in range(1, self.n):
             pl.semaphore_signal(barrier, inc=1, device_id={"fsdp": self.to(k)}, device_id_type=MESH)
         if line:
-            pl.semaphore_signal(barrier, inc=1, device_id={"replica": self.inner}, device_id_type=MESH)
-
-            @pl.when(self.has_outer)
-            def _():
-                pl.semaphore_signal(barrier, inc=1, device_id={"replica": self.outer}, device_id_type=MESH)
-                pl.semaphore_wait(barrier, 1)
-
-        pl.semaphore_wait(barrier, self.n - 1 + int(line))
+            for k in range(1, self.n_z):
+                pl.semaphore_signal(barrier, inc=1, device_id={"replica": self.plane(k)}, device_id_type=MESH)
+
+        pl.semaphore_wait(barrier, self.n - 1 + (self.n_z - 1 if line else 0))
 
 
 def remote(src, dst, send, recv, axis, index):
@@ -196,13 +202,16 @@
 
         self.inward(j).start()
 
-    def down(self, j):
+    def meet(self, j):
         self.here(1, j).wait()
-
-        @pl.when(self.at.mid)
-        def _():
-            self.came[1, j] = (self.chunk[j].astype(F32) + self.came[1, j].astype(F32)).astype(BF)
-
+        self.came[1, j] = (self.chunk[j].astype(F32) + self.came[1, j].astype(F32)).astype(BF)
+        self.pass_on(j)
+
+    def take(self, j):
+        self.here(1, j).wait()
+        self.pass_on(j)
+
+    def pass_on(self, j):
         @pl.when(self.at.has_outer)
         def _():
             self.outward(j, self.came.at[1, j]).start()
@@ -223,25 +232,47 @@
         lax.fori_loop(0, self.count, step, 0)
 
 
-def run_line(line, first, last):
-    lag = min(LAG, last - first)
-
-    def head(j, carry):
-        line.up(j)
-        return carry
-
-    def body(j, carry):
-        line.up(j)
-        line.down(j - lag)
-        return carry
-
-    def tail(j, carry):
-        line.down(j)
-        return carry
-
-    lax.fori_loop(first, first + lag, head, 0)
-    lax.fori_loop(first + lag, last, body, 0)
-    lax.fori_loop(last - lag, last, tail, 0)
+class Lines:
+    def __init__(self, *lines):
+        self.lines = lines
+        self.order = [(i, j) for i, line in enumerate(lines) for j in range(line.count)]
+        self.at = 0
+
+    def run(self, steps=None):
+        last = len(self.order) + LAG_END
+        stop = last if steps is None else min(self.at + steps, len(self.order))
+        while self.at < stop:
+            first, size = self.at, 1
+            now = self.parts(first)
+            while first + size < stop and self.kinds(first + size) == self.kinds(first):
+                size += 1
+
+            def step(m, carry, now=now):
+                up, mid, rest = now
+                if up:
+                    self.lines[up[0]].up(up[1] + m)
+                if mid:
+                    @pl.when(self.lines[mid[0]].at.mid)
+                    def _():
+                        self.lines[mid[0]].meet(mid[1] + m)
+                if rest:
+                    @pl.when(jnp.logical_not(self.lines[rest[0]].at.mid))
+                    def _():
+                        self.lines[rest[0]].take(rest[1] + m)
+                return carry
+
+            lax.fori_loop(0, size, step, 0)
+            self.at += size
+
+    def parts(self, t):
+        return [self.order[i] if 0 <= i < len(self.order) else None for i in (t, t - LAG_MID, t - LAG_END)]
+
+    def kinds(self, t):
+        return [part and part[0] for part in self.parts(t)]
+
+    def settle(self):
+        for line in self.lines:
+            line.settle()
 
 
 def rms_of(values):
@@ -358,6 +389,158 @@
 
 def norm_back(d_normed, normed, rms):
     return rms * (d_normed - normed * jnp.mean(d_normed * normed, axis=-1, keepdims=True))
+
+
+def grad_chunks(at, grad, chunk, send, recv):
+    depth = chunk.shape[1]
+
+    def rows(t):
+        return grad.at[pl.ds(pl.multiple_of(t * depth, depth), depth)]
+
+    copies = [pltpu.make_async_copy(rows(at.f), chunk.at[0], recv.at[0])]
+    for j in range(1, at.n):
+        copies.append(remote(rows(at.near(j)), chunk.at[j], send.at[j], recv.at[j], "fsdp", at.near(j)))
+    return copies
+
+
+def start_all(copies):
+    for c in copies:
+        c.start()
+
+
+def sends_done(copies):
+    for c in copies[1:]:
+        c.wait_send()
+
+
+def turn_kernel(n, n_z, part_ref, h_ref, g_ref, gain_ref, down_ref,
+                dh_ref, dhall_ref, dgain_ref, gdown_ref,
+                near, mine, far, own, chunk, came, s_r, s_a, s_c, r_c, s_z, r_z, s_o):
+    at = Place(n, n_z)
+    share = chunk.shape[2]
+    at.greet(True)
+    total = ScatterSum(at, part_ref, near, mine, far, s_r)
+    down = grad_chunks(at, down_ref, chunk, s_c, r_c)
+    lines = Lines(LineSum(at, chunk, came, r_c, s_z, r_z, by_sender(at, gdown_ref, share), s_o))
+    half = at.n // 2
+    total.start()
+    start_all(down[:half])
+    lines.run(2)
+    total.forward()
+    lines.run(half - 2)
+    total.wait()
+    start_all(down[half:])
+    dgain_ref[...] = jnp.zeros_like(dgain_ref)
+
+    def back(strip):
+        d_n2 = total.total(strip)
+        h = h_ref[strip]
+        r2 = rms_of(h)
+        u2 = h * r2
+        dgain_ref[...] += jnp.sum(d_n2 * u2, axis=0, keepdims=True)
+        d_h = g_ref[strip].astype(F32) + norm_back(d_n2 * gain_ref[...], u2, r2)
+        dh_ref[strip] = d_h
+        own[strip] = d_h.astype(BF)
+
+    strips(h_ref.shape[0], back)
+    gather = Gather(at, own, dhall_ref, s_a)
+    gather.start()
+    lines.run(half)
+    gather.forward()
+    lines.run()
+    gather.wait()
+    sends_done(down)
+    lines.settle()
+
+
+def by_sender(at, ref, share):
+    def place(j):
+        return ref.at[:, pl.ds(pl.multiple_of(at.near_from(j) * share, HEAD_WIDTH), share)]
+
+    return place
+
+
+def end_kernel(n, n_z, part_ref, party_ref, x_ref, h_ref, dh_ref, gain_ref, dgain_ref, dheads_ref,
+               gate_ref, up_ref, qkv_ref, gout_ref,
+               dx_ref, y_ref, gains_ref, ggate_ref, gup_ref, gqkv_ref, ggout_ref,
+               near, mine, far, ynear, ymine, yfar, own_gain, plane_gain, line_gain, all_gain,
+               gate_k, gate_m, up_k, up_m, qkv_k, qkv_m, out_k, out_m,
+               s_r, s_y, s_p, r_p, s_q, r_q, s_c, r_c, s_z, r_z, s_o, s_l, r_l):
+    at = Place(n, n_z)
+    share, share_out = gate_k.shape[2], out_k.shape[2]
+    rows = x_ref.shape[0]
+    at.greet(True)
+
+    def line(i, chunk, came, place, arrive):
+        return LineSum(at, chunk, came, arrive, s_z.at[i], r_z.at[i], place, s_o.at[i])
+
+    gate = grad_chunks(at, gate_ref, gate_k, s_c.at[0], r_c.at[0])
+    up = grad_chunks(at, up_ref, up_k, s_c.at[1], r_c.at[1])
+    qkv = grad_chunks(at, qkv_ref, qkv_k, s_c.at[2], r_c.at[2])
+
+    def out_cols(ref):
+        return lambda j: ref.at[:, pl.ds(pl.multiple_of(j * share_out, HEAD_WIDTH), share_out)]
+
+    outs = [pltpu.make_async_copy(out_cols(gout_ref)(j), out_k.at[j], r_l.at[j]) for j in range(out_k.shape[0])]
+
+    def qkv_place(j):
+        return gqkv_ref.at[at.near_from(j)]
+
+    lines = Lines(
+        line(3, out_k, out_m, out_cols(ggout_ref), r_l),
+        line(0, gate_k, gate_m, by_sender(at, ggate_ref, share), r_c.at[0]),
+        line(1, up_k, up_m, by_sender(at, gup_ref, share), r_c.at[1]),
+        line(2, qkv_k, qkv_m, qkv_place, r_c.at[2]),
+    )
+    start_all(outs)
+    total = ScatterSum(at, part_ref, near, mine, far, s_r)
+    y = ScatterSum(at, party_ref, ynear, ymine, yfar, s_y)
+    start_all(gate)
+    total.start()
+    lines.run(out_k.shape[0])
+    total.forward()
+    start_all(up)
+    lines.run(n - 2)
+    total.wait()
+    own_gain[...] = jnp.zeros_like(own_gain)
+    own_gain[1:2] = dgain_ref[...]
+    own_gain[2:3, :2 * HEAD_WIDTH] = dheads_ref[...]
+
+    def back(strip):
+        d_n1 = total.total(strip)
+        x = x_ref[strip].astype(F32)
+        r1 = rms_of(x)
+        u1 = x * r1
+        own_gain[0:1] += jnp.sum(d_n1 * u1, axis=0, keepdims=True)
+        dx_ref[strip] = (dh_ref[strip] + norm_back(d_n1 * gain_ref[...], u1, r1)).astype(BF)
+
+    strips(rows, back)
+    gains = Exchange(at, [(lambda t: own_gain, lambda s: plane_gain.at[s])], s_p, r_p)
+    gains.start()
+    y.start()
+    lines.run(4)
+    y.forward()
+    start_all(qkv)
+    lines.run(4)
+    gains.wait()
+    line_gain[...] = jnp.sum(plane_gain[...], axis=0)
+    others = [
+        remote(line_gain, all_gain.at[at.z], s_q.at[k], r_q.at[k], "replica", at.plane(k)) for k in range(1, n_z)]
+    start_all(others)
+    all_gain[at.z] = line_gain[...]
+    y.wait()
+
+    def finish(strip):
+        y_ref[strip] = (h_ref[strip] + y.total(strip)).astype(BF)
+
+    strips(rows, finish)
+    lines.run()
+    for c in others:
+        c.wait()
+    gains_ref[...] = jnp.sum(all_gain[...], axis=0)
+    for copies in (gate, up, qkv):
+        sends_done(copies)
+    lines.settle()
 
 
 def begin(n, n_z, x, gain, place, w_qkv):
@@ -402,6 +585,62 @@
     )(part, x, gain, g, gate, up, down)
 
 
+def turn(n, n_z, part, h, g, gain, down):
+    rows, width = h.shape
+    chips, share, depth = n // 2, down.shape[1], width // n
+    block = functools.partial(pltpu.VMEM, dtype=BF)
+    return pl.pallas_call(
+        functools.partial(turn_kernel, n, n_z),
+        out_shape=(
+            jax.ShapeDtypeStruct((rows, width), F32),
+            jax.ShapeDtypeStruct((n * rows, width), BF),
+            jax.ShapeDtypeStruct((1, width), F32),
+            jax.ShapeDtypeStruct((depth, n * share), BF),
+        ),
+        in_specs=[ANY, VMEM, VMEM, VMEM, ANY],
+        out_specs=(VMEM, ANY, VMEM, ANY),
+        scratch_shapes=[
+            block((chips, rows, width)), block((chips, rows, width)), block((chips - 1, rows, width)), block((rows, width)),
+            block((n, depth, share)), block((2, n, depth, share)),
+            DMA((5, n)), DMA((6, n)), DMA((n,)), DMA((n,)), DMA((2, n)), DMA((2, n)), DMA((n,))],
+        compiler_params=pltpu.CompilerParams(collective_id=2, has_side_effects=True, vmem_limit_bytes=56 << 20),
+        name="turn",
+    )(part, h, g, gain, down)
+
+
+def end(n, n_z, part, part_y, x, h, d_h, gain, d_gain, d_heads, gate, up, qkv, out):
+    rows, width = x.shape
+    chips, share, share_qkv, depth = n // 2, gate.shape[1], qkv.shape[1], width // n
+    share_out = 4 * HEAD_WIDTH
+    outs = width // share_out
+    block = functools.partial(pltpu.VMEM, dtype=BF)
+    sums = [block((chips, rows, width)), block((chips, rows, width)), block((chips - 1, rows, width))]
+    gains = (8, width)
+    return pl.pallas_call(
+        functools.partial(end_kernel, n, n_z),
+        out_shape=(
+            jax.ShapeDtypeStruct((rows, width), BF),
+            jax.ShapeDtypeStruct((rows, width), BF),
+            jax.ShapeDtypeStruct(gains, F32),
+            jax.ShapeDtypeStruct((depth, n * share), BF),
+            jax.ShapeDtypeStruct((depth, n * share), BF),
+            jax.ShapeDtypeStruct((n, depth, share_qkv), BF),
+            jax.ShapeDtypeStruct((depth, width), BF),
+        ),
+        in_specs=[ANY, ANY] + [VMEM] * 6 + [ANY] * 4,
+        out_specs=(VMEM, VMEM, VMEM, ANY, ANY, ANY, ANY),
+        scratch_shapes=sums + sums + [
+            pltpu.VMEM(gains, F32), pltpu.VMEM((n,) + gains, F32), pltpu.VMEM(gains, F32), pltpu.VMEM((n_z,) + gains, F32),
+            block((n, depth, share)), block((2, n, depth, share)), block((n, depth, share)), block((2, n, depth, share)),
+            block((n, depth, share_qkv)), block((2, n, depth, share_qkv)),
+            block((outs, depth, share_out)), block((2, outs, depth, share_out)),
+            DMA((5, n)), DMA((5, n)), DMA((1, n)), DMA((1, n)), DMA((n_z,)), DMA((n_z,)),
+            DMA((3, n)), DMA((3, n)), DMA((4, 2, n)), DMA((4, 2, n)), DMA((4, n)), DMA((outs,)), DMA((outs,))],
+        compiler_params=pltpu.CompilerParams(collective_id=3, has_side_effects=True, vmem_limit_bytes=60 << 20),
+        name="end",
+    )(part, part_y, x, h, d_h, gain, d_gain, d_heads, gate, up, qkv, out)
+
+
 def row_positions(flat_lens, ranks, first_row, count):
     earlier = (ranks[:, None] < ranks[None, :]).astype(jnp.int32)
     starts = jnp.sum(flat_lens[:, None] * earlier, axis=0)
@@ -429,16 +668,6 @@
     n1, w_qkv_c, places = begin(n_fsdp, n_replica, tokens, gain_attn[None], place, w_qkv)
     pos_all = places.reshape(n_fsdp, -1)[:, :rows].reshape(-1)
 
-    def gather(a):
-        return lax.all_gather(a, "fsdp", axis=0, tiled=True)
-
-    def scatter_sum(a):
-        return lax.psum_scatter(a.astype(BF), "fsdp", scatter_dimension=0, tiled=True).astype(F32)
-
-    x = tokens.astype(F32)
-    g = cotangent.astype(F32)
-    r1 = lax.rsqrt(jnp.mean(x * x, axis=1, keepdims=True) + EPSILON)
-    u1 = x * r1
     total = n1.shape[0]
 
     proj = dot(n1, w_qkv_c)
@@ -480,23 +709,20 @@
     h, n2, g_all, gate_c, up_c, down_c = middle(
         n_fsdp, n_replica, dot(ctx_low, w_out).astype(BF), tokens, gain_mlp[None], cotangent, w_gate, w_up, w_down_t)
 
-    r2 = lax.rsqrt(jnp.mean(h * h, axis=1, keepdims=True) + EPSILON)
-    u2 = h * r2
     gate = dot(n2, gate_c)
     up = dot(n2, up_c)
     sg = jax.nn.sigmoid(gate)
     silu = gate * sg
     act = (silu * up).astype(BF)
-    output = (h + scatter_sum(dot_cols(act, down_c))).astype(BF)
+    part_y = dot_cols(act, down_c).astype(BF)
 
     d_act = dot(g_all, down_c)
     d_gate = (d_act * up * sg * (1.0 + gate * (1.0 - sg))).astype(BF)
     d_up = (d_act * silu).astype(BF)
 
-    d_n2 = scatter_sum(dot_cols(d_gate, gate_c) + dot_cols(d_up, up_c))
-    d_gain_mlp = jnp.sum(d_n2 * u2, axis=0)
-    d_h = g + norm_back(d_n2 * gain_mlp, u2, r2)
-    dh_all = gather(d_h.astype(BF))
+    d_h, dh_all, d_gain_mlp, g_down = turn(
+        n_fsdp, n_replica, (dot_cols(d_gate, gate_c) + dot_cols(d_up, up_c)).astype(BF), h, cotangent, gain_mlp[None],
+        dot_rows(g_all, act).astype(BF))
     d_ctx = dot_cols(dh_all, w_out).astype(BF).reshape(groups, rows, heads, HEAD_WIDTH)
     d_v = jnp.einsum("ghqk,gqhd->gkd", probs_low, d_ctx, preferred_element_type=F32)
     d_p = jnp.einsum("gqhd,gkd->ghqk", d_ctx, v_win, preferred_element_type=F32)
@@ -518,28 +744,12 @@
     dq = norm_back(dq_g * gain_query, q_hat, rq)
     dk = norm_back(dk_g * gain_key, k_hat, rk)
     d_proj = jnp.concatenate([dq.reshape(total, qw), dk, d_v], axis=1).astype(BF)
-    d_n1 = scatter_sum(dot_cols(d_proj, w_qkv_c))
-    d_gain_attn = jnp.sum(d_n1 * u1, axis=0)
-    input_grad = (d_h + norm_back(d_n1 * gain_attn, u1, r1)).astype(BF)
-
-    def reduce_cols(grad):
-        share = grad.shape[1]
-        low = grad.astype(BF).reshape(n_fsdp, n_replica, width // n_fsdp // n_replica, share)
-        low = low.transpose(1, 0, 2, 3).reshape(width, share)
-        part = lax.psum_scatter(low, "replica", scatter_dimension=0, tiled=True)
-        part = lax.all_to_all(part.reshape(n_fsdp, -1, share), "fsdp", split_axis=0, concat_axis=1)
-        whole = lax.all_gather(part, "replica", axis=0, tiled=True)
-        return whole.astype(F32)
-
-    def reduce_rows(grad):
-        low = lax.psum_scatter(grad.astype(BF), "replica", scatter_dimension=0, tiled=True)
-        return lax.all_gather(low, "replica", axis=0, tiled=True).astype(F32)
-
-    g_down = reduce_cols(dot_rows(g_all, act)).reshape(depth, -1)
-    g_gate = reduce_cols(dot_rows(n2, d_gate)).reshape(depth, -1)
-    g_up = reduce_cols(dot_rows(n2, d_up)).reshape(depth, -1)
-    g_out = reduce_rows(dot_rows(ctx_low, dh_all))
-    g_qkv = reduce_cols(dot_rows(n1, d_proj))
+    d_heads = jnp.concatenate([d_gain_query, d_gain_key])[None]
+    input_grad, output, gains, g_gate, g_up, g_qkv, g_out = end(
+        n_fsdp, n_replica, dot_cols(d_proj, w_qkv_c).astype(BF), part_y, tokens, h, d_h, gain_attn[None], d_gain_mlp, d_heads,
+        dot_rows(n2, d_gate).astype(BF), dot_rows(n2, d_up).astype(BF),
+        dot_rows(n1, d_proj).astype(BF), dot_rows(ctx_low, dh_all).astype(BF))
+    g_qkv = g_qkv.transpose(1, 0, 2).astype(F32)
 
     def of_key_heads(part):
         return jnp.sum(part.reshape(depth, KEY_VALUE_HEADS, shared, HEAD_WIDTH), axis=2).reshape(depth, k_w)
@@ -548,8 +758,9 @@
         g_qkv[:, :, :qw].reshape(depth, q_w),
         of_key_heads(g_qkv[:, :, qw:qw + HEAD_WIDTH]),
         of_key_heads(g_qkv[:, :, qw + HEAD_WIDTH:])], axis=1)
-    sums = lax.psum((d_gain_attn, d_gain_mlp, d_gain_query, d_gain_key), ("fsdp", "replica"))
-    return (output, input_grad, g_qkv, g_out, g_gate, g_up, g_down) + tuple(sums)
+    return (
+        output, input_grad, g_qkv, g_out.astype(F32), g_gate.astype(F32), g_up.astype(F32), g_down.astype(F32),
+        gains[0], gains[1], gains[2, :HEAD_WIDTH], gains[2, HEAD_WIDTH:2 * HEAD_WIDTH])
 
 
 def solution(mesh):

time: 1050 us -> 897 us (0.85)
  Pallas kernels: 276 us -> 674 us
  waiting for transfers between devices: 370 us -> 0.01 us
  blocking collectives: 101 us -> 0 us
  local copies, waits for them, and re-layouts: 88.7 us -> 44.5 us
  between operations: 16.4 us -> 1.99 us
  other arithmetic: 60.4 us -> 46.7 us
    pallas_call x0 -> x2, Pallas kernels: none -> 398 us  [the longest x1 261 us: end(): pl.pallas_call(functools.partial(end_kernel, n, n_z), out_shape=(jax.Shap...]
    all_gather x6 -> x0, waiting for transfers between devices: 194 us -> none  [the longest x4 169 us: reduce_cols(): whole = lax.all_gather(part, 'replica', axis=0, tiled=True)]
    reduce_scatter x8 -> x0, waiting for transfers between devices: 176 us -> none  [the longest x4 102 us: reduce_cols(): part = lax.psum_scatter(low, 'replica', scatter_dimension=0, tiled=True)]
    all_to_all x4 -> x0, blocking collectives: 61.8 us -> none  [reduce_cols(): lax.all_to_all(part.reshape(n_fsdp, -1, share), 'fsdp', split_axis=0, con...]
    psum x1 -> x0, blocking collectives: 39.5 us -> none  [per_device(): lax.psum((d_gain_attn, d_gain_mlp, d_gain_query, d_gain_key), ('fsdp', 'r...]
    unnamed x121 -> x120, local copies, waits for them, and re-layouts: 39.5 us -> 16 us
    all_gather x4 -> x0, local copies, waits for them, and re-layouts: 19 us -> none  [reduce_cols(): whole = lax.all_gather(part, 'replica', axis=0, tiled=True)]
    reshape x3 -> x0, other arithmetic: 16 us -> none  [the longest x1 5.64 us: per_device(): g_up = reduce_cols(dot_rows(n2, d_up)).reshape(depth, -1)]
  transfers between devices with their start and end apart: 16 -> 2, of which waited for: 11 -> 0; matrix products, arithmetic and copies ran while one was open for 18% -> 3% of each run, Pallas kernels for 0% -> 0%
where the time goes in v3:
time: 897 us; the launch traced here: 890 us
  Pallas kernels  674 us (75%)
  matrix products  117 us (13%)
  other arithmetic  46.7 us (5%)
  local copies, waits for them, and re-layouts  44.5 us (5%)
    pallas_call x1, Pallas kernels, end(): pl.pallas_call(functools.partial(end_kernel, n, n_z), out_shape=(jax.Shap...  261 us
    pallas_call x1, Pallas kernels, middle(): pl.pallas_call(functools.partial(middle_kernel, n, n_z), out_shape=(jax.S...  210 us
    pallas_call x1, Pallas kernels, turn(): pl.pallas_call(functools.partial(turn_kernel, n, n_z), out_shape=(jax.Sha...  138 us
    pallas_call x1, Pallas kernels, begin(): pl.pallas_call(functools.partial(begin_kernel, n, n_z), out_shape=(jax.Sh...  66.1 us
    dot_general x5, matrix products, dot_cols(): lax.dot_general(left, right, (((1,), (1,)), ((), ())), preferred_element_...  35.7 us
    dot_general x5, matrix products, dot(): return jnp.dot(left, right, preferred_element_type=F32)  33.6 us
    dot_general x5, matrix products, dot_rows(): lax.dot_general(left, right, (((0,), (0,)), ((), ())), preferred_element_...  33.3 us
  transfers between devices with their start and end apart: 2, of which 0 were waited for; matrix products, arithmetic and copies ran while one was open for 3% of the time, Pallas kernels for 0%

profile of v3, /device:TPU:0, one launch (start us, length us, event | category | flops | bytes accessed | tf_op | source)
XLA Modules:
  0.0 889.7 jit_solution(13253764789427323073)
XLA Ops:
  3.6 1.6 copy-done.5
  5.9 66.1 %begin.1 = (bf16[1536,2048]{1,0:T(8,128)(2,1)S(1)}, bf16[2048,512]{1,0:T(8,128)(2,1)S(1)}, s32[8,8,128]{2,1,0:T(8,128)S(1)}) custom-call(bf16[192,2048]{1,0:T(8,128)(2,1)S(1)} %copy-done.1, f32[1,2048]{1,0:T(1,128)S(1)} %bitcast.139, s32[8,128]{1,0:T(8,128)S(1)} %pad_bitcast_fusion.place_ref, bf16[256,4096]{1,0:T(8,128)(2,1)S(1)} %copy-done.5), custom_call_target="tpu_custom_call" | custom-call | tf_op jit(solution)/shard_map/begin/pallas_call | solution.py:549
  72.0 3.6 fusion.67
  78.7 2.5 fusion.41
  82.3 4.2 collective-permute-start
  88.2 2.3 copy.70
  90.5 2.1 copy.59
  92.6 2.1 copy.60
  94.8 1.7 copy.58
  96.5 2.0 multiply_multiply_fusion
  100.3 1.8 fusion.28
  102.1 2.6 fusion.66
  104.8 2.2 fusion.14
  107.8 4.5 convolution_convert_fusion.1.part_ref
  112.3 209.6 %middle.1 = (f32[192,2048]{1,0:T(8,128)S(1)}, bf16[1536,2048]{1,0:T(8,128)(2,1)}, bf16[1536,2048]{1,0:T(8,128)(2,1)}, bf16[2048,768]{1,0:T(8,128)(2,1)}, bf16[20...) custom-call(bf16[1536,2048]{1,0:T(8,128)(2,1)} %convolution_convert_fusion.1.part_ref, bf16[192,2048]{1,0:T(8,128)(2,1)S(1)} %copy-done.2, ...), custom_call_target="tpu_custom_call" | custom-call | tf_op jit(solution)/shard_map/middle/pallas_call | solution.py:569
  322.0 8.7 fusion.68
  330.7 6.6 fusion.69
  337.4 10.1 %multiply_convert_fusion = (bf16[1536,768]{1,0:T(8,128)(2,1)}, bf16[1536,768]{1,0:T(8,128)(2,1)}, bf16[1536,768]{1,0:T(8,128)(2,1)}) fusion(f32[1536,768]{1,0:T(8,128)} %fusion.69, f32[1536,768]{1,0:T(8,128)S(1)} %fusion.68, bf16[1536,2048]{1,0:T(8,128)(2,1)S(1)} %copy-done.44, bf16[2048,768]{1,0:T(8,128)(2,1)S(1)} %copy-done.45), kind=kOutput, calls=%fused_computation.11 | convolution fusion | flops 4849532928 | bytes 25952256 | tf_op jit(solution)/shard_map/dot_general | solution.py:365
  347.5 8.8 convolution_convert_fusion.5.down_ref
  356.4 7.1 convolution_convert_fusion.party_ref
  363.4 6.5 convolution_convert_fusion.4.gate_ref
  370.0 7.9 fusion.70
  377.9 6.7 convolution_convert_fusion.3.up_ref
  384.6 9.8 %add_convert_fusion.part_ref = bf16[1536,2048]{1,0:T(8,128)(2,1)} fusion(f32[1536,2048]{1,0:T(8,128)} %fusion.70, bf16[1536,768]{1,0:T(8,128)(2,1)S(1)} %copy-done.49, bf16[2048,768]{1,0:T(8,128)(2,1)S(1)} %copy-done.45), kind=kOutput, calls=%fused_computation.1 | convolution fusion | flops 4838129664 | bytes 24379392 | tf_op jit(solution)/shard_map/dot_general | solution.py:373
  394.4 137.7 %turn.1 = (f32[192,2048]{1,0:T(8,128)}, bf16[1536,2048]{1,0:T(8,128)(2,1)}, f32[1,2048]{1,0:T(1,128)}, bf16[256,6144]{1,0:T(8,128)(2,1)}) custom-call(bf16[1536,2048]{1,0:T(8,128)(2,1)} %add_convert_fusion.part_ref, f32[192,2048]{1,0:T(8,128)} %copy-done.3, bf16[192,2048]{1,0:T(8,128)(2,1)} %g_ref.3, f32[1,2048]{1,0:T(1,128)} %bitcast.136, ...), custom_call_target="tpu_custom_call" | custom-call | tf_op jit(solution)/shard_map/turn/pallas_call | solution.py:592
  532.1 5.5 convolution_convert_fusion.8
  537.6 2.9 reshape.257
  540.5 3.4 convolution_bitcast_fusion
  544.0 3.7 fusion.1
  550.0 2.2 multiply_bitcast_fusion
  553.7 2.0 multiply_reduce_fusion
  557.9 1.9 copy.71
  559.8 3.0 fusion.12
  562.8 5.5 convert_element_type.118
  568.4 2.8 convolution_convert_fusion.7.gout_ref
  574.2 1.9 fusion.48
  577.7 8.4 convolution_convert_fusion.6.qkv_ref
  586.1 5.4 convolution_convert_fusion.2.part_ref
  592.1 260.8 %end.1 = (bf16[192,2048]{1,0:T(8,128)(2,1)}, bf16[192,2048]{1,0:T(8,128)(2,1)}, f32[8,2048]{1,0:T(8,128)}, bf16[256,6144]{1,0:T(8,128)(2,1)}, bf16[256,6144]{1,0...) custom-call(bf16[1536,2048]{1,0:T(8,128)(2,1)} %convolution_convert_fusion.2.part_ref, ...), custom_call_target="tpu_custom_call" | custom-call | tf_op jit(solution)/shard_map/end/pallas_call | solution.py:619
  855.6 2.2 convert_bitcast_fusion
  860.4 1.6 convert_element_type.115
  862.0 2.6 copy.77
  864.6 1.8 copy.76
  866.4 2.7 copy.78
  869.1 3.8 pad_maximum_fusion
  872.9 5.6 copy.79
  878.5 5.5 convert_element_type.116
  884.0 3.4 convert_element_type.117
  (171 shorter events, 30.1 us)
Async XLA Ops:
  0.6 107.1 %copy-start = (bf16[256,2048]{1,0:T(8,128)(2,1)S(1)}, bf16[256,2048]{1,0:T(8,128)(2,1)}, u32[]{:S(2)}) copy-start(bf16[256,2048]{1,0:T(8,128)(2,1)} %param.18) | copy-start | bytes 3145732
  0.7 78.1 %copy-start.42 = (f32[64]{0:T(128)}, f32[64]{0:T(128)S(1)}, u32[]{:S(2)}) copy-start(f32[64]{0:T(128)S(1)} %multiply_power_fusion) | copy-start | bytes 772
  72.0 3.7 copy-start.8
  72.0 3.7 copy-start.9
  72.0 5.4 copy-start.39
  77.5 3.8 copy-start.37
  77.5 3.7 copy-start.35
  82.3 17.3 %collective-permute-start = (bf16[8,96,256]{2,1,0:T(8,128)(2,1)}, bf16[8,96,256]{2,1,0:T(8,128)(2,1)}, u32[]{:S(2)}, u32[]{:S(2)}) collective-permute-start(bf16[8,96,256]{2,1,0:T(8,128)(2,1)} %slice.131), channel_id=1, source_target_pairs={{0,1},{1,2},{2,3},{4,5},{5,6},{6,7},{8,9},{9,10},{10,11},{12,13},{... | collective-permute-start | bytes 1179656 | tf_op jit(solution)/shard_map/ppermute | solution.py:690
  88.2 6.6 slice-start
  88.2 8.3 copy-start.41
  104.8 2.2 copy-start.17
  107.8 4.5 copy-start.2
  107.8 4.5 copy-start.4
  107.8 4.5 copy-start.6
  322.0 8.7 copy-start.3
  322.0 8.7 copy-start.44
  322.0 8.7 copy-start.46
  330.7 6.6 copy-start.45
  330.7 16.8 %slice-start.6 = ((s8[6291456]{0:T(1024)(128)(4,1)}), s8[4194304]{0:T(1024)(128)(4,1)S(1)}, s32[]{:S(2)}) async-start(s8[6291456]{0:T(1024)(128)(4,1)} %bitcast.168), calls=%async_computation.6 | async-start | bytes 8388608
  337.4 10.1 %slice-start.7 = ((s8[6291456]{0:T(1024)(128)(4,1)}), s8[2097152]{0:T(1024)(128)(4,1)S(1)}, s32[]{:S(2)}) async-start(s8[6291456]{0:T(1024)(128)(4,1)} %bitcast.168), calls=%async_computation.7 | async-start | bytes 4194304
  347.5 8.9 copy-start.47
  347.5 8.9 copy-start.50
  356.4 7.1 copy-start.48
  370.0 7.9 copy-start.49
  540.5 3.4 copy-start.33
  540.5 7.2 slice-start.4
  543.9 11.9 %copy-start.18 = (f32[8,288,128]{2,1,0:T(8,128)}, f32[8,288,128]{2,1,0:T(8,128)S(1)}, u32[]{:S(2)}) copy-start(f32[8,288,128]{2,1,0:T(8,128)S(1)} %convolution_bitcast_fusion) | copy-start | bytes 3538948
  544.0 3.8 slice-start.5
  550.0 5.8 copy-start.20
  550.0 2.3 copy-start.28
  556.6 14.5 %collective-permute-start.1 = (bf16[8,96,256]{2,1,0:T(8,128)(2,1)}, bf16[8,96,256]{2,1,0:T(8,128)(2,1)}, u32[]{:S(2)}, u32[]{:S(2)}) collective-permute-start(bf16[8,96,256]{2,1,0:T(8,128)(2,1)} %fusion.24), channel_id=1, source_target_pairs={{1,0},{2,1},{3,2},{5,4},{6,5},{7,6},{9,8},{10,9},{11,10},{13,12},{... | collective-permute-start | bytes 1179656 | tf_op jit(solution)/shard_map/ppermute | solution.py:734
  559.8 8.6 slice-start.1
  562.8 5.5 slice-start.2
  568.3 2.8 copy-start.19
  568.3 2.8 copy-start.21
  573.4 2.8 copy-start.36
  573.4 2.8 copy-start.40
  573.9 3.8 copy-start.30
  574.2 3.3 copy-start.12
  574.2 3.5 copy-start.34
  577.7 8.5 copy-start.10
  857.8 2.6 copy-start.13
  857.8 2.6 copy-start.29
  860.4 4.2 slice-start.3
  866.4 2.7 copy-start.15
  878.5 5.5 copy-start.27
  884.0 3.5 copy-start.32
  884.0 4.3 copy-start.31
  (13 other events, 18.5 us)

commit v4 on v2

--- a/solution.py
+++ b/solution.py
@@ -2,6 +2,7 @@
 
 import jax
 import jax.numpy as jnp
+import numpy as np
 from jax import lax
 from jax.experimental import pallas as pl
 from jax.experimental.pallas import tpu as pltpu
@@ -24,7 +25,10 @@
 VMEM = pl.BlockSpec(memory_space=pltpu.VMEM)
 DMA = pltpu.SemaphoreType.DMA
 STRIP = 16
-LAG = 3
+LAG_MID = 2
+LAG_END = 6
+RING = 4
+LEAD = 5
 
 
 class Place:
@@ -43,6 +47,15 @@
     def to(self, k):
         return lax.rem(self.f + k, self.n)
 
+    def near(self, j):
+        return 2 * lax.rem(self.chip + j // 2, self.chips) + lax.rem(self.core + lax.rem(j, 2), 2)
+
+    def near_from(self, j):
+        return 2 * lax.rem(self.chip + self.chips - j // 2, self.chips) + lax.rem(self.core + lax.rem(j, 2), 2)
+
+    def plane(self, k):
+        return lax.rem(self.z + k, self.n_z)
+
     def chip_at(self, k):
         return lax.rem(self.chip + k, self.chips)
 
@@ -51,14 +64,10 @@
         for k in range(1, self.n):
             pl.semaphore_signal(barrier, inc=1, device_id={"fsdp": self.to(k)}, device_id_type=MESH)
         if line:
-            pl.semaphore_signal(barrier, inc=1, device_id={"replica": self.inner}, device_id_type=MESH)
-
-            @pl.when(self.has_outer)
-            def _():
-                pl.semaphore_signal(barrier, inc=1, device_id={"replica": self.outer}, device_id_type=MESH)
-                pl.semaphore_wait(barrier, 1)
-
-        pl.semaphore_wait(barrier, self.n - 1 + int(line))
+            for k in range(1, self.n_z):
+                pl.semaphore_signal(barrier, inc=1, device_id={"replica": self.plane(k)}, device_id_type=MESH)
+
+        pl.semaphore_wait(barrier, self.n - 1 + (self.n_z - 1 if line else 0))
 
 
 def remote(src, dst, send, recv, axis, index):
@@ -124,7 +133,8 @@
 
 
 class ScatterSum:
-    def __init__(self, at, part, near, own, far, sem):
+    def __init__(self, at, part, near, own, far, sem, made=False):
+        self.made = made
         self.at, self.near, self.own, self.far = at, near, own, far
         rows = own.shape[1]
         self.rows = rows
@@ -135,8 +145,10 @@
         self.across, self.load, self.send = [], [], []
         for k in range(at.chips):
             q = at.chip_at(k)
-            self.across.append(remote(block(2 * q + 1 - at.core), near.at[k], sem.at[0, k], sem.at[1, k], "fsdp", at.sib))
-            self.load.append(pltpu.make_async_copy(block(2 * q + at.core), own.at[k], sem.at[2, k]))
+            other = part.at[k] if made else block(2 * q + 1 - at.core)
+            self.across.append(remote(other, near.at[k], sem.at[0, k], sem.at[1, k], "fsdp", at.sib))
+            if not made:
+                self.load.append(pltpu.make_async_copy(block(2 * q + at.core), own.at[k], sem.at[2, k]))
             if k:
                 self.send.append(
                     remote(own.at[k], far.at[k - 1], sem.at[3, k], sem.at[4, k], "fsdp", 2 * q + at.core))
@@ -144,12 +156,14 @@
     def start(self):
         for k in list(range(1, self.at.chips)) + [0]:
             self.across[k].start()
-            self.load[k].start()
+            if not self.made:
+                self.load[k].start()
 
     def forward(self):
         for k in list(range(1, self.at.chips)) + [0]:
             self.across[k].wait()
-            self.load[k].wait()
+            if not self.made:
+                self.load[k].wait()
 
             def add(at, k=k):
                 self.own[k, at] = (self.own[k, at].astype(F32) + self.near[k, at].astype(F32)).astype(BF)
@@ -170,78 +184,135 @@
 
 
 class LineSum:
-    def __init__(self, at, chunk, came, arrive, send, recv, out, out_sem):
-        self.at, self.chunk, self.came, self.arrive = at, chunk, came, arrive
-        self.send, self.recv, self.out, self.out_sem = send, recv, out, out_sem
+    def __init__(self, at, chunk, ring, arrive, send, recv, credit, out, out_sem, skip=0, feed=None):
+        self.at, self.chunk, self.ring, self.arrive, self.skip = at, chunk, ring, arrive, skip
+        self.send, self.recv, self.credit, self.out, self.out_sem = send, recv, credit, out, out_sem
+        self.feed = feed
         self.count = chunk.shape[0]
         self.kind = at.mid.astype(jnp.int32)
 
+    def slot(self, j):
+        return lax.rem(j, RING)
+
     def inward(self, j):
-        return remote(self.chunk.at[j], self.came.at[self.kind, j], self.send.at[0, j], self.recv.at[self.kind, j],
-                      "replica", self.at.inner)
+        return remote(self.chunk.at[j], self.ring.at[self.kind, self.slot(j)], self.send.at[0, j],
+                      self.recv.at[self.kind, j], "replica", self.at.inner)
 
     def outward(self, j, src):
-        return remote(src, self.came.at[1, j], self.send.at[1, j], self.recv.at[1, j], "replica", self.at.outer)
-
-    def here(self, kind, j):
-        return pltpu.make_async_copy(self.came.at[kind, j], self.came.at[kind, j], self.recv.at[kind, j])
+        return remote(src, self.out(j), self.send.at[1, j], self.recv.at[2, j], "replica", self.at.outer)
+
+    def keep(self, j):
+        return pltpu.make_async_copy(self.chunk.at[j], self.out(j), self.out_sem.at[j])
+
+    def take_in(self, kind, j, plane):
+        here = self.ring.at[kind, self.slot(j)]
+        pltpu.make_async_copy(here, here, self.recv.at[kind, j]).wait()
+        self.chunk[j] = (self.chunk[j].astype(F32) + self.ring[kind, self.slot(j)].astype(F32)).astype(BF)
+
+        @pl.when(j + RING < self.count)
+        def _():
+            pl.semaphore_signal(self.credit, inc=1, device_id={"replica": plane}, device_id_type=MESH)
 
     def up(self, j):
-        pltpu.make_async_copy(self.chunk.at[j], self.chunk.at[j], self.arrive.at[j]).wait()
+        if self.feed:
+            @pl.when(j + LEAD < self.count)
+            def _():
+                self.feed(j + LEAD)
+
+        @pl.when(j >= self.skip)
+        def _():
+            pltpu.make_async_copy(self.chunk.at[j], self.chunk.at[j], self.arrive.at[j]).wait()
 
         @pl.when(self.at.has_outer)
         def _():
-            self.here(0, j).wait()
-            self.chunk[j] = (self.chunk[j].astype(F32) + self.came[0, j].astype(F32)).astype(BF)
+            self.take_in(0, j, self.at.outer)
+
+        @pl.when(j >= RING)
+        def _():
+            pl.semaphore_wait(self.credit, 1)
 
         self.inward(j).start()
 
-    def down(self, j):
-        self.here(1, j).wait()
-
-        @pl.when(self.at.mid)
-        def _():
-            self.came[1, j] = (self.chunk[j].astype(F32) + self.came[1, j].astype(F32)).astype(BF)
+    def meet(self, j):
+        self.inward(j).wait_send()
+        self.take_in(1, j, self.at.inner)
 
         @pl.when(self.at.has_outer)
         def _():
-            self.outward(j, self.came.at[1, j]).start()
-
-        pltpu.make_async_copy(self.came.at[1, j], self.out(j), self.out_sem.at[j]).start()
+            self.outward(j, self.chunk.at[j]).start()
+
+        self.keep(j).start()
+
+    def take(self, j):
+        pltpu.make_async_copy(self.out(j), self.out(j), self.recv.at[2, j]).wait()
+
+        @pl.when(self.at.has_outer)
+        def _():
+            self.outward(j, self.out(j)).start()
 
     def settle(self):
         def step(j, carry):
-            self.inward(j).wait_send()
+            @pl.when(self.at.mid)
+            def _():
+                self.keep(j).wait()
+
+            @pl.when(jnp.logical_not(self.at.mid))
+            def _():
+                self.inward(j).wait_send()
 
             @pl.when(self.at.has_outer)
             def _():
-                self.outward(j, self.came.at[1, j]).wait_send()
-
-            pltpu.make_async_copy(self.came.at[1, j], self.out(j), self.out_sem.at[j]).wait()
+                self.outward(j, self.chunk.at[j]).wait_send()
+
             return carry
 
         lax.fori_loop(0, self.count, step, 0)
 
 
-def run_line(line, first, last):
-    lag = min(LAG, last - first)
-
-    def head(j, carry):
-        line.up(j)
-        return carry
-
-    def body(j, carry):
-        line.up(j)
-        line.down(j - lag)
-        return carry
-
-    def tail(j, carry):
-        line.down(j)
-        return carry
-
-    lax.fori_loop(first, first + lag, head, 0)
-    lax.fori_loop(first + lag, last, body, 0)
-    lax.fori_loop(last - lag, last, tail, 0)
+class Lines:
+    def __init__(self, *lines):
+        self.lines = lines
+        self.order = [(i, j) for i, line in enumerate(lines) for j in range(line.count)]
+        self.at = 0
+
+    def run(self, steps=None, body=None):
+        begin = self.at
+        last = len(self.order) + LAG_END
+        stop = last if steps is None else min(self.at + steps, len(self.order))
+        while self.at < stop:
+            first, size = self.at, 1
+            now = self.parts(first)
+            while first + size < stop and self.kinds(first + size) == self.kinds(first):
+                size += 1
+
+            def step(m, carry, now=now, first=first):
+                up, mid, rest = now
+                if up:
+                    self.lines[up[0]].up(up[1] + m)
+                if mid:
+                    @pl.when(self.lines[mid[0]].at.mid)
+                    def _():
+                        self.lines[mid[0]].meet(mid[1] + m)
+                if rest:
+                    @pl.when(jnp.logical_not(self.lines[rest[0]].at.mid))
+                    def _():
+                        self.lines[rest[0]].take(rest[1] + m)
+                if body:
+                    body(first - begin + m)
+                return carry
+
+            lax.fori_loop(0, size, step, 0)
+            self.at += size
+
+    def parts(self, t):
+        return [self.order[i] if 0 <= i < len(self.order) else None for i in (t, t - LAG_MID, t - LAG_END)]
+
+    def kinds(self, t):
+        return [part and part[0] for part in self.parts(t)]
+
+    def settle(self):
+        for line in self.lines:
+            line.settle()
 
 
 def rms_of(values):
@@ -358,6 +429,313 @@
 
 def norm_back(d_normed, normed, rms):
     return rms * (d_normed - normed * jnp.mean(d_normed * normed, axis=-1, keepdims=True))
+
+
+class Feed:
+    def __init__(self, at, grads, chunk, send, recv):
+        self.at, self.grads, self.chunk, self.send, self.recv = at, grads, chunk, send, recv
+        self.depth = chunk.shape[1]
+
+    def rows(self, grad, t):
+        return grad.at[pl.ds(pl.multiple_of(t * self.depth, self.depth), self.depth)]
+
+    def copy(self, grad, c, j):
+        to = self.at.near(j)
+        return remote(self.rows(grad, to), self.chunk.at[c], self.send.at[c], self.recv.at[c], "fsdp", to)
+
+    def start(self, c):
+        n = self.at.n
+        j = lax.rem(c, n)
+        for i, grad in enumerate(self.grads):
+            @pl.when((c // n == i) & (j == 0))
+            def _(grad=grad):
+                pltpu.make_async_copy(self.rows(grad, self.at.f), self.chunk.at[c], self.recv.at[c]).start()
+
+            @pl.when((c // n == i) & (j > 0))
+            def _(grad=grad):
+                self.copy(grad, c, j).start()
+
+    def settle(self):
+        def step(c, carry):
+            @pl.when(lax.rem(c, self.at.n) > 0)
+            def _():
+                self.copy(self.grads[0], c, lax.rem(c, self.at.n)).wait_send()
+
+            return carry
+
+        lax.fori_loop(0, len(self.grads) * self.at.n, step, 0)
+
+
+def start_all(copies):
+    for c in copies:
+        c.start()
+
+
+def rotate_with(values, cosine, sine):
+    return values * cosine + pltpu.roll(values, HEAD_WIDTH // 2, 1) * sine
+
+
+def rotation_table():
+    places = HEAD_WIDTH * -(-LMAX // HEAD_WIDTH)
+    inverse = ROPE_BASE ** (-(2.0 * np.arange(HEAD_WIDTH // 2)) / HEAD_WIDTH)
+    angles = np.arange(places)[:, None] * inverse[None, :]
+    cosine, sine = np.cos(angles), np.sin(angles)
+    rest = np.concatenate([cosine, cosine, -sine, sine], axis=1).astype(np.float32)
+    terms = []
+    for _ in range(3):
+        terms.append(rest.astype(jnp.bfloat16))
+        rest = rest - terms[-1].astype(np.float32)
+    return jnp.asarray(np.stack(terms))
+
+
+def rotation_of(places, table):
+    lane = lax.broadcasted_iota(jnp.int32, (places.shape[0], table.shape[1]), 1).astype(F32)
+    pick = (lane == places.astype(F32)[:, :1]).astype(F32).astype(BF)
+    both = dot(pick, table[0]) + dot(pick, table[1]) + dot(pick, table[2])
+    return both[:, :HEAD_WIDTH], both[:, HEAD_WIDTH:]
+
+
+def window_mask(places, rows, halo):
+    i_at = lax.broadcasted_iota(jnp.int32, (rows, halo + rows), 0) + halo
+    j_at = lax.broadcasted_iota(jnp.int32, (rows, halo + rows), 1)
+    back = (i_at - j_at).astype(F32)
+    return (back >= 0) & (back <= places.astype(F32)[:, :1])
+
+
+def softmax_of(queries, keys, mask):
+    scores = jnp.where(mask, dot_cols(queries, keys) * HEAD_WIDTH ** (-0.5), NEG_FILL)
+    terms = jnp.exp(scores - jnp.max(scores, axis=1, keepdims=True))
+    return terms / jnp.sum(terms, axis=1, keepdims=True)
+
+
+def back_kernel(n, n_z, part_ref, party_ref, x_ref, h_ref, g_ref, gain1_ref, gain2_ref, gainq_ref, gaink_ref,
+                down_ref, gate_ref, up_ref, wout_ref, wqkv_ref, q_ref, kv_ref, ctx_ref, proj_ref, table_ref, place_ref,
+                n1_ref,
+                dx_ref, y_ref, gains_ref, gmlp_ref, gqkv_ref, dhall_ref,
+                near, mine, far, stage, own, dh, own_gain, plane_gain, line_gain, all_gain,
+                chunk, ring, chunk2, ring2, dh_block, gout, d_kv, d_proj, halo_out, halo_in, n1_cols, qkv_send,
+                s_r, s_a, s_p, r_p, s_q, r_q, s_c, r_c, s_z, r_z, s_o, s_c2, r_c2, s_z2, r_z2, s_o2, credit, done, s_d, s_n, s_h):
+    at = Place(n, n_z)
+    share, share_out = chunk.shape[2], chunk2.shape[2]
+    rows, width = x_ref.shape
+    depth = chunk.shape[1]
+    outs = -(-width // share_out)
+    heads = QUERY_HEADS // n
+    qw = heads * HEAD_WIDTH
+    halo = LMAX
+    scale = HEAD_WIDTH ** (-0.5)
+    at.greet(True)
+
+    def mlp_place(j):
+        s = at.near_from(lax.rem(j, n))
+        return gmlp_ref.at[j // n, :, pl.ds(pl.multiple_of(s * share, HEAD_WIDTH), share)]
+
+    def attn_place(j):
+        return gqkv_ref.at[jnp.where(j < outs, j, outs + at.near_from(jnp.maximum(j - outs, 0)))]
+
+    feed = Feed(at, (down_ref, gate_ref, up_ref), chunk, s_c, r_c)
+    lines = Lines(
+        LineSum(at, chunk, ring, r_c, s_z, r_z, credit.at[0], mlp_place, s_o, 0, feed.start),
+        LineSum(at, chunk2, ring2, r_c2, s_z2, r_z2, credit.at[1], attn_place, s_o2, outs))
+    sum_n2 = ScatterSum(at, part_ref, near, mine, far, s_r.at[0])
+    for c in range(LEAD):
+        feed.start(jnp.int32(c))
+    sum_n2.start()
+    lines.run(1)
+    sum_n2.forward()
+    lines.run(n - 3)
+    sum_n2.wait()
+    own_gain[...] = jnp.zeros_like(own_gain)
+
+    def back_mlp(strip):
+        d_n2 = sum_n2.total(strip)
+        h = h_ref[strip]
+        r2 = rms_of(h)
+        u2 = h * r2
+        own_gain[1:2] += jnp.sum(d_n2 * u2, axis=0, keepdims=True)
+        d_h = g_ref[strip].astype(F32) + norm_back(d_n2 * gain2_ref[...], u2, r2)
+        dh[strip] = d_h
+        own[strip] = d_h.astype(BF)
+
+    strips(rows, back_mlp)
+    gather = Gather(at, own, dhall_ref, s_a)
+    gather.start()
+    lines.run(n // 2 + 1)
+    gather.forward()
+    lines.run(1)
+    gather.wait()
+    sum_y = ScatterSum(at, party_ref, near, mine, far, s_r.at[2])
+    sum_y.start()
+    lines.run(1)
+    sum_y.forward()
+    gout[...] = jnp.zeros_like(gout)
+
+    def rows_of(g):
+        return pl.ds(pl.multiple_of(g * rows, rows), rows)
+
+    def block_of(g):
+        return pltpu.make_async_copy(dhall_ref.at[rows_of(g)], dh_block, s_d.at[0])
+
+    def attention(g):
+        at_rows = rows_of(g)
+        block_of(g).start()
+        mask = window_mask(place_ref[at_rows], rows, halo)
+        keys, values = kv_ref[g, :, :HEAD_WIDTH], kv_ref[g, :, HEAD_WIDTH:]
+        cosine, sine = rotation_of(place_ref[at_rows], table_ref)
+        block_of(g).wait()
+        d_ctx = dot_cols(dh_block[...], wout_ref[...]).astype(BF)
+        gout[:, :width] += dot_rows(ctx_ref[at_rows], dh_block[...])
+        d_k = jnp.zeros((halo + rows, HEAD_WIDTH), F32)
+        d_v = jnp.zeros((halo + rows, HEAD_WIDTH), F32)
+        for head in range(heads):
+            lanes = slice(head * HEAD_WIDTH, (head + 1) * HEAD_WIDTH)
+            queries, d_c = q_ref[at_rows, lanes], d_ctx[:, lanes]
+            probs = softmax_of(queries, keys, mask)
+            d_v += dot_rows(probs.astype(BF), d_c)
+            d_p = dot_cols(d_c, values)
+            d_s = (probs * (d_p - jnp.sum(probs * d_p, axis=1, keepdims=True))).astype(BF)
+            d_k += dot_rows(d_s, queries) * scale
+            dq_g = rotate_with(dot(d_s, keys) * scale, cosine, -sine)
+            raw = proj_ref[at_rows, lanes]
+            rms = rms_of(raw)
+            hat = raw * rms
+            own_gain[2:3, :HEAD_WIDTH] += jnp.sum(dq_g * hat, axis=0, keepdims=True)
+            d_proj[at_rows, lanes] = norm_back(dq_g * gainq_ref[...], hat, rms).astype(BF)
+        halo_out[g, :, :HEAD_WIDTH] = d_k[:halo].astype(BF)
+        halo_out[g, :, HEAD_WIDTH:] = d_v[:halo].astype(BF)
+        d_kv[g, :, :HEAD_WIDTH] = d_k[halo:]
+        d_kv[g, :, HEAD_WIDTH:] = d_v[halo:]
+
+    lines.run(n, attention)
+
+    not_first, not_last = at.z > 0, at.z < n_z - 1
+
+    def halo_copy():
+        return remote(halo_out, halo_in, s_h.at[0], s_h.at[1], "replica", jnp.maximum(at.z - 1, 0))
+
+    @pl.when(not_first)
+    def _():
+        halo_copy().start()
+
+    for i in range(outs):
+        chunk2[i] = gout[:, i * share_out:(i + 1) * share_out].astype(BF)
+    lines.run(1)
+    sum_y.wait()
+
+    def finish(strip):
+        y_ref[strip] = (h_ref[strip] + sum_y.total(strip)).astype(BF)
+
+    strips(rows, finish)
+    for k in range(1, n):
+        pl.semaphore_signal(done, inc=1, device_id={"fsdp": at.to(k)}, device_id_type=MESH)
+
+    @pl.when(not_last)
+    def _():
+        pltpu.make_async_copy(halo_in, halo_in, s_h.at[1]).wait()
+
+    @pl.when(jnp.logical_not(not_last))
+    def _():
+        halo_in[...] = jnp.zeros_like(halo_in)
+
+    def keys_back(g):
+        at_rows = rows_of(g)
+        d_kv[g, rows - halo:] += halo_in[g].astype(F32)
+        cosine, sine = rotation_of(place_ref[at_rows], table_ref)
+        dk_g = rotate_with(d_kv[g, :, :HEAD_WIDTH], cosine, -sine)
+        raw = proj_ref[at_rows, qw:qw + HEAD_WIDTH]
+        rms = rms_of(raw)
+        hat = raw * rms
+        own_gain[2:3, HEAD_WIDTH:2 * HEAD_WIDTH] += jnp.sum(dk_g * hat, axis=0, keepdims=True)
+        d_proj[at_rows, qw:qw + HEAD_WIDTH] = norm_back(dk_g * gaink_ref[...], hat, rms).astype(BF)
+        d_proj[at_rows, qw + HEAD_WIDTH:] = d_kv[g, :, HEAD_WIDTH:].astype(BF)
+
+    per_step = n // 2
+
+    def keys_back_some(i):
+        for m in range(per_step):
+            keys_back(i * per_step + m)
+
+    lines.run(2, keys_back_some)
+
+    def cols_of(j):
+        return pltpu.make_async_copy(
+            n1_ref.at[:, pl.ds(pl.multiple_of(at.near(j) * depth, depth), depth)], n1_cols.at[lax.rem(j, 2)],
+            s_n.at[lax.rem(j, 2)])
+
+    own_qkv = pltpu.make_async_copy(qkv_send.at[0], chunk2.at[outs], r_c2.at[outs])
+
+    def qkv_copy(j):
+        return remote(qkv_send.at[j], chunk2.at[outs + j], s_c2.at[j], r_c2.at[outs + j], "fsdp", at.near(j))
+
+    cols_of(0).start()
+
+    def qkv_grad(j):
+        @pl.when(j + 1 < n)
+        def _():
+            cols_of(j + 1).start()
+
+        cols_of(j).wait()
+        qkv_send[j] = dot_rows(n1_cols[lax.rem(j, 2)], d_proj[...]).astype(BF)
+
+        @pl.when(j == 0)
+        def _():
+            own_qkv.start()
+
+        @pl.when(j > 0)
+        def _():
+            qkv_copy(j).start()
+
+    per_out = n // 4
+
+    def qkv_grads(i):
+        for m in range(per_out):
+            qkv_grad(i * per_out + m)
+
+    lines.run(4, qkv_grads)
+    sum_n1 = ScatterSum(at, stage, near, mine, far, s_r.at[1], made=True)
+
+    def n1_part(k):
+        q = at.chip_at(k)
+        stage[k] = dot_cols(d_proj[rows_of(2 * q + 1 - at.core)], wqkv_ref[...]).astype(BF)
+        mine[k] = dot_cols(d_proj[rows_of(2 * q + at.core)], wqkv_ref[...]).astype(BF)
+
+    lines.run(at.chips, n1_part)
+    pl.semaphore_wait(done, n - 1)
+    sum_n1.start()
+    lines.run(1)
+    sum_n1.forward()
+    lines.run()
+    sum_n1.wait()
+
+    def back_attn(strip):
+        d_n1 = sum_n1.total(strip)
+        x = x_ref[strip].astype(F32)
+        r1 = rms_of(x)
+        u1 = x * r1
+        own_gain[0:1] += jnp.sum(d_n1 * u1, axis=0, keepdims=True)
+        dx_ref[strip] = (dh[strip] + norm_back(d_n1 * gain1_ref[...], u1, r1)).astype(BF)
+
+    strips(rows, back_attn)
+    gains = Exchange(at, [(lambda t: own_gain, lambda s: plane_gain.at[s])], s_p, r_p)
+    gains.start()
+    gains.wait()
+    line_gain[...] = jnp.sum(plane_gain[...], axis=0)
+    others = [
+        remote(line_gain, all_gain.at[at.z], s_q.at[k], r_q.at[k], "replica", at.plane(k)) for k in range(1, n_z)]
+    start_all(others)
+    all_gain[at.z] = line_gain[...]
+    for c in others:
+        c.wait()
+    gains_ref[...] = jnp.sum(all_gain[...], axis=0)
+    feed.settle()
+    for j in range(1, n):
+        qkv_copy(j).wait_send()
+
+    @pl.when(not_first)
+    def _():
+        halo_copy().wait_send()
+
+    lines.settle()
 
 
 def begin(n, n_z, x, gain, place, w_qkv):
@@ -402,6 +780,45 @@
     )(part, x, gain, g, gate, up, down)
 
 
+def back(n, n_z, part, part_y, x, h, g, gain1, gain2, gain_q, gain_k, down, gate, up, w_out, w_qkv, q, kv, ctx, proj,
+         table, places, n1):
+    rows, width = x.shape
+    chips, share, wide, depth = n // 2, down.shape[1], w_qkv.shape[1], width // n
+    outs = -(-width // wide)
+    block = functools.partial(pltpu.VMEM, dtype=BF)
+    gains = (8, width)
+    count2 = outs + n
+    return pl.pallas_call(
+        functools.partial(back_kernel, n, n_z),
+        out_shape=(
+            jax.ShapeDtypeStruct((rows, width), BF),
+            jax.ShapeDtypeStruct((rows, width), BF),
+            jax.ShapeDtypeStruct(gains, F32),
+            jax.ShapeDtypeStruct((3, depth, n * share), BF),
+            jax.ShapeDtypeStruct((count2, depth, wide), BF),
+            jax.ShapeDtypeStruct((n * rows, width), BF),
+        ),
+        in_specs=[ANY, ANY] + [VMEM] * 7 + [ANY] * 3 + [VMEM] * 8 + [ANY],
+        out_specs=(VMEM, VMEM, VMEM, ANY, ANY, ANY),
+        scratch_shapes=[
+            block((chips, rows, width)), block((chips, rows, width)), block((chips - 1, rows, width)),
+            block((chips, rows, width)), block((rows, width)), pltpu.VMEM((rows, width), F32),
+            pltpu.VMEM(gains, F32), pltpu.VMEM((n,) + gains, F32), pltpu.VMEM(gains, F32), pltpu.VMEM((n_z,) + gains, F32),
+            block((3 * n, depth, share)), block((2, RING, depth, share)),
+            block((count2, depth, wide)), block((2, RING, depth, wide)),
+            block((rows, width)), pltpu.VMEM((depth, outs * wide), F32),
+            pltpu.VMEM((n, rows, 2 * HEAD_WIDTH), F32), block((n * rows, wide)),
+            block((n, LMAX, 2 * HEAD_WIDTH)), block((n, LMAX, 2 * HEAD_WIDTH)),
+            block((2, n * rows, depth)), block((n, depth, wide)),
+            DMA((3, 5, n)), DMA((6, n)), DMA((1, n)), DMA((1, n)), DMA((n_z,)), DMA((n_z,)),
+            DMA((3 * n,)), DMA((3 * n,)), DMA((2, 3 * n)), DMA((3, 3 * n)), DMA((3 * n,)),
+            DMA((n,)), DMA((count2,)), DMA((2, count2)), DMA((3, count2)), DMA((count2,)),
+            pltpu.SemaphoreType.REGULAR((2,)), pltpu.SemaphoreType.REGULAR, DMA((1,)), DMA((2,)), DMA((2,))],
+        compiler_params=pltpu.CompilerParams(collective_id=2, has_side_effects=True, vmem_limit_bytes=63 << 20),
+        name="back",
+    )(part, part_y, x, h, g, gain1, gain2, gain_q, gain_k, down, gate, up, w_out, w_qkv, q, kv, ctx, proj, table, places, n1)
+
+
 def row_positions(flat_lens, ranks, first_row, count):
     earlier = (ranks[:, None] < ranks[None, :]).astype(jnp.int32)
     starts = jnp.sum(flat_lens[:, None] * earlier, axis=0)
@@ -429,16 +846,6 @@
     n1, w_qkv_c, places = begin(n_fsdp, n_replica, tokens, gain_attn[None], place, w_qkv)
     pos_all = places.reshape(n_fsdp, -1)[:, :rows].reshape(-1)
 
-    def gather(a):
-        return lax.all_gather(a, "fsdp", axis=0, tiled=True)
-
-    def scatter_sum(a):
-        return lax.psum_scatter(a.astype(BF), "fsdp", scatter_dimension=0, tiled=True).astype(F32)
-
-    x = tokens.astype(F32)
-    g = cotangent.astype(F32)
-    r1 = lax.rsqrt(jnp.mean(x * x, axis=1, keepdims=True) + EPSILON)
-    u1 = x * r1
     total = n1.shape[0]
 
     proj = dot(n1, w_qkv_c)
@@ -480,66 +887,27 @@
     h, n2, g_all, gate_c, up_c, down_c = middle(
         n_fsdp, n_replica, dot(ctx_low, w_out).astype(BF), tokens, gain_mlp[None], cotangent, w_gate, w_up, w_down_t)
 
-    r2 = lax.rsqrt(jnp.mean(h * h, axis=1, keepdims=True) + EPSILON)
-    u2 = h * r2
     gate = dot(n2, gate_c)
     up = dot(n2, up_c)
     sg = jax.nn.sigmoid(gate)
     silu = gate * sg
     act = (silu * up).astype(BF)
-    output = (h + scatter_sum(dot_cols(act, down_c))).astype(BF)
+    part_y = dot_cols(act, down_c).astype(BF)
 
     d_act = dot(g_all, down_c)
     d_gate = (d_act * up * sg * (1.0 + gate * (1.0 - sg))).astype(BF)
     d_up = (d_act * silu).astype(BF)
 
-    d_n2 = scatter_sum(dot_cols(d_gate, gate_c) + dot_cols(d_up, up_c))
-    d_gain_mlp = jnp.sum(d_n2 * u2, axis=0)
-    d_h = g + norm_back(d_n2 * gain_mlp, u2, r2)
-    dh_all = gather(d_h.astype(BF))
-    d_ctx = dot_cols(dh_all, w_out).astype(BF).reshape(groups, rows, heads, HEAD_WIDTH)
-    d_v = jnp.einsum("ghqk,gqhd->gkd", probs_low, d_ctx, preferred_element_type=F32)
-    d_p = jnp.einsum("gqhd,gkd->ghqk", d_ctx, v_win, preferred_element_type=F32)
-    delta = jnp.sum(probs * d_p, axis=3, keepdims=True)
-    d_s = (probs * (d_p - delta)).astype(BF)
-    d_q = jnp.einsum("ghqk,gkd->gqhd", d_s, k_win, preferred_element_type=F32) * scale
-    d_k = jnp.einsum("ghqk,gqhd->gkd", d_s, q_grp, preferred_element_type=F32) * scale
-    d_kv = jnp.concatenate([d_k, d_v], axis=2)
-    d_kv_after = lax.ppermute(d_kv[:, :halo].astype(BF), "replica", down_pairs).astype(F32)
-    d_kv = d_kv[:, halo:]
-    d_kv = jnp.concatenate([d_kv[:, :rows - halo], d_kv[:, rows - halo:] + d_kv_after], axis=1)
-    d_k = d_kv[..., :HEAD_WIDTH].reshape(total, HEAD_WIDTH)
-    d_v = d_kv[..., HEAD_WIDTH:].reshape(total, HEAD_WIDTH)
-    d_q = d_q.reshape(total, heads, HEAD_WIDTH)
-    dq_g = rotate(d_q, cosine[:, None], -sine[:, None])
-    dk_g = rotate(d_k, cosine, -sine)
-    d_gain_query = jnp.sum(dq_g * q_hat, axis=(0, 1))
-    d_gain_key = jnp.sum(dk_g * k_hat, axis=0)
-    dq = norm_back(dq_g * gain_query, q_hat, rq)
-    dk = norm_back(dk_g * gain_key, k_hat, rk)
-    d_proj = jnp.concatenate([dq.reshape(total, qw), dk, d_v], axis=1).astype(BF)
-    d_n1 = scatter_sum(dot_cols(d_proj, w_qkv_c))
-    d_gain_attn = jnp.sum(d_n1 * u1, axis=0)
-    input_grad = (d_h + norm_back(d_n1 * gain_attn, u1, r1)).astype(BF)
-
-    def reduce_cols(grad):
-        share = grad.shape[1]
-        low = grad.astype(BF).reshape(n_fsdp, n_replica, width // n_fsdp // n_replica, share)
-        low = low.transpose(1, 0, 2, 3).reshape(width, share)
-        part = lax.psum_scatter(low, "replica", scatter_dimension=0, tiled=True)
-        part = lax.all_to_all(part.reshape(n_fsdp, -1, share), "fsdp", split_axis=0, concat_axis=1)
-        whole = lax.all_gather(part, "replica", axis=0, tiled=True)
-        return whole.astype(F32)
-
-    def reduce_rows(grad):
-        low = lax.psum_scatter(grad.astype(BF), "replica", scatter_dimension=0, tiled=True)
-        return lax.all_gather(low, "replica", axis=0, tiled=True).astype(F32)
-
-    g_down = reduce_cols(dot_rows(g_all, act)).reshape(depth, -1)
-    g_gate = reduce_cols(dot_rows(n2, d_gate)).reshape(depth, -1)
-    g_up = reduce_cols(dot_rows(n2, d_up)).reshape(depth, -1)
-    g_out = reduce_rows(dot_rows(ctx_low, dh_all))
-    g_qkv = reduce_cols(dot_rows(n1, d_proj))
+    places = jnp.broadcast_to(pos_all.astype(BF)[:, None], (total, HEAD_WIDTH))
+    input_grad, output, gains, g_mlp, g_attn, _ = back(
+        n_fsdp, n_replica, (dot_cols(d_gate, gate_c) + dot_cols(d_up, up_c)).astype(BF), part_y, tokens, h, cotangent,
+        gain_attn[None], gain_mlp[None], gain_query[None], gain_key[None],
+        dot_rows(g_all, act).astype(BF), dot_rows(n2, d_gate).astype(BF), dot_rows(n2, d_up).astype(BF),
+        w_out, w_qkv_c, q_low.reshape(total, qw), kv_window, ctx_low, proj[:, :qw + HEAD_WIDTH],
+        rotation_table(), places, n1)
+    outs = g_attn.shape[0] - n_fsdp
+    g_out = g_attn[:outs].transpose(1, 0, 2).reshape(depth, -1)[:, :width]
+    g_qkv = g_attn[outs:].transpose(1, 0, 2).astype(F32)
 
     def of_key_heads(part):
         return jnp.sum(part.reshape(depth, KEY_VALUE_HEADS, shared, HEAD_WIDTH), axis=2).reshape(depth, k_w)
@@ -548,8 +916,9 @@
         g_qkv[:, :, :qw].reshape(depth, q_w),
         of_key_heads(g_qkv[:, :, qw:qw + HEAD_WIDTH]),
         of_key_heads(g_qkv[:, :, qw + HEAD_WIDTH:])], axis=1)
-    sums = lax.psum((d_gain_attn, d_gain_mlp, d_gain_query, d_gain_key), ("fsdp", "replica"))
-    return (output, input_grad, g_qkv, g_out, g_gate, g_up, g_down) + tuple(sums)
+    return (
+        output, input_grad, g_qkv, g_out.astype(F32), g_mlp[1].astype(F32), g_mlp[2].astype(F32), g_mlp[0].astype(F32),
+        gains[0], gains[1], gains[2, :HEAD_WIDTH], gains[2, HEAD_WIDTH:2 * HEAD_WIDTH])
 
 
 def solution(mesh):

time: 1050 us -> 811 us (0.77)
  waiting for transfers between devices: 370 us -> 0.01 us
  Pallas kernels: 276 us -> 641 us
  blocking collectives: 101 us -> 0 us
  local copies, waits for them, and re-layouts: 88.7 us -> 45.7 us
  matrix products: 123 us -> 84.4 us
  other arithmetic: 60.4 us -> 28 us
  between operations: 16.4 us -> 1.53 us
    pallas_call x0 -> x1, Pallas kernels: none -> 365 us  [back(): pl.pallas_call(functools.partial(back_kernel, n, n_z), out_shape=(jax.Sha...]
    all_gather x6 -> x0, waiting for transfers between devices: 194 us -> none  [the longest x4 169 us: reduce_cols(): whole = lax.all_gather(part, 'replica', axis=0, tiled=True)]
    reduce_scatter x8 -> x0, waiting for transfers between devices: 176 us -> none  [the longest x4 102 us: reduce_cols(): part = lax.psum_scatter(low, 'replica', scatter_dimension=0, tiled=True)]
    all_to_all x4 -> x0, blocking collectives: 61.8 us -> none  [reduce_cols(): lax.all_to_all(part.reshape(n_fsdp, -1, share), 'fsdp', split_axis=0, con...]
    psum x1 -> x0, blocking collectives: 39.5 us -> none  [per_device(): lax.psum((d_gain_attn, d_gain_mlp, d_gain_query, d_gain_key), ('fsdp', 'r...]
    unnamed x121 -> x77, local copies, waits for them, and re-layouts: 39.5 us -> 19.7 us
    all_gather x4 -> x0, local copies, waits for them, and re-layouts: 19 us -> none  [reduce_cols(): whole = lax.all_gather(part, 'replica', axis=0, tiled=True)]
    reshape x3 -> x0, other arithmetic: 16 us -> none  [the longest x1 5.64 us: per_device(): g_up = reduce_cols(dot_rows(n2, d_up)).reshape(depth, -1)]
  transfers between devices with their start and end apart: 16 -> 1, of which waited for: 11 -> 0; matrix products, arithmetic and copies ran while one was open for 18% -> 1% of each run, Pallas kernels for 0% -> 0%
where the time goes in v4:
time: 811 us; the launch traced here: 804 us
  Pallas kernels  641 us (79%)
  matrix products  84.4 us (10%)
  local copies, waits for them, and re-layouts  45.7 us (6%)
  other arithmetic  28 us (3%)
    pallas_call x1, Pallas kernels, back(): pl.pallas_call(functools.partial(back_kernel, n, n_z), out_shape=(jax.Sha...  365 us
    pallas_call x1, Pallas kernels, middle(): pl.pallas_call(functools.partial(middle_kernel, n, n_z), out_shape=(jax.S...  210 us
    pallas_call x1, Pallas kernels, begin(): pl.pallas_call(functools.partial(begin_kernel, n, n_z), out_shape=(jax.Sh...  66.1 us
    dot_general x5, matrix products, dot(): return jnp.dot(left, right, preferred_element_type=F32)  35.6 us
    dot_general x3, matrix products, dot_cols(): lax.dot_general(left, right, (((1,), (1,)), ((), ())), preferred_element_...  25.1 us
    dot_general x3, matrix products, dot_rows(): lax.dot_general(left, right, (((0,), (0,)), ((), ())), preferred_element_...  21.8 us
    unnamed x77, local copies, waits for them, and re-layouts  19.7 us
  transfers between devices with their start and end apart: 1, of which 0 were waited for; matrix products, arithmetic and copies ran while one was open for 1% of the time, Pallas kernels for 0%

profile of v4, /device:TPU:0, one launch (start us, length us, event | category | flops | bytes accessed | tf_op | source)
XLA Modules:
  0.0 804.1 jit_solution(2642037621136828018)
XLA Ops:
  2.9 1.1 copy-done
  4.0 1.6 copy-done.4
  6.3 66.1 %begin.1 = (bf16[1536,2048]{1,0:T(8,128)(2,1)S(1)}, bf16[2048,512]{1,0:T(8,128)(2,1)S(1)}, s32[8,8,128]{2,1,0:T(8,128)S(1)}) custom-call(bf16[192,2048]{1,0:T(8,128)(2,1)S(1)} %copy-done, f32[1,2048]{1,0:T(1,128)S(1)} %bitcast.95, s32[8,128]{1,0:T(8,128)S(1)} %pad_bitcast_fusion.place_ref, bf16[256,4096]{1,0:T(8,128)(2,1)S(1)} %copy-done.4), custom_call_target="tpu_custom_call" | custom-call | tf_op jit(solution)/shard_map/begin/pallas_call | solution.py:744
  72.4 3.7 fusion.28
  78.7 3.1 subtract_convert_fusion.1
  81.7 0.9 pad_maximum_fusion.2
  82.7 2.3 copy.45
  84.9 1.8 slice.113
  86.7 3.6 collective-permute-start
  91.9 1.2 concatenate.28
  93.1 0.9 pad_maximum_fusion.3
  94.0 1.2 concatenate.29
  95.3 2.4 copy.62.proj_ref
  97.8 1.6 copy.46
  99.4 1.2 copy.61.q_ref
  100.5 1.5 copy.47
  102.6 0.9 fusion.10
  103.5 2.4 fusion.27
  105.9 1.0 fusion.9
  107.8 1.0 copy.68
  108.8 4.5 convolution_convert_fusion.1.part_ref
  113.3 209.6 %middle.1 = (f32[192,2048]{1,0:T(8,128)S(1)}, bf16[1536,2048]{1,0:T(8,128)(2,1)}, bf16[1536,2048]{1,0:T(8,128)(2,1)}, bf16[2048,768]{1,0:T(8,128)(2,1)}, bf16[20...) custom-call(bf16[1536,2048]{1,0:T(8,128)(2,1)} %convolution_convert_fusion.1.part_ref, bf16[192,2048]{1,0:T(8,128)(2,1)S(1)} %copy-done.1, ...), custom_call_target="tpu_custom_call" | custom-call | tf_op jit(solution)/shard_map/middle/pallas_call | solution.py:764
  323.0 10.1 %fusion.29 = f32[1536,768]{1,0:T(8,128)} fusion(bf16[1536,2048]{1,0:T(8,128)(2,1)} %get-tuple-element.40, bf16[2048,768]{1,0:T(8,128)(2,1)} %get-tuple-element.41), kind=kOutput, calls=%fused_computation.81 | convolution fusion | flops 4831838208 | bytes 14155776 | tf_op jit(solution)/shard_map/dot_general | solution.py:405
  333.0 6.7 fusion.30
  339.7 10.7 %multiply_convert_fusion = (bf16[1536,768]{1,0:T(8,128)(2,1)}, bf16[1536,768]{1,0:T(8,128)(2,1)S(1)}, bf16[1536,768]{1,0:T(8,128)(2,1)}) fusion(f32[1536,768]{1,0:T(8,128)} %fusion.30, f32[1536,768]{1,0:T(8,128)} %fusion.29, bf16[1536,2048]{1,0:T(8,128)(2,1)S(1)} %copy-done.27, bf16[2048,768]{1,0:T(8,128)(2,1)S(1)} %copy-done.28), kind=kOutput, calls=%fused_computation.5 | convolution fusion | flops 4849532928 | bytes 25952256 | tf_op jit(solution)/shard_map/dot_general | solution.py:405
  350.5 8.4 %convolution_convert_fusion.4.down_ref = bf16[2048,768]{1,0:T(8,128)(2,1)} fusion(bf16[1536,2048]{1,0:T(8,128)(2,1)S(1)} %bitcast.117, bf16[1536,768]{1,0:T(8,128)(2,1)} %get-tuple-element.76), kind=kOutput, calls=%fused_computation.17 | convolution fusion | flops 4833411072 | bytes 11796480 | tf_op jit(solution)/shard_map/dot_general | solution.py:409
  358.9 7.0 convolution_convert_fusion.party_ref
  365.9 6.7 convolution_convert_fusion.3.gate_ref
  372.6 8.2 %fusion.31 = f32[1536,2048]{1,0:T(8,128)} fusion(bf16[1536,768]{1,0:T(8,128)(2,1)S(1)} %get-tuple-element.77, bf16[2048,768]{1,0:T(8,128)(2,1)S(1)} %copy-done.29), kind=kOutput, calls=%fused_computation.83 | convolution fusion | flops 4831838208 | bytes 18087936 | tf_op jit(solution)/shard_map/dot_general | solution.py:413
  380.8 6.7 convolution_convert_fusion.2.up_ref
  387.5 9.8 %add_convert_fusion.part_ref = bf16[1536,2048]{1,0:T(8,128)(2,1)} fusion(f32[1536,2048]{1,0:T(8,128)} %fusion.31, bf16[1536,768]{1,0:T(8,128)(2,1)S(1)} %copy-done.31, bf16[2048,768]{1,0:T(8,128)(2,1)S(1)} %copy-done.28), kind=kOutput, calls=%fused_computation.1 | convolution fusion | flops 4838129664 | bytes 24379392 | tf_op jit(solution)/shard_map/dot_general | solution.py:413
  397.4 1.1 pad_maximum_fusion.1.kv_ref
  398.5 1.0 broadcast_in_dim.39.place_ref
  399.6 365.1 %back.1 = (bf16[192,2048]{1,0:T(8,128)(2,1)}, bf16[192,2048]{1,0:T(8,128)(2,1)}, f32[8,2048]{1,0:T(8,128)}, bf16[3,256,6144]{2,1,0:T(8,128)(2,1)}, bf16[12,256,5...) custom-call(bf16[1536,2048]{1,0:T(8,128)(2,1)} %add_convert_fusion.part_ref, ...), custom_call_target="tpu_custom_call" | custom-call | tf_op jit(solution)/shard_map/back/pallas_call | solution.py:791
  764.7 1.4 slice_bitcast_fusion
  766.0 1.5 fusion.26
  767.6 1.5 convert_bitcast_fusion.1
  769.7 1.3 fusion.25
  771.0 1.0 copy-done.10
  772.0 1.8 copy.55
  773.8 3.0 copy.57
  776.8 2.5 copy.53
  779.3 1.8 copy.52
  781.2 1.3 copy.54
  783.1 3.8 pad_maximum_fusion
  786.9 5.6 copy.56
  792.5 9.4 %bitcast_convert_fusion = (f32[256,6144]{1,0:T(8,128)}, f32[256,6144]{1,0:T(8,128)}, f32[256,6144]{1,0:T(8,128)}) fusion(bf16[3,256,6144]{2,1,0:T(8,128)(2,1)} %get-tuple-element.49), kind=kLoop, calls=%fused_computation.18 | loop fusion | flops 4718592 | bytes 28311552 | tf_op jit(solution)/shard_map/convert_element_type | solution.py:920
  801.9 0.9 copy.72
  (98 shorter events, 10.5 us)
Async XLA Ops:
  1.2 75.1 %copy-start.24 = (s32[192]{0:T(256)}, s32[192]{0:T(256)S(1)}, u32[]{:S(2)}) copy-start(s32[192]{0:T(256)S(1)} %iota_add_fusion) | copy-start | bytes 2308
  2.9 1.1 copy-start
  4.0 1.6 copy-start.4
  5.6 0.7 copy-start.7
  72.4 3.7 copy-start.2
  72.4 3.7 copy-start.5
  76.1 14.4 %copy-start.9 = (f32[1536,512]{0,1:T(8,128)}, f32[1536,512]{0,1:T(8,128)S(1)}, u32[]{:S(2)}) copy-start(f32[1536,512]{0,1:T(8,128)S(1)} %fusion.28) | copy-start | bytes 9437188
  86.7 3.9 copy-start.26
  86.7 15.9 %collective-permute-start = (bf16[8,96,256]{2,1,0:T(8,128)(2,1)}, bf16[8,96,256]{2,1,0:T(8,128)(2,1)S(1)}, u32[]{:S(2)}, u32[]{:S(2)}) collective-permute-start(bf16[8,96,256]{2,1,0:T(8,128)(2,1)} %slice.113), channel_id=1, source_target_pairs={{0,1},{1,2},{2,3},{4,5},{5,6},{6,7},{8,9},{9,10},{10,11},{12,13},{... | collective-permute-start | bytes 1179656 | tf_op jit(solution)/shard_map/ppermute | solution.py:868
  90.5 1.0 copy-start.18
  90.5 1.1 copy-start.19
  91.6 3.6 copy-start.23
  91.6 3.7 slice-start
  95.2 4.2 copy-start.15
  97.8 4.3 copy-start.25
  97.8 4.4 copy-start.22
  97.8 4.8 copy-start.11
  102.6 3.3 copy-start.16
  107.0 1.8 copy-start.13
  108.8 4.5 copy-start.1
  108.8 4.5 copy-start.3
  108.8 4.5 copy-start.8
  322.9 10.1 %copy-start.6 = (f32[192,2048]{1,0:T(8,128)}, f32[192,2048]{1,0:T(8,128)S(1)}, u32[]{:S(2)}) copy-start(f32[192,2048]{1,0:T(8,128)S(1)} %get-tuple-element.45.h_ref) | copy-start | bytes 4718596
  322.9 10.1 %copy-start.27 = (bf16[1536,2048]{1,0:T(8,128)(2,1)S(1)}, bf16[1536,2048]{1,0:T(8,128)(2,1)}, u32[]{:S(2)}) copy-start(bf16[1536,2048]{1,0:T(8,128)(2,1)} %get-tuple-element.42) | copy-start | bytes 18874372
  322.9 10.1 %copy-start.29 = (bf16[2048,768]{1,0:T(8,128)(2,1)S(1)}, bf16[2048,768]{1,0:T(8,128)(2,1)}, u32[]{:S(2)}) copy-start(bf16[2048,768]{1,0:T(8,128)(2,1)} %get-tuple-element.44) | copy-start | bytes 9437188
  333.0 6.7 copy-start.28
  333.0 17.4 %slice-start.2 = ((s8[6291456]{0:T(1024)(128)(4,1)}), s8[4194304]{0:T(1024)(128)(4,1)S(1)}, s32[]{:S(2)}) async-start(s8[6291456]{0:T(1024)(128)(4,1)} %bitcast.116), calls=%async_computation.2 | async-start | bytes 8388608
  339.7 10.7 %slice-start.3 = ((s8[6291456]{0:T(1024)(128)(4,1)}), s8[2097152]{0:T(1024)(128)(4,1)S(1)}, s32[]{:S(2)}) async-start(s8[6291456]{0:T(1024)(128)(4,1)} %bitcast.116), calls=%async_computation.3 | async-start | bytes 4194304
  350.5 8.4 %copy-start.30 = (bf16[2048,768]{1,0:T(8,128)(2,1)S(1)}, bf16[2048,768]{1,0:T(8,128)(2,1)}, u32[]{:S(2)}) copy-start(bf16[2048,768]{1,0:T(8,128)(2,1)} %get-tuple-element.41) | copy-start | bytes 9437188
  350.5 8.4 %copy-start.32 = (bf16[1536,768]{1,0:T(8,128)(2,1)S(1)}, bf16[1536,768]{1,0:T(8,128)(2,1)}, u32[]{:S(2)}) copy-start(bf16[1536,768]{1,0:T(8,128)(2,1)} %get-tuple-element.76) | copy-start | bytes 7077892
  372.6 8.2 %copy-start.31 = (bf16[1536,768]{1,0:T(8,128)(2,1)S(1)}, bf16[1536,768]{1,0:T(8,128)(2,1)}, u32[]{:S(2)}) copy-start(bf16[1536,768]{1,0:T(8,128)(2,1)} %get-tuple-element.78) | copy-start | bytes 7077892
  387.5 9.8 %copy-start.17 = (bf16[8,96,256]{2,1,0:T(8,128)(2,1)S(1)}, bf16[8,96,256]{2,1,0:T(8,128)(2,1)}, u32[]{:S(2)}) copy-start(bf16[8,96,256]{2,1,0:T(8,128)(2,1)} %copy-done.16) | copy-start | bytes 1179652
  764.7 4.4 copy-start.14
  769.6 2.3 copy-start.10
  773.8 5.6 slice-start.1
  781.2 2.0 copy-start.12
  792.5 9.4 %copy-start.21 = (bf16[192,2048]{1,0:T(8,128)(2,1)S(1)}, bf16[192,2048]{1,0:T(8,128)(2,1)}, u32[]{:S(2)}) copy-start(bf16[192,2048]{1,0:T(8,128)(2,1)} %get-tuple-element.107) | copy-start | bytes 2359300
  792.5 10.3 %copy-start.20 = (bf16[192,2048]{1,0:T(8,128)(2,1)S(1)}, bf16[192,2048]{1,0:T(8,128)(2,1)}, u32[]{:S(2)}) copy-start(bf16[192,2048]{1,0:T(8,128)(2,1)} %get-tuple-element.108) | copy-start | bytes 2359300

commit v5 on v4

--- a/solution.py
+++ b/solution.py
@@ -29,6 +29,22 @@
 LAG_END = 6
 RING = 4
 LEAD = 5
+
+
+def dot(left, right):
+    return jnp.dot(left, right, preferred_element_type=F32)
+
+
+def dot_rows(left, right):
+    return lax.dot_general(left, right, (((0,), (0,)), ((), ())), preferred_element_type=F32)
+
+
+def dot_cols(left, right):
+    return lax.dot_general(left, right, (((1,), (1,)), ((), ())), preferred_element_type=F32)
+
+
+def norm_back(d_normed, normed, rms):
+    return rms * (d_normed - normed * jnp.mean(d_normed * normed, axis=-1, keepdims=True))
 
 
 class Place:
@@ -134,47 +150,57 @@
 
 class ScatterSum:
     def __init__(self, at, part, near, own, far, sem, made=False):
-        self.made = made
-        self.at, self.near, self.own, self.far = at, near, own, far
-        rows = own.shape[1]
-        self.rows = rows
-
-        def block(i):
-            return part.at[pl.ds(pl.multiple_of(i * rows, rows), rows)]
-
-        self.across, self.load, self.send = [], [], []
-        for k in range(at.chips):
-            q = at.chip_at(k)
-            other = part.at[k] if made else block(2 * q + 1 - at.core)
-            self.across.append(remote(other, near.at[k], sem.at[0, k], sem.at[1, k], "fsdp", at.sib))
-            if not made:
-                self.load.append(pltpu.make_async_copy(block(2 * q + at.core), own.at[k], sem.at[2, k]))
-            if k:
-                self.send.append(
-                    remote(own.at[k], far.at[k - 1], sem.at[3, k], sem.at[4, k], "fsdp", 2 * q + at.core))
+        self.at, self.part, self.near, self.own, self.far, self.sem, self.made = at, part, near, own, far, sem, made
+        self.rows = own.shape[1]
+        self.order = list(range(1, at.chips)) + [0]
+
+    def block(self, i):
+        return self.part.at[pl.ds(pl.multiple_of(i * self.rows, self.rows), self.rows)]
+
+    def across(self, k):
+        at = self.at
+        other = self.part.at[k] if self.made else self.block(2 * at.chip_at(k) + 1 - at.core)
+        return remote(other, self.near.at[k], self.sem.at[0, k], self.sem.at[1, k], "fsdp", at.sib)
+
+    def load(self, k):
+        return pltpu.make_async_copy(
+            self.block(2 * self.at.chip_at(k) + self.at.core), self.own.at[k], self.sem.at[2, k])
+
+    def send(self, k):
+        at = self.at
+        return remote(self.own.at[k], self.far.at[k - 1], self.sem.at[3, k], self.sem.at[4, k], "fsdp",
+                      2 * at.chip_at(k) + at.core)
 
     def start(self):
-        for k in list(range(1, self.at.chips)) + [0]:
-            self.across[k].start()
+        for k in self.order:
+            self.across(k).start()
             if not self.made:
-                self.load[k].start()
+                self.load(k).start()
+
+    def pass_on(self, k):
+        self.across(k).wait()
+        if not self.made:
+            self.load(k).wait()
+
+        def add(at):
+            self.own[k, at] = (self.own[k, at].astype(F32) + self.near[k, at].astype(F32)).astype(BF)
+
+        strips(self.rows, add)
+
+        @pl.when(k > 0)
+        def _():
+            self.send(k).start()
 
     def forward(self):
-        for k in list(range(1, self.at.chips)) + [0]:
-            self.across[k].wait()
-            if not self.made:
-                self.load[k].wait()
-
-            def add(at, k=k):
-                self.own[k, at] = (self.own[k, at].astype(F32) + self.near[k, at].astype(F32)).astype(BF)
-
-            strips(self.rows, add)
-            if k:
-                self.send[k - 1].start()
+        def step(i, carry):
+            self.pass_on(lax.rem(i + 1, self.at.chips))
+            return carry
+
+        lax.fori_loop(0, self.at.chips, step, 0)
 
     def wait(self):
-        for c in self.send:
-            c.wait()
+        for k in range(1, self.at.chips):
+            self.send(k).wait()
 
     def total(self, at):
         out = self.own[0, at].astype(F32)
@@ -345,90 +371,201 @@
             lambda s: wc.at[pl.ds(pl.multiple_of(s * depth, depth), depth)])
 
 
-def begin_kernel(n, n_z, x_ref, gain_ref, place_ref, wqkv_ref, n1_ref, wc_ref, places_ref,
-                 own, s_x, r_x, s_g, s_p, r_p):
+class Weights:
+    def __init__(self, at, pairs, send, recv, z_send, z_recv):
+        self.at, self.pairs, self.send, self.recv, self.z_send, self.z_recv = at, pairs, send, recv, z_send, z_recv
+        self.depth, self.share = pairs[0][0].shape[0], pairs[0][1].shape[1]
+        self.mine = at.core == lax.rem(at.z, 2)
+        self.parity = lax.rem(at.z + at.core, 2)
+        self.partner = at.z + 1 - 2 * lax.rem(at.z, 2)
+
+    def cols(self, i, t):
+        return self.pairs[i][0].at[:, pl.ds(pl.multiple_of(t * self.share, HEAD_WIDTH), self.share)]
+
+    def rows(self, i, s):
+        return self.pairs[i][1].at[pl.ds(pl.multiple_of(s * self.depth, self.depth), self.depth)]
+
+    def local(self, i):
+        return pltpu.make_async_copy(self.cols(i, self.at.f), self.rows(i, self.at.f), self.recv.at[i, 0])
+
+    def copy(self, i, j):
+        to = self.at.near(j)
+        return remote(self.cols(i, to), self.rows(i, self.at.f), self.send.at[i, j], self.recv.at[i, j], "fsdp", to)
+
+    def beside(self, i, j):
+        here = self.rows(i, self.at.near_from(j))
+        return remote(here, here, self.z_send.at[i, j], self.z_recv.at[i, j], "replica", self.partner)
+
+    def start(self, i):
+        self.local(i).start()
+        self.copy(i, 1).start()
+
+        @pl.when(self.mine)
+        def _():
+            for j in range(2, self.at.n):
+                self.copy(i, j).start()
+
+    def hand_over(self, i):
+        for m in range(1, self.at.chips):
+            j = 2 * m + self.parity
+            here = self.rows(i, self.at.near_from(j))
+            pltpu.make_async_copy(here, here, self.recv.at[i, j]).wait()
+            self.beside(i, j).start()
+
+    def wait(self, i):
+        self.local(i).wait()
+        self.copy(i, 1).wait()
+
+        @pl.when(self.mine)
+        def _():
+            for j in range(2, self.at.n):
+                self.copy(i, j).wait_send()
+
+        for m in range(1, self.at.chips):
+            self.beside(i, 2 * m + self.parity).wait_send()
+            self.beside(i, 2 * m + 1 - self.parity).wait_recv()
+
+
+def front_kernel(n, n_z, x_ref, gain1_ref, gain2_ref, gainq_ref, gaink_ref, place_ref, table_ref, wout_ref,
+                 wqkv_ref, g_ref, gate_ref, up_ref, down_ref,
+                 h_ref, q_ref, kv_ref, ctx_ref, proj_ref, places_ref,
+                 n1_ref, wc_ref, n2_ref, gall_ref, gate_c, up_c, down_c,
+                 near, mine, far, stage, own, n1_block, wc,
+                 s_x, r_x, s_p, r_p, s_g, s_n, s_w, s_h, s_r, s_a, s_b, s_c, r_c, s_z, r_z):
     at = Place(n, n_z)
     rows = x_ref.shape[0]
-    at.greet(False)
-    weights = Exchange(at, qkv_pieces(at, wqkv_ref, wc_ref, QUERY_HEADS * HEAD_WIDTH // n), s_x, r_x)
-    place = Exchange(at, [(lambda t: place_ref, lambda s: places_ref.at[s])], s_p, r_p)
-    place.start()
+    heads = QUERY_HEADS // n
+    qw = heads * HEAD_WIDTH
+    halo = LMAX
+    at.greet(True)
+    weights = Exchange(at, qkv_pieces(at, wqkv_ref, wc_ref, qw), s_x, r_x)
+
+    def rows_of(g):
+        return pl.ds(pl.multiple_of(g * rows, rows), rows)
+
+    places = Exchange(at, [(lambda t: place_ref, lambda s: places_ref.at[rows_of(s)])], s_p, r_p)
+    mlp = Weights(at, [(gate_ref, gate_c), (up_ref, up_c), (down_ref, down_c)], s_c, r_c, s_z, r_z)
+    places.start()
+
+    def norm1(strip):
+        x = x_ref[strip].astype(F32)
+        own[strip] = (x * rms_of(x) * gain1_ref[...]).astype(BF)
+
+    strips(rows, norm1)
+    n1 = Gather(at, own, n1_ref, s_g)
+    n1.start()
     weights.start()
-
-    def norm(strip):
-        x = x_ref[strip].astype(F32)
-        own[strip] = (x * rms_of(x) * gain_ref[...]).astype(BF)
-
-    strips(rows, norm)
-    gather = Gather(at, own, n1_ref, s_g)
-    gather.start()
-    gather.forward()
-    gather.wait()
-    place.wait()
+    n1.forward()
+    n1.wait()
+    places.wait()
     weights.wait()
-
-
-def middle_kernel(n, n_z, part_ref, x_ref, gain_ref, g_ref, gate_ref, up_ref, down_ref,
-                  h_ref, n2_ref, gall_ref, gate_c, up_c, down_c,
-                  near, mine, far, own, s_r, s_a, s_b, s_x, r_x, s_y, r_y):
-    at = Place(n, n_z)
-    share = gate_c.shape[1]
-    at.greet(False)
-    total = ScatterSum(at, part_ref, near, mine, far, s_r)
-    total.start()
-    total.forward()
-    first = Exchange(at, [col_piece(gate_ref, gate_c, share), col_piece(up_ref, up_c, share)], s_x, r_x)
-    second = Exchange(at, [col_piece(down_ref, down_c, share)], s_y, r_y)
-    first.start()
-    total.wait()
-
-    def norm(strip):
-        h = x_ref[strip].astype(F32) + total.total(strip)
+    mlp.start(0)
+    mlp.start(1)
+    to_vmem = pltpu.make_async_copy(wc_ref, wc, s_w.at[0])
+    to_vmem.start()
+
+    def block_of(g):
+        return pltpu.make_async_copy(n1_ref.at[rows_of(g)], n1_block.at[lax.rem(g, 2)], s_n.at[lax.rem(g, 2)])
+
+    block_of(0).start()
+    to_vmem.wait()
+
+    def project(g, carry):
+        @pl.when(g + 1 < n)
+        def _():
+            block_of(g + 1).start()
+
+        at_rows = rows_of(g)
+        cosine, sine = rotation_of(places_ref[at_rows], table_ref)
+        block_of(g).wait()
+        proj = dot(n1_block[lax.rem(g, 2)], wc[...])
+        proj_ref[at_rows] = proj[:, :qw + HEAD_WIDTH]
+        for head in range(heads + 1):
+            lanes = slice(head * HEAD_WIDTH, (head + 1) * HEAD_WIDTH)
+            raw = proj[:, lanes]
+            gain = gainq_ref if head < heads else gaink_ref
+            turned = rotate_with(raw * rms_of(raw) * gain[...], cosine, sine).astype(BF)
+            if head < heads:
+                q_ref[at_rows, lanes] = turned
+            else:
+                kv_ref[g, halo:, :HEAD_WIDTH] = turned
+        kv_ref[g, halo:, HEAD_WIDTH:] = proj[:, qw + HEAD_WIDTH:].astype(BF)
+        return carry
+
+    lax.fori_loop(0, n, project, 0)
+    not_first, not_last = at.z > 0, at.z < n_z - 1
+
+    def halo_copy():
+        return remote(kv_ref.at[:, pl.ds(rows, halo)], kv_ref.at[:, pl.ds(0, halo)], s_h.at[0], s_h.at[1], "replica",
+                      jnp.minimum(at.z + 1, n_z - 1))
+
+    @pl.when(not_last)
+    def _():
+        halo_copy().start()
+
+    @pl.when(not_first)
+    def _():
+        here = kv_ref.at[:, pl.ds(0, halo)]
+        pltpu.make_async_copy(here, here, s_h.at[1]).wait()
+
+    @pl.when(jnp.logical_not(not_first))
+    def _():
+        kv_ref[:, :halo] = jnp.zeros((n, halo, 2 * HEAD_WIDTH), BF)
+
+    sum_o = ScatterSum(at, stage, near, mine, far, s_r, made=True)
+
+    def attend(g):
+        at_rows = rows_of(g)
+        mask = window_mask(places_ref[at_rows], rows, halo)
+        keys, values = kv_ref[g, :, :HEAD_WIDTH], kv_ref[g, :, HEAD_WIDTH:]
+        for head in range(heads):
+            lanes = slice(head * HEAD_WIDTH, (head + 1) * HEAD_WIDTH)
+            probs = softmax_of(q_ref[at_rows, lanes], keys, mask).astype(BF)
+            ctx_ref[at_rows, lanes] = dot(probs, values).astype(BF)
+        return dot(ctx_ref[at_rows], wout_ref[...]).astype(BF)
+
+    def attend_both(i, carry):
+        k = lax.rem(i + 1, at.chips)
+        q = at.chip_at(k)
+        stage[k] = attend(2 * q + 1 - at.core)
+        sum_o.across(k).start()
+        mine[k] = attend(2 * q + at.core)
+
+        @pl.when(i > 0)
+        def _():
+            sum_o.pass_on(jnp.maximum(i, 1))
+
+        return carry
+
+    lax.fori_loop(0, at.chips, attend_both, 0)
+    sum_o.pass_on(0)
+    mlp.start(2)
+    mlp.hand_over(0)
+    sum_o.wait()
+
+    def norm2(strip):
+        h = x_ref[strip].astype(F32) + sum_o.total(strip)
         h_ref[strip] = h
-        own[strip] = (h * rms_of(h) * gain_ref[...]).astype(BF)
-
-    strips(x_ref.shape[0], norm)
+        own[strip] = (h * rms_of(h) * gain2_ref[...]).astype(BF)
+
+    strips(rows, norm2)
     n2 = Gather(at, own, n2_ref, s_a)
     g_all = Gather(at, g_ref, gall_ref, s_b)
     n2.start()
+    mlp.hand_over(1)
     g_all.start()
-    second.start()
     n2.forward()
+    mlp.hand_over(2)
     g_all.forward()
     n2.wait()
     g_all.wait()
-    first.wait()
-    second.wait()
-
-
-def dot(left, right):
-    return jnp.dot(left, right, preferred_element_type=F32)
-
-
-def dot_rows(left, right):
-    return lax.dot_general(left, right, (((0,), (0,)), ((), ())), preferred_element_type=F32)
-
-
-def dot_cols(left, right):
-    return lax.dot_general(left, right, (((1,), (1,)), ((), ())), preferred_element_type=F32)
-
-
-def rope_tables(positions):
-    half_size = HEAD_WIDTH // 2
-    steps_up = jnp.arange(half_size, dtype=F32)
-    inverse = ROPE_BASE ** (-(2.0 * steps_up) / HEAD_WIDTH)
-    angles = positions.astype(F32)[:, None] * inverse[None, :]
-    return jnp.cos(angles), jnp.sin(angles)
-
-
-def rotate(values, cosine, sine):
-    half_size = HEAD_WIDTH // 2
-    first, second = values[..., :half_size], values[..., half_size:]
-    return jnp.concatenate([first * cosine - second * sine, second * cosine + first * sine], axis=-1)
-
-
-def norm_back(d_normed, normed, rms):
-    return rms * (d_normed - normed * jnp.mean(d_normed * normed, axis=-1, keepdims=True))
+
+    @pl.when(not_last)
+    def _():
+        halo_copy().wait_send()
+
+    for i in range(3):
+        mlp.wait(i)
 
 
 class Feed:
@@ -531,7 +668,8 @@
         return gmlp_ref.at[j // n, :, pl.ds(pl.multiple_of(s * share, HEAD_WIDTH), share)]
 
     def attn_place(j):
-        return gqkv_ref.at[jnp.where(j < outs, j, outs + at.near_from(jnp.maximum(j - outs, 0)))]
+        col = jnp.where(j < outs, j, outs + at.near_from(jnp.maximum(j - outs, 0)))
+        return gqkv_ref.at[:, pl.ds(pl.multiple_of(col * share_out, HEAD_WIDTH), share_out)]
 
     feed = Feed(at, (down_ref, gate_ref, up_ref), chunk, s_c, r_c)
     lines = Lines(
@@ -738,46 +876,30 @@
     lines.settle()
 
 
-def begin(n, n_z, x, gain, place, w_qkv):
+def front(n, n_z, x, gain1, gain2, gain_q, gain_k, place, table, w_out, w_qkv, g, gate, up, down):
     rows, width = x.shape
-    total, wide = n * rows, (QUERY_HEADS // n + 2) * HEAD_WIDTH
+    chips, share, total = n // 2, gate.shape[1] // n, n * rows
+    qw = QUERY_HEADS * HEAD_WIDTH // n
+    wide = qw + 2 * HEAD_WIDTH
+    block = functools.partial(pltpu.VMEM, dtype=BF)
+    shape = jax.ShapeDtypeStruct
     return pl.pallas_call(
-        functools.partial(begin_kernel, n, n_z),
+        functools.partial(front_kernel, n, n_z),
         out_shape=(
-            jax.ShapeDtypeStruct((total, width), BF),
-            jax.ShapeDtypeStruct((width, wide), BF),
-            jax.ShapeDtypeStruct((n,) + place.shape, place.dtype),
-        ),
-        in_specs=[VMEM, VMEM, ANY, ANY],
-        out_specs=(ANY, ANY, ANY),
+            shape((rows, width), F32), shape((total, qw), BF), shape((n, LMAX + rows, 2 * HEAD_WIDTH), BF),
+            shape((total, qw), BF), shape((total, qw + HEAD_WIDTH), F32), shape((total, HEAD_WIDTH), BF),
+            shape((total, width), BF), shape((width, wide), BF), shape((total, width), BF), shape((total, width), BF),
+        ) + (shape((width, share), BF),) * 3,
+        in_specs=[VMEM] * 8 + [ANY] * 5,
+        out_specs=(VMEM,) * 6 + (ANY,) * 7,
         scratch_shapes=[
-            pltpu.VMEM((rows, width), BF), DMA((3, n)), DMA((3, n)), DMA((6, n)), DMA((1, n)), DMA((1, n))],
-        compiler_params=pltpu.CompilerParams(collective_id=0, has_side_effects=True, vmem_limit_bytes=32 << 20),
-        name="begin",
-    )(x, gain, place, w_qkv)
-
-
-def middle(n, n_z, part, x, gain, g, gate, up, down):
-    rows, width = x.shape
-    total, share, chips = n * rows, gate.shape[1] // n, n // 2
-    columns = jax.ShapeDtypeStruct((width, share), BF)
-    return pl.pallas_call(
-        functools.partial(middle_kernel, n, n_z),
-        out_shape=(
-            jax.ShapeDtypeStruct((rows, width), F32),
-            jax.ShapeDtypeStruct((total, width), BF),
-            jax.ShapeDtypeStruct((total, width), BF),
-            columns, columns, columns,
-        ),
-        in_specs=[ANY, VMEM, VMEM, ANY, ANY, ANY, ANY],
-        out_specs=(VMEM, ANY, ANY, ANY, ANY, ANY),
-        scratch_shapes=[
-            pltpu.VMEM((chips, rows, width), BF), pltpu.VMEM((chips, rows, width), BF),
-            pltpu.VMEM((chips - 1, rows, width), BF), pltpu.VMEM((rows, width), BF),
-            DMA((5, n)), DMA((6, n)), DMA((6, n)), DMA((2, n)), DMA((2, n)), DMA((1, n)), DMA((1, n))],
-        compiler_params=pltpu.CompilerParams(collective_id=1, has_side_effects=True, vmem_limit_bytes=48 << 20),
-        name="middle",
-    )(part, x, gain, g, gate, up, down)
+            block((chips, rows, width)), block((chips, rows, width)), block((chips - 1, rows, width)),
+            block((chips, rows, width)), block((rows, width)), block((2, rows, width)), block((width, wide)),
+            DMA((3, n)), DMA((3, n)), DMA((1, n)), DMA((1, n)), DMA((6, n)), DMA((2,)), DMA((1,)), DMA((2,)),
+            DMA((5, n)), DMA((6, n)), DMA((6, n)), DMA((3, n)), DMA((3, n)), DMA((3, n)), DMA((3, n))],
+        compiler_params=pltpu.CompilerParams(collective_id=0, has_side_effects=True, vmem_limit_bytes=60 << 20),
+        name="front",
+    )(x, gain1, gain2, gain_q, gain_k, place, table, w_out, w_qkv, g, gate, up, down)
 
 
 def back(n, n_z, part, part_y, x, h, g, gain1, gain2, gain_q, gain_k, down, gate, up, w_out, w_qkv, q, kv, ctx, proj,
@@ -795,7 +917,7 @@
             jax.ShapeDtypeStruct((rows, width), BF),
             jax.ShapeDtypeStruct(gains, F32),
             jax.ShapeDtypeStruct((3, depth, n * share), BF),
-            jax.ShapeDtypeStruct((count2, depth, wide), BF),
+            jax.ShapeDtypeStruct((depth, count2 * wide), BF),
             jax.ShapeDtypeStruct((n * rows, width), BF),
         ),
         in_specs=[ANY, ANY] + [VMEM] * 7 + [ANY] * 3 + [VMEM] * 8 + [ANY],
@@ -842,50 +964,11 @@
 
     pos = row_positions(dealt_lens[0].reshape(-1), seq_order[0], replica * rows, rows)
     depth = w_qkv.shape[0]
-    place = jnp.zeros((8, HEAD_WIDTH), jnp.int32).reshape(-1).at[:rows].set(pos).reshape(8, HEAD_WIDTH)
-    n1, w_qkv_c, places = begin(n_fsdp, n_replica, tokens, gain_attn[None], place, w_qkv)
-    pos_all = places.reshape(n_fsdp, -1)[:, :rows].reshape(-1)
-
-    total = n1.shape[0]
-
-    proj = dot(n1, w_qkv_c)
-    q_rows = proj[:, :qw].reshape(total, heads, HEAD_WIDTH)
-    k_rows = proj[:, qw:qw + HEAD_WIDTH]
-    v_low = proj[:, qw + HEAD_WIDTH:].astype(BF)
-    rq = lax.rsqrt(jnp.mean(q_rows * q_rows, axis=2, keepdims=True) + EPSILON)
-    q_hat = q_rows * rq
-    rk = lax.rsqrt(jnp.mean(k_rows * k_rows, axis=1, keepdims=True) + EPSILON)
-    k_hat = k_rows * rk
-    cosine, sine = rope_tables(pos_all)
-    q_low = rotate(q_hat * gain_query, cosine[:, None], sine[:, None]).astype(BF)
-    k_low = rotate(k_hat * gain_key, cosine, sine).astype(BF)
-
-    groups = n_fsdp
-    halo = LMAX
-    kv = jnp.concatenate([k_low, v_low], axis=1).reshape(groups, rows, 2 * HEAD_WIDTH)
-    up_pairs = [(i, i + 1) for i in range(n_replica - 1)]
-    down_pairs = [(i + 1, i) for i in range(n_replica - 1)]
-    kv_before = lax.ppermute(kv[:, rows - halo:], "replica", up_pairs)
-    kv_window = jnp.concatenate([kv_before, kv], axis=1)
-    k_win, v_win = kv_window[..., :HEAD_WIDTH], kv_window[..., HEAD_WIDTH:]
-    q_grp = q_low.reshape(groups, rows, heads, HEAD_WIDTH)
-    pos_grp = pos_all.reshape(groups, rows)
-    i_at = halo + jnp.arange(rows, dtype=jnp.int32)
-    j_at = jnp.arange(halo + rows, dtype=jnp.int32)
-    mask = (j_at[None, None, :] <= i_at[None, :, None]) & (
-        j_at[None, None, :] >= i_at[None, :, None] - pos_grp[:, :, None])
-    mask = mask[:, None]
-    scale = HEAD_WIDTH ** (-0.5)
-    scores = jnp.einsum("gqhd,gkd->ghqk", q_grp, k_win, preferred_element_type=F32) * scale
-    scores = jnp.where(mask, scores, NEG_FILL)
-    top = jnp.max(scores, axis=3, keepdims=True)
-    terms = jnp.exp(scores - top)
-    probs = terms / jnp.sum(terms, axis=3, keepdims=True)
-    probs_low = probs.astype(BF)
-    ctx = jnp.einsum("ghqk,gkd->gqhd", probs_low, v_win, preferred_element_type=F32)
-    ctx_low = ctx.reshape(total, qw).astype(BF)
-    h, n2, g_all, gate_c, up_c, down_c = middle(
-        n_fsdp, n_replica, dot(ctx_low, w_out).astype(BF), tokens, gain_mlp[None], cotangent, w_gate, w_up, w_down_t)
+    place = jnp.broadcast_to(pos.astype(BF)[:, None], (rows, HEAD_WIDTH))
+    table = rotation_table()
+    gains = (gain_attn[None], gain_mlp[None], gain_query[None], gain_key[None])
+    h, q_low, kv_window, ctx_low, proj, places, n1, w_qkv_c, n2, g_all, gate_c, up_c, down_c = front(
+        n_fsdp, n_replica, tokens, *gains, place, table, w_out, w_qkv, cotangent, w_gate, w_up, w_down_t)
 
     gate = dot(n2, gate_c)
     up = dot(n2, up_c)
@@ -898,27 +981,23 @@
     d_gate = (d_act * up * sg * (1.0 + gate * (1.0 - sg))).astype(BF)
     d_up = (d_act * silu).astype(BF)
 
-    places = jnp.broadcast_to(pos_all.astype(BF)[:, None], (total, HEAD_WIDTH))
-    input_grad, output, gains, g_mlp, g_attn, _ = back(
-        n_fsdp, n_replica, (dot_cols(d_gate, gate_c) + dot_cols(d_up, up_c)).astype(BF), part_y, tokens, h, cotangent,
-        gain_attn[None], gain_mlp[None], gain_query[None], gain_key[None],
+    input_grad, output, gain_sums, g_mlp, g_attn, _ = back(
+        n_fsdp, n_replica, (dot_cols(d_gate, gate_c) + dot_cols(d_up, up_c)).astype(BF), part_y, tokens, h, cotangent, *gains,
         dot_rows(g_all, act).astype(BF), dot_rows(n2, d_gate).astype(BF), dot_rows(n2, d_up).astype(BF),
-        w_out, w_qkv_c, q_low.reshape(total, qw), kv_window, ctx_low, proj[:, :qw + HEAD_WIDTH],
-        rotation_table(), places, n1)
-    outs = g_attn.shape[0] - n_fsdp
-    g_out = g_attn[:outs].transpose(1, 0, 2).reshape(depth, -1)[:, :width]
-    g_qkv = g_attn[outs:].transpose(1, 0, 2).astype(F32)
-
-    def of_key_heads(part):
-        return jnp.sum(part.reshape(depth, KEY_VALUE_HEADS, shared, HEAD_WIDTH), axis=2).reshape(depth, k_w)
-
-    g_qkv = jnp.concatenate([
-        g_qkv[:, :, :qw].reshape(depth, q_w),
-        of_key_heads(g_qkv[:, :, qw:qw + HEAD_WIDTH]),
-        of_key_heads(g_qkv[:, :, qw + HEAD_WIDTH:])], axis=1)
+        w_out, w_qkv_c, q_low, kv_window, ctx_low, proj, table, places, n1)
+    wide = qw + 2 * HEAD_WIDTH
+    g_out = g_attn[:, :width]
+    by_device = [g_attn[:, at:at + wide] for at in range(g_attn.shape[1] - n_fsdp * wide, g_attn.shape[1], wide)]
+
+    def of_key_heads(first):
+        parts = [part[:, first:first + HEAD_WIDTH].astype(F32) for part in by_device]
+        return [sum(parts[i + 1:i + shared], parts[i]) for i in range(0, n_fsdp, shared)]
+
+    g_qkv = jnp.concatenate(
+        [part[:, :qw].astype(F32) for part in by_device] + of_key_heads(qw) + of_key_heads(qw + HEAD_WIDTH), axis=1)
     return (
         output, input_grad, g_qkv, g_out.astype(F32), g_mlp[1].astype(F32), g_mlp[2].astype(F32), g_mlp[0].astype(F32),
-        gains[0], gains[1], gains[2, :HEAD_WIDTH], gains[2, HEAD_WIDTH:2 * HEAD_WIDTH])
+        gain_sums[0], gain_sums[1], gain_sums[2, :HEAD_WIDTH], gain_sums[2, HEAD_WIDTH:2 * HEAD_WIDTH])
 
 
 def solution(mesh):

time: 811 us -> 694 us (0.86)
  Pallas kernels: 641 us -> 599 us
  local copies, waits for them, and re-layouts: 45.7 us -> 8.7 us
  matrix products: 84.4 us -> 68.1 us
  other arithmetic: 28 us -> 13.2 us
    pallas_call x2 -> x1, Pallas kernels: 276 us -> 233 us  [front(): pl.pallas_call(functools.partial(front_kernel, n, n_z), out_shape=(shape(...]
    unnamed x77 -> x47, local copies, waits for them, and re-layouts: 19.7 us -> 4.31 us
    dot_general x5 -> x3, matrix products: 35.6 us -> 26.4 us  [dot(): return jnp.dot(left, right, preferred_element_type=F32)]
    slice x11 -> x1, local copies, waits for them, and re-layouts: 10.3 us -> 1.53 us  [per_device(): gain_sums[1]]
  transfers between devices with their start and end apart: 1 -> 0, of which waited for: 0 -> 0; matrix products, arithmetic and copies ran while one was open for 1% -> 0% of each run, Pallas kernels for 0% -> 0%
where the time goes in v5:
time: 694 us; the launch traced here: 690 us
  Pallas kernels  599 us (86%)
  matrix products  68.1 us (10%)
  other arithmetic  13.2 us (2%)
  local copies, waits for them, and re-layouts  8.7 us (1%)
    pallas_call x1, Pallas kernels, back(): pl.pallas_call(functools.partial(back_kernel, n, n_z), out_shape=(jax.Sha...  366 us
    pallas_call x1, Pallas kernels, front(): pl.pallas_call(functools.partial(front_kernel, n, n_z), out_shape=(shape(...  233 us
    dot_general x3, matrix products, dot(): return jnp.dot(left, right, preferred_element_type=F32)  26.4 us
    dot_general x3, matrix products, dot_rows(): lax.dot_general(left, right, (((0,), (0,)), ((), ())), preferred_element_...  21.9 us
    dot_general x3, matrix products, dot_cols(): lax.dot_general(left, right, (((1,), (1,)), ((), ())), preferred_element_...  19.9 us

profile of v5, /device:TPU:0, one launch (start us, length us, event | category | flops | bytes accessed | tf_op | source)
XLA Modules:
  0.0 690.4 jit_solution(3929986911585175141)
XLA Ops:
  0.6 0.8 mul.35
  1.4 0.8 select_reduce_fusion.1
  2.2 0.1 select_reduce_fusion
  2.3 0.7 broadcast_in_dim.36.place_ref
  3.1 232.9 %front.1 = (f32[192,2048]{1,0:T(8,128)}, bf16[1536,256]{1,0:T(8,128)(2,1)}, bf16[8,288,256]{2,1,0:T(8,128)(2,1)}, bf16[1536,256]{1,0:T(8,128)(2,1)}, f32[1536,38...) custom-call(bf16[192,2048]{1,0:T(8,128)(2,1)} %x_ref.3, ...), custom_call_target="tpu_custom_call" | custom-call | tf_op jit(solution)/shard_map/front/pallas_call | solution.py:886
  236.0 0.0 copy-start.4
  236.0 0.0 copy-start.6
  236.0 9.6 %fusion.2 = f32[1536,768]{1,0:T(8,128)} fusion(bf16[1536,2048]{1,0:T(8,128)(2,1)} %get-tuple-element.29, bf16[2048,768]{1,0:T(8,128)(2,1)} %get-tuple-element.30), kind=kOutput, calls=%fused_computation.45 | convolution fusion | flops 4831838208 | bytes 14155776 | tf_op jit(solution)/shard_map/dot_general | solution.py:35
  245.6 0.0 copy-done.4
  245.6 0.0 copy-done.6
  245.6 0.0 copy-start.5
  245.6 0.0 slice-start
  245.7 6.6 fusion.3
  252.3 0.0 copy-done.5
  252.3 0.0 slice-start.1
  252.3 10.1 %multiply_convert_fusion = (bf16[1536,768]{1,0:T(8,128)(2,1)}, bf16[1536,768]{1,0:T(8,128)(2,1)S(1)}, bf16[1536,768]{1,0:T(8,128)(2,1)S(1)}) fusion(f32[1536,768]{1,0:T(8,128)} %fusion.3, f32[1536,768]{1,0:T(8,128)} %fusion.2, bf16[1536,2048]{1,0:T(8,128)(2,1)S(1)} %copy-done.4, bf16[2048,768]{1,0:T(8,128)(2,1)S(1)} %copy-done.5), kind=kOutput, calls=%fused_computation.2 | convolution fusion | flops 4849532928 | bytes 25952256 | tf_op jit(solution)/shard_map/dot_general | solution.py:35
  262.4 0.0 slice-done
  262.4 0.0 slice-done.1
  262.4 0.0 copy-start.7
  262.4 0.0 copy-start.8
  262.4 8.5 %convolution_convert_fusion.3.down_ref = bf16[2048,768]{1,0:T(8,128)(2,1)} fusion(bf16[1536,2048]{1,0:T(8,128)(2,1)S(1)} %bitcast.50, bf16[1536,768]{1,0:T(8,128)(2,1)} %get-tuple-element.50), kind=kOutput, calls=%fused_computation.9 | convolution fusion | flops 4833411072 | bytes 11796480 | tf_op jit(solution)/shard_map/dot_general | solution.py:39
  270.9 0.0 copy-done.7
  270.9 0.0 copy-done.8
  270.9 7.2 %convolution_convert_fusion.party_ref = bf16[1536,2048]{1,0:T(8,128)(2,1)} fusion(bf16[1536,768]{1,0:T(8,128)(2,1)S(1)} %copy-done.8, bf16[2048,768]{1,0:T(8,128)(2,1)S(1)} %copy-done.7), kind=kOutput, calls=%fused_computation.1 | convolution fusion | flops 4834983936 | bytes 11796480 | tf_op jit(solution)/shard_map/dot_general | solution.py:43
  278.2 6.7 convolution_convert_fusion.2.gate_ref
  284.8 6.7 convolution_convert_fusion.1.up_ref
  291.5 5.1 fusion.4
  296.7 7.5 %add_convert_fusion.part_ref = bf16[1536,2048]{1,0:T(8,128)(2,1)} fusion(f32[1536,2048]{1,0:T(8,128)S(1)} %fusion.4, bf16[1536,768]{1,0:T(8,128)(2,1)S(1)} %get-tuple-element.52, bf16[2048,768]{1,0:T(8,128)(2,1)S(1)} %copy-done.5), kind=kOutput, calls=%fused_computation | convolution fusion | flops 4838129664 | bytes 24379392 | tf_op jit(solution)/shard_map/dot_general | solution.py:43
  304.2 366.3 %back.1 = (bf16[192,2048]{1,0:T(8,128)(2,1)}, bf16[192,2048]{1,0:T(8,128)(2,1)}, f32[8,2048]{1,0:T(8,128)}, bf16[3,256,6144]{2,1,0:T(8,128)(2,1)}, bf16[256,6144...) custom-call(bf16[1536,2048]{1,0:T(8,128)(2,1)} %add_convert_fusion.part_ref, ...), custom_call_target="tpu_custom_call" | custom-call | tf_op jit(solution)/shard_map/back/pallas_call | solution.py:913
  670.5 0.0 copy-start.1
  670.5 1.4 slice_bitcast_fusion
  671.9 1.5 fusion.1
  673.4 2.8 slice_convert_fusion
  676.2 0.0 copy-done.1
  676.3 0.0 copy-start
  676.9 2.6 concatenate.7
  679.6 1.9 copy-done
  681.5 0.0 copy-start.3
  681.5 0.0 copy-start.2
  681.5 6.9 bitcast_convert_fusion
  688.4 0.0 copy-done.3
  688.4 0.9 copy.50
  689.2 0.0 copy-done.2
  689.2 0.9 copy.51
  (27 shorter events, 0.7 us)
Async XLA Ops:
  236.0 9.6 %copy-start.4 = (bf16[1536,2048]{1,0:T(8,128)(2,1)S(1)}, bf16[1536,2048]{1,0:T(8,128)(2,1)}, u32[]{:S(2)}) copy-start(bf16[1536,2048]{1,0:T(8,128)(2,1)} %get-tuple-element.31) | copy-start | bytes 18874372
  236.0 9.6 %copy-start.6 = (bf16[2048,768]{1,0:T(8,128)(2,1)S(1)}, bf16[2048,768]{1,0:T(8,128)(2,1)}, u32[]{:S(2)}) copy-start(bf16[2048,768]{1,0:T(8,128)(2,1)} %get-tuple-element.33) | copy-start | bytes 9437188
  245.6 6.7 copy-start.5
  245.6 16.8 %slice-start = ((s8[6291456]{0:T(1024)(128)(4,1)}), s8[4194304]{0:T(1024)(128)(4,1)S(1)}, s32[]{:S(2)}) async-start(s8[6291456]{0:T(1024)(128)(4,1)} %bitcast.49), calls=%async_computation | async-start | bytes 8388608
  252.3 10.1 %slice-start.1 = ((s8[6291456]{0:T(1024)(128)(4,1)}), s8[2097152]{0:T(1024)(128)(4,1)S(1)}, s32[]{:S(2)}) async-start(s8[6291456]{0:T(1024)(128)(4,1)} %bitcast.49), calls=%async_computation.1 | async-start | bytes 4194304
  262.4 8.5 %copy-start.7 = (bf16[2048,768]{1,0:T(8,128)(2,1)S(1)}, bf16[2048,768]{1,0:T(8,128)(2,1)}, u32[]{:S(2)}) copy-start(bf16[2048,768]{1,0:T(8,128)(2,1)} %get-tuple-element.30) | copy-start | bytes 9437188
  262.4 8.5 %copy-start.8 = (bf16[1536,768]{1,0:T(8,128)(2,1)S(1)}, bf16[1536,768]{1,0:T(8,128)(2,1)}, u32[]{:S(2)}) copy-start(bf16[1536,768]{1,0:T(8,128)(2,1)} %get-tuple-element.50) | copy-start | bytes 7077892
  670.5 5.7 copy-start.1
  676.3 5.2 copy-start
  681.5 6.9 copy-start.3
  681.5 7.8 %copy-start.2 = (bf16[192,2048]{1,0:T(8,128)(2,1)S(1)}, bf16[192,2048]{1,0:T(8,128)(2,1)}, u32[]{:S(2)}) copy-start(bf16[192,2048]{1,0:T(8,128)(2,1)} %get-tuple-element.69) | copy-start | bytes 2359300

commit v6 on v5

--- a/solution.py
+++ b/solution.py
@@ -27,7 +27,6 @@
 STRIP = 16
 LAG_MID = 2
 LAG_END = 6
-RING = 4
 LEAD = 5
 
 
@@ -116,6 +115,64 @@
             c.wait()
 
 
+class SquareGather:
+    def __init__(self, at, own, whole, sem):
+        rows = own.shape[0]
+        half = rows // 2
+        beside = (2 * (at.chip + 1 - 2 * lax.rem(at.chip, 2)) + at.core, 2 * at.chip_at(2) + at.core)
+
+        def part(i, h):
+            return whole.at[pl.ds(pl.multiple_of(i * rows + h * half, half), half)]
+
+        def block(i):
+            return whole.at[pl.ds(pl.multiple_of(i * rows, rows), rows)]
+
+        def across(i, k):
+            return remote(block(i), block(i), sem.at[0, k], sem.at[1, k], "fsdp", at.sib)
+
+        self.local = pltpu.make_async_copy(own, block(at.f), sem.at[0, 0])
+        self.out = [[remote(own.at[pl.ds(h * half, half)], part(at.f, h), sem.at[2 + w, h], sem.at[4 + w, h], "fsdp", beside[w])
+                     for h in range(2)] for w in range(2)]
+        self.on = [remote(part(beside[w], w), part(beside[w], w), sem.at[2 + w, 2], sem.at[4 + w, 2], "fsdp", beside[1 - w])
+                   for w in range(2)]
+        far = 2 * (at.chips - 1 - at.chip) + at.core
+        self.across = [remote(own, block(at.f), sem.at[0, 1], sem.at[1, 1], "fsdp", at.sib)]
+        self.across += [across(beside[0], 2), across(beside[1], 3), across(far, 4)]
+
+    def start(self):
+        for w in range(2):
+            self.out[w][w].start()
+        for w in range(2):
+            self.out[w][1 - w].start()
+        self.across[0].start()
+        self.local.start()
+
+    def relay(self):
+        for w in range(2):
+            self.out[w][w].wait_recv()
+            self.on[w].start()
+
+    def forward(self):
+        for w in range(2):
+            self.out[w][1 - w].wait_recv()
+            self.across[1 + w].start()
+        for w in range(2):
+            self.on[w].wait_recv()
+        self.across[3].start()
+
+    def wait(self):
+        for w in range(2):
+            self.out[w][0].wait_send()
+            self.out[w][1].wait_send()
+            self.on[w].wait_send()
+        for c in self.across + [self.local]:
+            c.wait()
+
+
+def gather_rows(at, own, whole, sem):
+    return (SquareGather if at.chips == 4 else Gather)(at, own, whole, sem)
+
+
 class Gather:
     def __init__(self, at, own, whole, sem):
         rows = own.shape[0]
@@ -136,6 +193,9 @@
         for c in self.far + self.across + [self.local]:
             c.start()
 
+    def relay(self):
+        pass
+
     def forward(self):
         for far, on in zip(self.far, self.on):
             far.wait_recv()
@@ -214,11 +274,12 @@
         self.at, self.chunk, self.ring, self.arrive, self.skip = at, chunk, ring, arrive, skip
         self.send, self.recv, self.credit, self.out, self.out_sem = send, recv, credit, out, out_sem
         self.feed = feed
+        self.slots = ring.shape[1]
         self.count = chunk.shape[0]
         self.kind = at.mid.astype(jnp.int32)
 
     def slot(self, j):
-        return lax.rem(j, RING)
+        return lax.rem(j, self.slots)
 
     def inward(self, j):
         return remote(self.chunk.at[j], self.ring.at[self.kind, self.slot(j)], self.send.at[0, j],
@@ -235,7 +296,7 @@
         pltpu.make_async_copy(here, here, self.recv.at[kind, j]).wait()
         self.chunk[j] = (self.chunk[j].astype(F32) + self.ring[kind, self.slot(j)].astype(F32)).astype(BF)
 
-        @pl.when(j + RING < self.count)
+        @pl.when(j + self.slots < self.count)
         def _():
             pl.semaphore_signal(self.credit, inc=1, device_id={"replica": plane}, device_id_type=MESH)
 
@@ -253,7 +314,7 @@
         def _():
             self.take_in(0, j, self.at.outer)
 
-        @pl.when(j >= RING)
+        @pl.when(j >= self.slots)
         def _():
             pl.semaphore_wait(self.credit, 1)
 
@@ -452,9 +513,10 @@
         own[strip] = (x * rms_of(x) * gain1_ref[...]).astype(BF)
 
     strips(rows, norm1)
-    n1 = Gather(at, own, n1_ref, s_g)
+    n1 = gather_rows(at, own, n1_ref, s_g)
     n1.start()
     weights.start()
+    n1.relay()
     n1.forward()
     n1.wait()
     places.wait()
@@ -549,12 +611,14 @@
         own[strip] = (h * rms_of(h) * gain2_ref[...]).astype(BF)
 
     strips(rows, norm2)
-    n2 = Gather(at, own, n2_ref, s_a)
-    g_all = Gather(at, g_ref, gall_ref, s_b)
+    n2 = gather_rows(at, own, n2_ref, s_a)
+    g_all = gather_rows(at, g_ref, gall_ref, s_b)
     n2.start()
     mlp.hand_over(1)
+    n2.relay()
     g_all.start()
     n2.forward()
+    g_all.relay()
     mlp.hand_over(2)
     g_all.forward()
     n2.wait()
@@ -646,12 +710,12 @@
 
 
 def back_kernel(n, n_z, part_ref, party_ref, x_ref, h_ref, g_ref, gain1_ref, gain2_ref, gainq_ref, gaink_ref,
-                down_ref, gate_ref, up_ref, wout_ref, wqkv_ref, q_ref, kv_ref, ctx_ref, proj_ref, table_ref, place_ref,
+                down_ref, n2_ref, dgate_ref, dup_ref, wout_ref, wqkv_ref, q_ref, kv_ref, ctx_ref, proj_ref, table_ref, place_ref,
                 n1_ref,
-                dx_ref, y_ref, gains_ref, gmlp_ref, gqkv_ref, dhall_ref,
-                near, mine, far, stage, own, dh, own_gain, plane_gain, line_gain, all_gain,
-                chunk, ring, chunk2, ring2, dh_block, gout, d_kv, d_proj, halo_out, halo_in, n1_cols, qkv_send,
-                s_r, s_a, s_p, r_p, s_q, r_q, s_c, r_c, s_z, r_z, s_o, s_c2, r_c2, s_z2, r_z2, s_o2, credit, done, s_d, s_n, s_h):
+                dx_ref, y_ref, gains_ref, gmlp_ref, gqkv_ref, dhall_ref, gate_ref, up_ref,
+                near, mine, far, stage, dh, plane_gain, all_gain,
+                chunk, ring, chunk2, ring2, dh_block, gout, d_kv, d_proj, halo_out, halo_in, n1_cols, qkv_send, d_in, tile_out,
+                s_r, s_a, s_p, r_p, s_q, r_q, s_c, r_c, s_z, r_z, s_o, s_c2, r_c2, s_z2, r_z2, s_o2, credit, done, s_d, s_n, s_h, s_e, s_t):
     at = Place(n, n_z)
     share, share_out = chunk.shape[2], chunk2.shape[2]
     rows, width = x_ref.shape
@@ -661,6 +725,8 @@
     qw = heads * HEAD_WIDTH
     halo = LMAX
     scale = HEAD_WIDTH ** (-0.5)
+    own = dh_block
+    own_gain = all_gain.at[at.z]
     at.greet(True)
 
     def mlp_place(j):
@@ -679,9 +745,59 @@
     for c in range(LEAD):
         feed.start(jnp.int32(c))
     sum_n2.start()
+    load = pltpu.make_async_copy(dgate_ref, d_in, s_e.at[0])
+    load.start()
     lines.run(1)
     sum_n2.forward()
-    lines.run(n - 3)
+
+    def fetch_cols(ref, j):
+        return pltpu.make_async_copy(
+            ref.at[:, pl.ds(pl.multiple_of(at.near(j) * depth, depth), depth)], n1_cols.at[lax.rem(j, 2)],
+            s_n.at[lax.rem(j, 2)])
+
+    def tiles(ref, per):
+        def put(j):
+            return pltpu.make_async_copy(
+                tile_out.at[lax.rem(j, 2)], ref.at[pl.ds(pl.multiple_of(at.near(j) * depth, depth), depth)],
+                s_t.at[lax.rem(j, 2)])
+
+        def tile(j):
+            @pl.when(j + 1 < n)
+            def _():
+                fetch_cols(n2_ref, j + 1).start()
+
+            fetch_cols(n2_ref, j).wait()
+
+            @pl.when(j > 1)
+            def _():
+                put(j - 2).wait()
+
+            tile_out[lax.rem(j, 2)] = dot_rows(n1_cols[lax.rem(j, 2)], d_in[...]).astype(BF)
+            put(j).start()
+
+        def body(step):
+            for r in range(per):
+                j = step * per + r
+
+                @pl.when(j < n)
+                def _(j=j):
+                    tile(j)
+
+        def end():
+            put(n - 2).wait()
+            put(n - 1).wait()
+
+        fetch_cols(n2_ref, 0).start()
+        return body, end
+
+    per_tile = -(-n // 3)
+    load.wait()
+    body, end = tiles(gate_ref, per_tile)
+    lines.run(3, body)
+    end()
+    load = pltpu.make_async_copy(dup_ref, d_in, s_e.at[0])
+    load.start()
+    lines.run(n - 8)
     sum_n2.wait()
     own_gain[...] = jnp.zeros_like(own_gain)
 
@@ -696,9 +812,15 @@
         own[strip] = d_h.astype(BF)
 
     strips(rows, back_mlp)
-    gather = Gather(at, own, dhall_ref, s_a)
+    gather = gather_rows(at, own, dhall_ref, s_a)
     gather.start()
-    lines.run(n // 2 + 1)
+    load.wait()
+    body, end = tiles(up_ref, per_tile)
+    lines.run(3, body)
+    end()
+    lines.run(n // 2 - 4)
+    gather.relay()
+    lines.run(2)
     gather.forward()
     lines.run(1)
     gather.wait()
@@ -796,9 +918,7 @@
     lines.run(2, keys_back_some)
 
     def cols_of(j):
-        return pltpu.make_async_copy(
-            n1_ref.at[:, pl.ds(pl.multiple_of(at.near(j) * depth, depth), depth)], n1_cols.at[lax.rem(j, 2)],
-            s_n.at[lax.rem(j, 2)])
+        return fetch_cols(n1_ref, j)
 
     own_qkv = pltpu.make_async_copy(qkv_send.at[0], chunk2.at[outs], r_c2.at[outs])
 
@@ -829,7 +949,6 @@
         for m in range(per_out):
             qkv_grad(i * per_out + m)
 
-    lines.run(4, qkv_grads)
     sum_n1 = ScatterSum(at, stage, near, mine, far, s_r.at[1], made=True)
 
     def n1_part(k):
@@ -837,12 +956,17 @@
         stage[k] = dot_cols(d_proj[rows_of(2 * q + 1 - at.core)], wqkv_ref[...]).astype(BF)
         mine[k] = dot_cols(d_proj[rows_of(2 * q + at.core)], wqkv_ref[...]).astype(BF)
 
-    lines.run(at.chips, n1_part)
+    def both(i):
+        qkv_grads(i)
+        for r in range(at.chips // 4):
+            n1_part(i * (at.chips // 4) + r)
+
+    lines.run(4, both)
     pl.semaphore_wait(done, n - 1)
     sum_n1.start()
     lines.run(1)
     sum_n1.forward()
-    lines.run()
+    lines.run(outs + n - 4 - 1 - 2 - -2)
     sum_n1.wait()
 
     def back_attn(strip):
@@ -856,12 +980,13 @@
     strips(rows, back_attn)
     gains = Exchange(at, [(lambda t: own_gain, lambda s: plane_gain.at[s])], s_p, r_p)
     gains.start()
+    lines.run(1)
     gains.wait()
-    line_gain[...] = jnp.sum(plane_gain[...], axis=0)
+    own_gain[...] = jnp.sum(plane_gain[...], axis=0)
     others = [
-        remote(line_gain, all_gain.at[at.z], s_q.at[k], r_q.at[k], "replica", at.plane(k)) for k in range(1, n_z)]
+        remote(own_gain, all_gain.at[at.z], s_q.at[k], r_q.at[k], "replica", at.plane(k)) for k in range(1, n_z)]
     start_all(others)
-    all_gain[at.z] = line_gain[...]
+    lines.run()
     for c in others:
         c.wait()
     gains_ref[...] = jnp.sum(all_gain[...], axis=0)
@@ -902,7 +1027,7 @@
     )(x, gain1, gain2, gain_q, gain_k, place, table, w_out, w_qkv, g, gate, up, down)
 
 
-def back(n, n_z, part, part_y, x, h, g, gain1, gain2, gain_q, gain_k, down, gate, up, w_out, w_qkv, q, kv, ctx, proj,
+def back(n, n_z, part, part_y, x, h, g, gain1, gain2, gain_q, gain_k, down, n2, d_gate, d_up, w_out, w_qkv, q, kv, ctx, proj,
          table, places, n1):
     rows, width = x.shape
     chips, share, wide, depth = n // 2, down.shape[1], w_qkv.shape[1], width // n
@@ -910,6 +1035,7 @@
     block = functools.partial(pltpu.VMEM, dtype=BF)
     gains = (8, width)
     count2 = outs + n
+    slots = 2 + 16 // n
     return pl.pallas_call(
         functools.partial(back_kernel, n, n_z),
         out_shape=(
@@ -919,26 +1045,28 @@
             jax.ShapeDtypeStruct((3, depth, n * share), BF),
             jax.ShapeDtypeStruct((depth, count2 * wide), BF),
             jax.ShapeDtypeStruct((n * rows, width), BF),
+            jax.ShapeDtypeStruct((width, share), BF),
+            jax.ShapeDtypeStruct((width, share), BF),
         ),
-        in_specs=[ANY, ANY] + [VMEM] * 7 + [ANY] * 3 + [VMEM] * 8 + [ANY],
-        out_specs=(VMEM, VMEM, VMEM, ANY, ANY, ANY),
+        in_specs=[ANY, ANY] + [VMEM] * 7 + [ANY] * 4 + [VMEM] * 8 + [ANY],
+        out_specs=(VMEM, VMEM, VMEM, ANY, ANY, ANY, ANY, ANY),
         scratch_shapes=[
             block((chips, rows, width)), block((chips, rows, width)), block((chips - 1, rows, width)),
-            block((chips, rows, width)), block((rows, width)), pltpu.VMEM((rows, width), F32),
-            pltpu.VMEM(gains, F32), pltpu.VMEM((n,) + gains, F32), pltpu.VMEM(gains, F32), pltpu.VMEM((n_z,) + gains, F32),
-            block((3 * n, depth, share)), block((2, RING, depth, share)),
-            block((count2, depth, wide)), block((2, RING, depth, wide)),
+            block((chips, rows, width)), pltpu.VMEM((rows, width), F32),
+            pltpu.VMEM((n,) + gains, F32), pltpu.VMEM((n_z,) + gains, F32),
+            block((3 * n, depth, share)), block((2, slots, depth, share)),
+            block((count2, depth, wide)), block((2, slots, depth, wide)),
             block((rows, width)), pltpu.VMEM((depth, outs * wide), F32),
             pltpu.VMEM((n, rows, 2 * HEAD_WIDTH), F32), block((n * rows, wide)),
             block((n, LMAX, 2 * HEAD_WIDTH)), block((n, LMAX, 2 * HEAD_WIDTH)),
-            block((2, n * rows, depth)), block((n, depth, wide)),
+            block((2, n * rows, depth)), block((n, depth, wide)), block((n * rows, share)), block((2, depth, share)),
             DMA((3, 5, n)), DMA((6, n)), DMA((1, n)), DMA((1, n)), DMA((n_z,)), DMA((n_z,)),
             DMA((3 * n,)), DMA((3 * n,)), DMA((2, 3 * n)), DMA((3, 3 * n)), DMA((3 * n,)),
             DMA((n,)), DMA((count2,)), DMA((2, count2)), DMA((3, count2)), DMA((count2,)),
-            pltpu.SemaphoreType.REGULAR((2,)), pltpu.SemaphoreType.REGULAR, DMA((1,)), DMA((2,)), DMA((2,))],
-        compiler_params=pltpu.CompilerParams(collective_id=2, has_side_effects=True, vmem_limit_bytes=63 << 20),
+            pltpu.SemaphoreType.REGULAR((2,)), pltpu.SemaphoreType.REGULAR, DMA((1,)), DMA((2,)), DMA((2,)), DMA((1,)), DMA((2,))],
+        compiler_params=pltpu.CompilerParams(collective_id=2, has_side_effects=True, vmem_limit_bytes=511 << 17),
         name="back",
-    )(part, part_y, x, h, g, gain1, gain2, gain_q, gain_k, down, gate, up, w_out, w_qkv, q, kv, ctx, proj, table, places, n1)
+    )(part, part_y, x, h, g, gain1, gain2, gain_q, gain_k, down, n2, d_gate, d_up, w_out, w_qkv, q, kv, ctx, proj, table, places, n1)
 
 
 def row_positions(flat_lens, ranks, first_row, count):
@@ -981,9 +1109,9 @@
     d_gate = (d_act * up * sg * (1.0 + gate * (1.0 - sg))).astype(BF)
     d_up = (d_act * silu).astype(BF)
 
-    input_grad, output, gain_sums, g_mlp, g_attn, _ = back(
+    input_grad, output, gain_sums, g_mlp, g_attn, _, _, _ = back(
         n_fsdp, n_replica, (dot_cols(d_gate, gate_c) + dot_cols(d_up, up_c)).astype(BF), part_y, tokens, h, cotangent, *gains,
-        dot_rows(g_all, act).astype(BF), dot_rows(n2, d_gate).astype(BF), dot_rows(n2, d_up).astype(BF),
+        dot_rows(g_all, act).astype(BF), n2, d_gate, d_up,
         w_out, w_qkv_c, q_low, kv_window, ctx_low, proj, table, places, n1)
     wide = qw + 2 * HEAD_WIDTH
     g_out = g_attn[:, :width]

time: 694 us -> 659 us (0.950)
  Pallas kernels: 599 us -> 575 us
  matrix products: 68.1 us -> 56.1 us
    pallas_call x1, Pallas kernels: 233 us -> 213 us  [front(): pl.pallas_call(functools.partial(front_kernel, n, n_z), out_shape=(shape(...]
    dot_general x3 -> x1, matrix products: 21.9 us -> 10.1 us  [dot_rows(): lax.dot_general(left, right, (((0,), (0,)), ((), ())), preferred_element_...]
where the time goes in v6:
time: 659 us; the launch traced here: 654 us
  Pallas kernels  575 us (87%)
  matrix products  56.1 us (9%)
  other arithmetic  13.2 us (2%)
  local copies, waits for them, and re-layouts  8.7 us (1%)
    pallas_call x1, Pallas kernels, back(): pl.pallas_call(functools.partial(back_kernel, n, n_z), out_shape=(jax.Sha...  362 us
    pallas_call x1, Pallas kernels, front(): pl.pallas_call(functools.partial(front_kernel, n, n_z), out_shape=(shape(...  213 us
    dot_general x3, matrix products, dot(): return jnp.dot(left, right, preferred_element_type=F32)  26.4 us
    dot_general x3, matrix products, dot_cols(): lax.dot_general(left, right, (((1,), (1,)), ((), ())), preferred_element_...  19.6 us

profile of v6, /device:TPU:0, one launch (start us, length us, event | category | flops | bytes accessed | tf_op | source)
XLA Modules:
  0.0 654.0 jit_solution(16536331371820468461)
XLA Ops:
  0.6 0.8 mul.35
  1.4 0.8 select_reduce_fusion.1
  2.2 0.1 select_reduce_fusion
  2.3 0.7 broadcast_in_dim.36.place_ref
  3.1 212.9 %front.1 = (f32[192,2048]{1,0:T(8,128)}, bf16[1536,256]{1,0:T(8,128)(2,1)}, bf16[8,288,256]{2,1,0:T(8,128)(2,1)}, bf16[1536,256]{1,0:T(8,128)(2,1)}, f32[1536,38...) custom-call(bf16[192,2048]{1,0:T(8,128)(2,1)} %x_ref.3, ...), custom_call_target="tpu_custom_call" | custom-call | tf_op jit(solution)/shard_map/front/pallas_call | solution.py:1011
  216.0 0.0 copy-start.1
  216.0 0.0 copy-start.8
  216.0 9.6 %fusion.2 = f32[1536,768]{1,0:T(8,128)} fusion(bf16[1536,2048]{1,0:T(8,128)(2,1)} %get-tuple-element.29, bf16[2048,768]{1,0:T(8,128)(2,1)} %get-tuple-element.30), kind=kOutput, calls=%fused_computation.43 | convolution fusion | flops 4831838208 | bytes 14155776 | tf_op jit(solution)/shard_map/dot_general | solution.py:34
  225.6 0.0 copy-done.1
  225.6 0.0 copy-done.8
  225.6 0.0 copy-start.7
  225.6 0.0 slice-start
  225.6 6.6 %fusion.3 = f32[1536,768]{1,0:T(8,128)} fusion(bf16[1536,2048]{1,0:T(8,128)(2,1)S(1)} %copy-done.1, bf16[2048,768]{1,0:T(8,128)(2,1)S(1)} %copy-done.8), kind=kOutput, calls=%fused_computation.44 | convolution fusion | flops 4831838208 | bytes 14155776 | tf_op jit(solution)/shard_map/dot_general | solution.py:34
  232.3 0.0 copy-done.7
  232.3 0.0 slice-start.1
  232.3 10.1 %multiply_convert_fusion = (bf16[1536,768]{1,0:T(8,128)(2,1)}, bf16[1536,768]{1,0:T(8,128)(2,1)S(1)}, bf16[1536,768]{1,0:T(8,128)(2,1)S(1)}) fusion(f32[1536,768]{1,0:T(8,128)} %fusion.3, f32[1536,768]{1,0:T(8,128)} %fusion.2, bf16[1536,2048]{1,0:T(8,128)(2,1)S(1)} %copy-done.1, bf16[2048,768]{1,0:T(8,128)(2,1)S(1)} %copy-done.7), kind=kOutput, calls=%fused_computation.2 | convolution fusion | flops 4849532928 | bytes 25952256 | tf_op jit(solution)/shard_map/dot_general | solution.py:34
  242.4 0.0 copy-start.3
  242.4 0.0 copy-start.4
  242.4 0.0 slice-done
  242.4 0.0 slice-done.1
  242.4 0.0 copy-start.9
  242.4 0.0 copy-start.10
  242.4 10.1 %convolution_convert_fusion.1.down_ref = bf16[2048,768]{1,0:T(8,128)(2,1)} fusion(bf16[1536,2048]{1,0:T(8,128)(2,1)S(1)} %bitcast.46, bf16[1536,768]{1,0:T(8,128)(2,1)} %get-tuple-element.50), kind=kOutput, calls=%fused_computation.7 | convolution fusion | flops 4833411072 | bytes 11796480 | tf_op jit(solution)/shard_map/dot_general | solution.py:38
  252.5 0.0 copy-done.9
  252.5 0.0 copy-done.10
  252.5 7.2 %convolution_convert_fusion.party_ref = bf16[1536,2048]{1,0:T(8,128)(2,1)} fusion(bf16[1536,768]{1,0:T(8,128)(2,1)S(1)} %copy-done.10, bf16[2048,768]{1,0:T(8,128)(2,1)S(1)} %copy-done.9), kind=kOutput, calls=%fused_computation.1 | convolution fusion | flops 4834983936 | bytes 11796480 | tf_op jit(solution)/shard_map/dot_general | solution.py:42
  259.7 0.0 copy-done.3
  259.7 5.1 fusion.4
  264.8 0.0 copy-done.4
  264.8 7.3 %add_convert_fusion.part_ref = bf16[1536,2048]{1,0:T(8,128)(2,1)} fusion(f32[1536,2048]{1,0:T(8,128)S(1)} %fusion.4, bf16[1536,768]{1,0:T(8,128)(2,1)S(1)} %get-tuple-element.52.dup_ref, bf16[2048,768]{1,0:T(8,128)(2,1)S(1)} %copy-done.7), kind=kOutput, calls=%fused_computation | convolution fusion | flops 4838129664 | bytes 24379392 | tf_op jit(solution)/shard_map/dot_general | solution.py:42
  272.2 362.0 %back.1 = (bf16[192,2048]{1,0:T(8,128)(2,1)}, bf16[192,2048]{1,0:T(8,128)(2,1)}, f32[8,2048]{1,0:T(8,128)}, bf16[3,256,6144]{2,1,0:T(8,128)(2,1)}, bf16[256,6144...) custom-call(bf16[1536,2048]{1,0:T(8,128)(2,1)} %add_convert_fusion.part_ref, ...), custom_call_target="tpu_custom_call" | custom-call | tf_op jit(solution)/shard_map/back/pallas_call | solution.py:1039
  634.1 0.0 copy-start.2
  634.1 1.4 slice_bitcast_fusion
  635.5 1.5 fusion.1
  637.0 2.8 slice_convert_fusion
  639.8 0.0 copy-done.2
  639.9 0.0 copy-start
  640.6 2.6 concatenate.7
  643.2 1.9 copy-done
  645.1 0.0 copy-start.6
  645.1 0.0 copy-start.5
  645.1 6.9 %bitcast_convert_fusion = (f32[256,6144]{1,0:T(8,128)}, f32[256,6144]{1,0:T(8,128)}, f32[256,6144]{1,0:T(8,128)}) fusion(bf16[3,256,6144]{2,1,0:T(8,128)(2,1)S(1)} %copy-done), kind=kLoop, calls=%fused_computation.8 | loop fusion | flops 4718592 | bytes 28311552 | tf_op jit(solution)/shard_map/convert_element_type | solution.py:1127
  652.0 0.0 copy-done.6
  652.0 0.9 copy.50
  652.9 0.0 copy-done.5
  652.9 0.9 copy.51
  (27 shorter events, 0.7 us)
Async XLA Ops:
  216.0 9.6 %copy-start.1 = (bf16[1536,2048]{1,0:T(8,128)(2,1)S(1)}, bf16[1536,2048]{1,0:T(8,128)(2,1)}, u32[]{:S(2)}) copy-start(bf16[1536,2048]{1,0:T(8,128)(2,1)} %get-tuple-element.31.n2_ref) | copy-start | bytes 18874372
  216.0 9.6 %copy-start.8 = (bf16[2048,768]{1,0:T(8,128)(2,1)S(1)}, bf16[2048,768]{1,0:T(8,128)(2,1)}, u32[]{:S(2)}) copy-start(bf16[2048,768]{1,0:T(8,128)(2,1)} %get-tuple-element.33) | copy-start | bytes 9437188
  225.6 6.7 %copy-start.7 = (bf16[2048,768]{1,0:T(8,128)(2,1)S(1)}, bf16[2048,768]{1,0:T(8,128)(2,1)}, u32[]{:S(2)}) copy-start(bf16[2048,768]{1,0:T(8,128)(2,1)} %get-tuple-element.32) | copy-start | bytes 9437188
  225.6 16.8 %slice-start = ((s8[6291456]{0:T(1024)(128)(4,1)}), s8[4194304]{0:T(1024)(128)(4,1)S(1)}, s32[]{:S(2)}) async-start(s8[6291456]{0:T(1024)(128)(4,1)} %bitcast.45), calls=%async_computation | async-start | bytes 8388608
  232.3 10.1 %slice-start.1 = ((s8[6291456]{0:T(1024)(128)(4,1)}), s8[2097152]{0:T(1024)(128)(4,1)S(1)}, s32[]{:S(2)}) async-start(s8[6291456]{0:T(1024)(128)(4,1)} %bitcast.45), calls=%async_computation.1 | async-start | bytes 4194304
  242.4 17.3 %copy-start.3 = (bf16[1536,768]{1,0:T(8,128)(2,1)}, bf16[1536,768]{1,0:T(8,128)(2,1)S(1)}, u32[]{:S(2)}) copy-start(bf16[1536,768]{1,0:T(8,128)(2,1)S(1)} %get-tuple-element.51.dgate_ref) | copy-start | bytes 7077892
  242.4 22.4 %copy-start.4 = (bf16[1536,768]{1,0:T(8,128)(2,1)}, bf16[1536,768]{1,0:T(8,128)(2,1)S(1)}, u32[]{:S(2)}) copy-start(bf16[1536,768]{1,0:T(8,128)(2,1)S(1)} %get-tuple-element.52.dup_ref) | copy-start | bytes 7077892
  242.4 10.1 %copy-start.9 = (bf16[2048,768]{1,0:T(8,128)(2,1)S(1)}, bf16[2048,768]{1,0:T(8,128)(2,1)}, u32[]{:S(2)}) copy-start(bf16[2048,768]{1,0:T(8,128)(2,1)} %get-tuple-element.30) | copy-start | bytes 9437188
  242.4 10.1 %copy-start.10 = (bf16[1536,768]{1,0:T(8,128)(2,1)S(1)}, bf16[1536,768]{1,0:T(8,128)(2,1)}, u32[]{:S(2)}) copy-start(bf16[1536,768]{1,0:T(8,128)(2,1)} %get-tuple-element.50) | copy-start | bytes 7077892
  634.1 5.7 copy-start.2
  639.9 5.2 copy-start
  645.1 6.9 %copy-start.6 = (bf16[192,2048]{1,0:T(8,128)(2,1)S(1)}, bf16[192,2048]{1,0:T(8,128)(2,1)}, u32[]{:S(2)}) copy-start(bf16[192,2048]{1,0:T(8,128)(2,1)} %get-tuple-element.68) | copy-start | bytes 2359300
  645.1 7.8 %copy-start.5 = (bf16[192,2048]{1,0:T(8,128)(2,1)S(1)}, bf16[192,2048]{1,0:T(8,128)(2,1)}, u32[]{:S(2)}) copy-start(bf16[192,2048]{1,0:T(8,128)(2,1)} %get-tuple-element.69) | copy-start | bytes 2359300

commit v7 on v6

--- a/solution.py
+++ b/solution.py
@@ -433,18 +433,17 @@
 
 
 class Weights:
-    def __init__(self, at, pairs, send, recv, z_send, z_recv):
-        self.at, self.pairs, self.send, self.recv, self.z_send, self.z_recv = at, pairs, send, recv, z_send, z_recv
-        self.depth, self.share = pairs[0][0].shape[0], pairs[0][1].shape[1]
+    def __init__(self, at, pieces, send, recv, z_send, z_recv):
+        self.at, self.pieces, self.send, self.recv, self.z_send, self.z_recv = at, pieces, send, recv, z_send, z_recv
         self.mine = at.core == lax.rem(at.z, 2)
         self.parity = lax.rem(at.z + at.core, 2)
         self.partner = at.z + 1 - 2 * lax.rem(at.z, 2)
 
     def cols(self, i, t):
-        return self.pairs[i][0].at[:, pl.ds(pl.multiple_of(t * self.share, HEAD_WIDTH), self.share)]
+        return self.pieces[i][0](t)
 
     def rows(self, i, s):
-        return self.pairs[i][1].at[pl.ds(pl.multiple_of(s * self.depth, self.depth), self.depth)]
+        return self.pieces[i][1](s)
 
     def local(self, i):
         return pltpu.make_async_copy(self.cols(i, self.at.f), self.rows(i, self.at.f), self.recv.at[i, 0])
@@ -492,20 +491,25 @@
                  h_ref, q_ref, kv_ref, ctx_ref, proj_ref, places_ref,
                  n1_ref, wc_ref, n2_ref, gall_ref, gate_c, up_c, down_c,
                  near, mine, far, stage, own, n1_block, wc,
-                 s_x, r_x, s_p, r_p, s_g, s_n, s_w, s_h, s_r, s_a, s_b, s_c, r_c, s_z, r_z):
+                 s_x, r_x, s_p, r_p, s_g, s_n, s_w, s_h, s_r, s_a, s_b, s_c, r_c, s_z, r_z, s_xz, r_xz):
     at = Place(n, n_z)
     rows = x_ref.shape[0]
     heads = QUERY_HEADS // n
     qw = heads * HEAD_WIDTH
     halo = LMAX
     at.greet(True)
-    weights = Exchange(at, qkv_pieces(at, wqkv_ref, wc_ref, qw), s_x, r_x)
+    weights = Weights(at, qkv_pieces(at, wqkv_ref, wc_ref, qw), s_x, r_x, s_xz, r_xz)
+    for i in range(3):
+        weights.start(i)
 
     def rows_of(g):
         return pl.ds(pl.multiple_of(g * rows, rows), rows)
 
     places = Exchange(at, [(lambda t: place_ref, lambda s: places_ref.at[rows_of(s)])], s_p, r_p)
-    mlp = Weights(at, [(gate_ref, gate_c), (up_ref, up_c), (down_ref, down_c)], s_c, r_c, s_z, r_z)
+    share = gate_c.shape[1]
+    mlp = Weights(
+        at, [col_piece(gate_ref, gate_c, share), col_piece(up_ref, up_c, share), col_piece(down_ref, down_c, share)],
+        s_c, r_c, s_z, r_z)
     places.start()
 
     def norm1(strip):
@@ -515,12 +519,14 @@
     strips(rows, norm1)
     n1 = gather_rows(at, own, n1_ref, s_g)
     n1.start()
-    weights.start()
     n1.relay()
+    for i in range(3):
+        weights.hand_over(i)
     n1.forward()
     n1.wait()
     places.wait()
-    weights.wait()
+    for i in range(3):
+        weights.wait(i)
     mlp.start(0)
     mlp.start(1)
     to_vmem = pltpu.make_async_copy(wc_ref, wc, s_w.at[0])
@@ -1021,7 +1027,8 @@
             block((chips, rows, width)), block((chips, rows, width)), block((chips - 1, rows, width)),
             block((chips, rows, width)), block((rows, width)), block((2, rows, width)), block((width, wide)),
             DMA((3, n)), DMA((3, n)), DMA((1, n)), DMA((1, n)), DMA((6, n)), DMA((2,)), DMA((1,)), DMA((2,)),
-            DMA((5, n)), DMA((6, n)), DMA((6, n)), DMA((3, n)), DMA((3, n)), DMA((3, n)), DMA((3, n))],
+            DMA((5, n)), DMA((6, n)), DMA((6, n)), DMA((3, n)), DMA((3, n)), DMA((3, n)), DMA((3, n)),
+            DMA((3, n)), DMA((3, n))],
         compiler_params=pltpu.CompilerParams(collective_id=0, has_side_effects=True, vmem_limit_bytes=60 << 20),
         name="front",
     )(x, gain1, gain2, gain_q, gain_k, place, table, w_out, w_qkv, g, gate, up, down)

time: 659 us -> 649 us (0.985)
  Pallas kernels: 575 us -> 564 us
    pallas_call x1, Pallas kernels: 213 us -> 202 us  [front(): pl.pallas_call(functools.partial(front_kernel, n, n_z), out_shape=(shape(...]
where the time goes in v7:
time: 649 us; the launch traced here: 644 us
  Pallas kernels  564 us (87%)
  matrix products  56.1 us (9%)
  other arithmetic  13.2 us (2%)
  local copies, waits for them, and re-layouts  8.7 us (1%)
    pallas_call x1, Pallas kernels, back(): pl.pallas_call(functools.partial(back_kernel, n, n_z), out_shape=(jax.Sha...  362 us
    pallas_call x1, Pallas kernels, front(): pl.pallas_call(functools.partial(front_kernel, n, n_z), out_shape=(shape(...  202 us
    dot_general x3, matrix products, dot(): return jnp.dot(left, right, preferred_element_type=F32)  26.4 us
    dot_general x3, matrix products, dot_cols(): lax.dot_general(left, right, (((1,), (1,)), ((), ())), preferred_element_...  19.6 us

profile of v7, /device:TPU:0, one launch (start us, length us, event | category | flops | bytes accessed | tf_op | source)
XLA Modules:
  0.0 643.6 jit_solution(2861927687400270903)
XLA Ops:
  0.6 0.8 mul.35
  1.4 0.8 select_reduce_fusion.1
  2.2 0.1 select_reduce_fusion
  2.3 0.7 broadcast_in_dim.36.place_ref
  3.1 202.1 %front.1 = (f32[192,2048]{1,0:T(8,128)}, bf16[1536,256]{1,0:T(8,128)(2,1)}, bf16[8,288,256]{2,1,0:T(8,128)(2,1)}, bf16[1536,256]{1,0:T(8,128)(2,1)}, f32[1536,38...) custom-call(bf16[192,2048]{1,0:T(8,128)(2,1)} %x_ref.3, ...), custom_call_target="tpu_custom_call" | custom-call | tf_op jit(solution)/shard_map/front/pallas_call | solution.py:1017
  205.2 0.0 copy-start.1
  205.2 0.0 copy-start.8
  205.2 9.6 %fusion.2 = f32[1536,768]{1,0:T(8,128)} fusion(bf16[1536,2048]{1,0:T(8,128)(2,1)} %get-tuple-element.29, bf16[2048,768]{1,0:T(8,128)(2,1)} %get-tuple-element.30), kind=kOutput, calls=%fused_computation.43 | convolution fusion | flops 4831838208 | bytes 14155776 | tf_op jit(solution)/shard_map/dot_general | solution.py:34
  214.8 0.0 copy-done.1
  214.8 0.0 copy-done.8
  214.8 0.0 copy-start.7
  214.8 0.0 slice-start
  214.8 6.6 %fusion.3 = f32[1536,768]{1,0:T(8,128)} fusion(bf16[1536,2048]{1,0:T(8,128)(2,1)S(1)} %copy-done.1, bf16[2048,768]{1,0:T(8,128)(2,1)S(1)} %copy-done.8), kind=kOutput, calls=%fused_computation.44 | convolution fusion | flops 4831838208 | bytes 14155776 | tf_op jit(solution)/shard_map/dot_general | solution.py:34
  221.4 0.0 copy-done.7
  221.4 0.0 slice-start.1
  221.4 10.1 %multiply_convert_fusion = (bf16[1536,768]{1,0:T(8,128)(2,1)}, bf16[1536,768]{1,0:T(8,128)(2,1)S(1)}, bf16[1536,768]{1,0:T(8,128)(2,1)S(1)}) fusion(f32[1536,768]{1,0:T(8,128)} %fusion.3, f32[1536,768]{1,0:T(8,128)} %fusion.2, bf16[1536,2048]{1,0:T(8,128)(2,1)S(1)} %copy-done.1, bf16[2048,768]{1,0:T(8,128)(2,1)S(1)} %copy-done.7), kind=kOutput, calls=%fused_computation.2 | convolution fusion | flops 4849532928 | bytes 25952256 | tf_op jit(solution)/shard_map/dot_general | solution.py:34
  231.6 0.0 copy-start.3
  231.6 0.0 copy-start.4
  231.6 0.0 slice-done
  231.6 0.0 slice-done.1
  231.6 0.0 copy-start.9
  231.6 0.0 copy-start.10
  231.6 10.1 %convolution_convert_fusion.1.down_ref = bf16[2048,768]{1,0:T(8,128)(2,1)} fusion(bf16[1536,2048]{1,0:T(8,128)(2,1)S(1)} %bitcast.46, bf16[1536,768]{1,0:T(8,128)(2,1)} %get-tuple-element.50), kind=kOutput, calls=%fused_computation.7 | convolution fusion | flops 4833411072 | bytes 11796480 | tf_op jit(solution)/shard_map/dot_general | solution.py:38
  241.7 0.0 copy-done.9
  241.7 0.0 copy-done.10
  241.7 7.2 %convolution_convert_fusion.party_ref = bf16[1536,2048]{1,0:T(8,128)(2,1)} fusion(bf16[1536,768]{1,0:T(8,128)(2,1)S(1)} %copy-done.10, bf16[2048,768]{1,0:T(8,128)(2,1)S(1)} %copy-done.9), kind=kOutput, calls=%fused_computation.1 | convolution fusion | flops 4834983936 | bytes 11796480 | tf_op jit(solution)/shard_map/dot_general | solution.py:42
  248.9 0.0 copy-done.3
  248.9 5.1 fusion.4
  254.0 0.0 copy-done.4
  254.0 7.3 %add_convert_fusion.part_ref = bf16[1536,2048]{1,0:T(8,128)(2,1)} fusion(f32[1536,2048]{1,0:T(8,128)S(1)} %fusion.4, bf16[1536,768]{1,0:T(8,128)(2,1)S(1)} %get-tuple-element.52.dup_ref, bf16[2048,768]{1,0:T(8,128)(2,1)S(1)} %copy-done.7), kind=kOutput, calls=%fused_computation | convolution fusion | flops 4838129664 | bytes 24379392 | tf_op jit(solution)/shard_map/dot_general | solution.py:42
  261.4 362.3 %back.1 = (bf16[192,2048]{1,0:T(8,128)(2,1)}, bf16[192,2048]{1,0:T(8,128)(2,1)}, f32[8,2048]{1,0:T(8,128)}, bf16[3,256,6144]{2,1,0:T(8,128)(2,1)}, bf16[256,6144...) custom-call(bf16[1536,2048]{1,0:T(8,128)(2,1)} %add_convert_fusion.part_ref, ...), custom_call_target="tpu_custom_call" | custom-call | tf_op jit(solution)/shard_map/back/pallas_call | solution.py:1046
  623.7 0.0 copy-start.2
  623.7 1.4 slice_bitcast_fusion
  625.1 1.5 fusion.1
  626.6 2.8 slice_convert_fusion
  629.4 0.0 copy-done.2
  629.4 0.0 copy-start
  630.1 2.6 concatenate.7
  632.8 1.9 copy-done
  634.6 0.0 copy-start.6
  634.6 0.0 copy-start.5
  634.6 6.9 %bitcast_convert_fusion = (f32[256,6144]{1,0:T(8,128)}, f32[256,6144]{1,0:T(8,128)}, f32[256,6144]{1,0:T(8,128)}) fusion(bf16[3,256,6144]{2,1,0:T(8,128)(2,1)S(1)} %copy-done), kind=kLoop, calls=%fused_computation.8 | loop fusion | flops 4718592 | bytes 28311552 | tf_op jit(solution)/shard_map/convert_element_type | solution.py:1134
  641.5 0.0 copy-done.6
  641.5 0.9 copy.50
  642.4 0.0 copy-done.5
  642.4 0.9 copy.51
  (27 shorter events, 0.7 us)
Async XLA Ops:
  205.2 9.6 %copy-start.1 = (bf16[1536,2048]{1,0:T(8,128)(2,1)S(1)}, bf16[1536,2048]{1,0:T(8,128)(2,1)}, u32[]{:S(2)}) copy-start(bf16[1536,2048]{1,0:T(8,128)(2,1)} %get-tuple-element.31.n2_ref) | copy-start | bytes 18874372
  205.2 9.6 %copy-start.8 = (bf16[2048,768]{1,0:T(8,128)(2,1)S(1)}, bf16[2048,768]{1,0:T(8,128)(2,1)}, u32[]{:S(2)}) copy-start(bf16[2048,768]{1,0:T(8,128)(2,1)} %get-tuple-element.33) | copy-start | bytes 9437188
  214.8 6.7 %copy-start.7 = (bf16[2048,768]{1,0:T(8,128)(2,1)S(1)}, bf16[2048,768]{1,0:T(8,128)(2,1)}, u32[]{:S(2)}) copy-start(bf16[2048,768]{1,0:T(8,128)(2,1)} %get-tuple-element.32) | copy-start | bytes 9437188
  214.8 16.8 %slice-start = ((s8[6291456]{0:T(1024)(128)(4,1)}), s8[4194304]{0:T(1024)(128)(4,1)S(1)}, s32[]{:S(2)}) async-start(s8[6291456]{0:T(1024)(128)(4,1)} %bitcast.45), calls=%async_computation | async-start | bytes 8388608
  221.4 10.1 %slice-start.1 = ((s8[6291456]{0:T(1024)(128)(4,1)}), s8[2097152]{0:T(1024)(128)(4,1)S(1)}, s32[]{:S(2)}) async-start(s8[6291456]{0:T(1024)(128)(4,1)} %bitcast.45), calls=%async_computation.1 | async-start | bytes 4194304
  231.6 17.3 %copy-start.3 = (bf16[1536,768]{1,0:T(8,128)(2,1)}, bf16[1536,768]{1,0:T(8,128)(2,1)S(1)}, u32[]{:S(2)}) copy-start(bf16[1536,768]{1,0:T(8,128)(2,1)S(1)} %get-tuple-element.51.dgate_ref) | copy-start | bytes 7077892
  231.6 22.4 %copy-start.4 = (bf16[1536,768]{1,0:T(8,128)(2,1)}, bf16[1536,768]{1,0:T(8,128)(2,1)S(1)}, u32[]{:S(2)}) copy-start(bf16[1536,768]{1,0:T(8,128)(2,1)S(1)} %get-tuple-element.52.dup_ref) | copy-start | bytes 7077892
  231.6 10.1 %copy-start.9 = (bf16[2048,768]{1,0:T(8,128)(2,1)S(1)}, bf16[2048,768]{1,0:T(8,128)(2,1)}, u32[]{:S(2)}) copy-start(bf16[2048,768]{1,0:T(8,128)(2,1)} %get-tuple-element.30) | copy-start | bytes 9437188
  231.6 10.1 %copy-start.10 = (bf16[1536,768]{1,0:T(8,128)(2,1)S(1)}, bf16[1536,768]{1,0:T(8,128)(2,1)}, u32[]{:S(2)}) copy-start(bf16[1536,768]{1,0:T(8,128)(2,1)} %get-tuple-element.50) | copy-start | bytes 7077892
  623.7 5.7 copy-start.2
  629.4 5.2 copy-start
  634.6 6.9 %copy-start.6 = (bf16[192,2048]{1,0:T(8,128)(2,1)S(1)}, bf16[192,2048]{1,0:T(8,128)(2,1)}, u32[]{:S(2)}) copy-start(bf16[192,2048]{1,0:T(8,128)(2,1)} %get-tuple-element.68) | copy-start | bytes 2359300
  634.6 7.8 %copy-start.5 = (bf16[192,2048]{1,0:T(8,128)(2,1)S(1)}, bf16[192,2048]{1,0:T(8,128)(2,1)}, u32[]{:S(2)}) copy-start(bf16[192,2048]{1,0:T(8,128)(2,1)} %get-tuple-element.69) | copy-start | bytes 2359300

commit v8 on v7

--- a/solution.py
+++ b/solution.py
@@ -426,10 +426,10 @@
     ]
 
 
-def col_piece(w, wc, share):
+def col_piece(w, wc, share, first=0):
     depth = w.shape[0]
     return (lambda t: w.at[:, pl.ds(pl.multiple_of(t * share, HEAD_WIDTH), share)],
-            lambda s: wc.at[pl.ds(pl.multiple_of(s * depth, depth), depth)])
+            lambda s: wc.at[pl.ds(pl.multiple_of(s * depth, depth), depth), pl.ds(first, share)])
 
 
 class Weights:
@@ -489,7 +489,7 @@
 def front_kernel(n, n_z, x_ref, gain1_ref, gain2_ref, gainq_ref, gaink_ref, place_ref, table_ref, wout_ref,
                  wqkv_ref, g_ref, gate_ref, up_ref, down_ref,
                  h_ref, q_ref, kv_ref, ctx_ref, proj_ref, places_ref,
-                 n1_ref, wc_ref, n2_ref, gall_ref, gate_c, up_c, down_c,
+                 n1_ref, wc_ref, n2_ref, gall_ref, pair_c, down_c,
                  near, mine, far, stage, own, n1_block, wc,
                  s_x, r_x, s_p, r_p, s_g, s_n, s_w, s_h, s_r, s_a, s_b, s_c, r_c, s_z, r_z, s_xz, r_xz):
     at = Place(n, n_z)
@@ -506,9 +506,9 @@
         return pl.ds(pl.multiple_of(g * rows, rows), rows)
 
     places = Exchange(at, [(lambda t: place_ref, lambda s: places_ref.at[rows_of(s)])], s_p, r_p)
-    share = gate_c.shape[1]
+    share = down_c.shape[1]
     mlp = Weights(
-        at, [col_piece(gate_ref, gate_c, share), col_piece(up_ref, up_c, share), col_piece(down_ref, down_c, share)],
+        at, [col_piece(gate_ref, pair_c, share), col_piece(up_ref, pair_c, share, share), col_piece(down_ref, down_c, share)],
         s_c, r_c, s_z, r_z)
     places.start()
 
@@ -716,7 +716,7 @@
 
 
 def back_kernel(n, n_z, part_ref, party_ref, x_ref, h_ref, g_ref, gain1_ref, gain2_ref, gainq_ref, gaink_ref,
-                down_ref, n2_ref, dgate_ref, dup_ref, wout_ref, wqkv_ref, q_ref, kv_ref, ctx_ref, proj_ref, table_ref, place_ref,
+                down_ref, n2_ref, dpair_ref, wout_ref, wqkv_ref, q_ref, kv_ref, ctx_ref, proj_ref, table_ref, place_ref,
                 n1_ref,
                 dx_ref, y_ref, gains_ref, gmlp_ref, gqkv_ref, dhall_ref, gate_ref, up_ref,
                 near, mine, far, stage, dh, plane_gain, all_gain,
@@ -751,7 +751,7 @@
     for c in range(LEAD):
         feed.start(jnp.int32(c))
     sum_n2.start()
-    load = pltpu.make_async_copy(dgate_ref, d_in, s_e.at[0])
+    load = pltpu.make_async_copy(dpair_ref.at[:, pl.ds(0, share)], d_in, s_e.at[0])
     load.start()
     lines.run(1)
     sum_n2.forward()
@@ -801,7 +801,7 @@
     body, end = tiles(gate_ref, per_tile)
     lines.run(3, body)
     end()
-    load = pltpu.make_async_copy(dup_ref, d_in, s_e.at[0])
+    load = pltpu.make_async_copy(dpair_ref.at[:, pl.ds(share, share)], d_in, s_e.at[0])
     load.start()
     lines.run(n - 8)
     sum_n2.wait()
@@ -1020,9 +1020,9 @@
             shape((rows, width), F32), shape((total, qw), BF), shape((n, LMAX + rows, 2 * HEAD_WIDTH), BF),
             shape((total, qw), BF), shape((total, qw + HEAD_WIDTH), F32), shape((total, HEAD_WIDTH), BF),
             shape((total, width), BF), shape((width, wide), BF), shape((total, width), BF), shape((total, width), BF),
-        ) + (shape((width, share), BF),) * 3,
+        ) + (shape((width, 2 * share), BF), shape((width, share), BF)),
         in_specs=[VMEM] * 8 + [ANY] * 5,
-        out_specs=(VMEM,) * 6 + (ANY,) * 7,
+        out_specs=(VMEM,) * 6 + (ANY,) * 6,
         scratch_shapes=[
             block((chips, rows, width)), block((chips, rows, width)), block((chips - 1, rows, width)),
             block((chips, rows, width)), block((rows, width)), block((2, rows, width)), block((width, wide)),
@@ -1034,7 +1034,7 @@
     )(x, gain1, gain2, gain_q, gain_k, place, table, w_out, w_qkv, g, gate, up, down)
 
 
-def back(n, n_z, part, part_y, x, h, g, gain1, gain2, gain_q, gain_k, down, n2, d_gate, d_up, w_out, w_qkv, q, kv, ctx, proj,
+def back(n, n_z, part, part_y, x, h, g, gain1, gain2, gain_q, gain_k, down, n2, d_pair, w_out, w_qkv, q, kv, ctx, proj,
          table, places, n1):
     rows, width = x.shape
     chips, share, wide, depth = n // 2, down.shape[1], w_qkv.shape[1], width // n
@@ -1055,7 +1055,7 @@
             jax.ShapeDtypeStruct((width, share), BF),
             jax.ShapeDtypeStruct((width, share), BF),
         ),
-        in_specs=[ANY, ANY] + [VMEM] * 7 + [ANY] * 4 + [VMEM] * 8 + [ANY],
+        in_specs=[ANY, ANY] + [VMEM] * 7 + [ANY] * 3 + [VMEM] * 8 + [ANY],
         out_specs=(VMEM, VMEM, VMEM, ANY, ANY, ANY, ANY, ANY),
         scratch_shapes=[
             block((chips, rows, width)), block((chips, rows, width)), block((chips - 1, rows, width)),
@@ -1073,7 +1073,7 @@
             pltpu.SemaphoreType.REGULAR((2,)), pltpu.SemaphoreType.REGULAR, DMA((1,)), DMA((2,)), DMA((2,)), DMA((1,)), DMA((2,))],
         compiler_params=pltpu.CompilerParams(collective_id=2, has_side_effects=True, vmem_limit_bytes=511 << 17),
         name="back",
-    )(part, part_y, x, h, g, gain1, gain2, gain_q, gain_k, down, n2, d_gate, d_up, w_out, w_qkv, q, kv, ctx, proj, table, places, n1)
+    )(part, part_y, x, h, g, gain1, gain2, gain_q, gain_k, down, n2, d_pair, w_out, w_qkv, q, kv, ctx, proj, table, places, n1)
 
 
 def row_positions(flat_lens, ranks, first_row, count):
@@ -1102,23 +1102,23 @@
     place = jnp.broadcast_to(pos.astype(BF)[:, None], (rows, HEAD_WIDTH))
     table = rotation_table()
     gains = (gain_attn[None], gain_mlp[None], gain_query[None], gain_key[None])
-    h, q_low, kv_window, ctx_low, proj, places, n1, w_qkv_c, n2, g_all, gate_c, up_c, down_c = front(
+    h, q_low, kv_window, ctx_low, proj, places, n1, w_qkv_c, n2, g_all, pair_c, down_c = front(
         n_fsdp, n_replica, tokens, *gains, place, table, w_out, w_qkv, cotangent, w_gate, w_up, w_down_t)
 
-    gate = dot(n2, gate_c)
-    up = dot(n2, up_c)
+    both = dot(n2, pair_c)
+    share = down_c.shape[1]
+    gate, up = both[:, :share], both[:, share:]
     sg = jax.nn.sigmoid(gate)
     silu = gate * sg
     act = (silu * up).astype(BF)
     part_y = dot_cols(act, down_c).astype(BF)
 
     d_act = dot(g_all, down_c)
-    d_gate = (d_act * up * sg * (1.0 + gate * (1.0 - sg))).astype(BF)
-    d_up = (d_act * silu).astype(BF)
+    d_pair = jnp.concatenate([d_act * up * sg * (1.0 + gate * (1.0 - sg)), d_act * silu], axis=1).astype(BF)
 
     input_grad, output, gain_sums, g_mlp, g_attn, _, _, _ = back(
-        n_fsdp, n_replica, (dot_cols(d_gate, gate_c) + dot_cols(d_up, up_c)).astype(BF), part_y, tokens, h, cotangent, *gains,
-        dot_rows(g_all, act).astype(BF), n2, d_gate, d_up,
+        n_fsdp, n_replica, dot_cols(d_pair, pair_c).astype(BF), part_y, tokens, h, cotangent, *gains,
+        dot_rows(g_all, act).astype(BF), n2, d_pair,
         w_out, w_qkv_c, q_low, kv_window, ctx_low, proj, table, places, n1)
     wide = qw + 2 * HEAD_WIDTH
     g_out = g_attn[:, :width]

time: 649 us -> 644 us (level)
  matrix products: 56.1 us -> 49.3 us
    dot_general x3 -> x2, matrix products: 26.4 us -> 22 us  [dot(): return jnp.dot(left, right, preferred_element_type=F32)]
    dot_general x3 -> x2, matrix products: 19.6 us -> 18.9 us  [dot_cols(): lax.dot_general(left, right, (((1,), (1,)), ((), ())), preferred_element_...]
where the time goes in v8:
time: 644 us; the launch traced here: 639 us
  Pallas kernels  565 us (88%)
  matrix products  49.3 us (8%)
  other arithmetic  15.8 us (2%)
  local copies, waits for them, and re-layouts  8.67 us (1%)
    pallas_call x1, Pallas kernels, back(): pl.pallas_call(functools.partial(back_kernel, n, n_z), out_shape=(jax.Sha...  362 us
    pallas_call x1, Pallas kernels, front(): pl.pallas_call(functools.partial(front_kernel, n, n_z), out_shape=(shape(...  202 us
    dot_general x2, matrix products, dot(): return jnp.dot(left, right, preferred_element_type=F32)  22 us
    dot_general x2, matrix products, dot_cols(): lax.dot_general(left, right, (((1,), (1,)), ((), ())), preferred_element_...  18.9 us

profile of v8, /device:TPU:0, one launch (start us, length us, event | category | flops | bytes accessed | tf_op | source)
XLA Modules:
  0.0 639.4 jit_solution(15414850207877822988)
XLA Ops:
  0.6 0.8 mul.35
  1.4 0.8 select_reduce_fusion.1
  2.2 0.1 select_reduce_fusion
  2.3 0.7 broadcast_in_dim.36.place_ref
  3.1 202.2 %front.1 = (f32[192,2048]{1,0:T(8,128)}, bf16[1536,256]{1,0:T(8,128)(2,1)}, bf16[8,288,256]{2,1,0:T(8,128)(2,1)}, bf16[1536,256]{1,0:T(8,128)(2,1)}, f32[1536,38...) custom-call(bf16[192,2048]{1,0:T(8,128)(2,1)} %x_ref.3, ...), custom_call_target="tpu_custom_call" | custom-call | tf_op jit(solution)/shard_map/front/pallas_call | solution.py:1017
  205.2 0.0 copy-start.5
  205.3 0.0 copy-start.6
  205.3 14.2 %fusion.2 = f32[1536,1536]{1,0:T(8,128)S(1)} fusion(bf16[1536,2048]{1,0:T(8,128)(2,1)} %get-tuple-element.30.n2_ref, bf16[2048,1536]{1,0:T(8,128)(2,1)} %get-tuple-element.31), kind=kOutput, calls=%fused_computation.44 | convolution fusion | flops 9663676416 | bytes 22020096 | tf_op jit(solution)/shard_map/dot_general | solution.py:34
  219.5 0.0 copy-done.5
  219.5 0.0 copy-done.6
  219.5 7.8 %multiply_convert_fusion.2 = (bf16[1536,768]{1,0:T(8,128)(2,1)S(1)}, bf16[1536,768]{1,0:T(8,128)(2,1)S(1)}, bf16[1536,768]{1,0:T(8,128)(2,1)}) fusion(f32[1536,1536]{1,0:T(8,128)S(1)} %fusion.2, bf16[1536,2048]{1,0:T(8,128)(2,1)S(1)} %copy-done.5, bf16[2048,768]{1,0:T(8,128)(2,1)S(1)} %copy-done.6), kind=kOutput, calls=%fused_computation.5 | convolution fusion | flops 4849532928 | bytes 25952256 | tf_op jit(solution)/shard_map/dot_general | solution.py:34
  227.3 0.0 copy-start.4
  227.3 8.3 %convolution_convert_fusion.2.down_ref = bf16[2048,768]{1,0:T(8,128)(2,1)} fusion(bf16[1536,2048]{1,0:T(8,128)(2,1)S(1)} %copy-done.5, bf16[1536,768]{1,0:T(8,128)(2,1)} %get-tuple-element.50), kind=kOutput, calls=%fused_computation.8 | convolution fusion | flops 4833411072 | bytes 11796480 | tf_op jit(solution)/shard_map/dot_general | solution.py:38
  235.7 0.0 copy-done.4
  235.7 11.9 %convolution_convert_fusion.1.part_ref = bf16[1536,2048]{1,0:T(8,128)(2,1)} fusion(bf16[2048,1536]{1,0:T(8,128)(2,1)S(1)} %copy-done.4, bf16[1536,768]{1,0:T(8,128)(2,1)S(1)} %get-tuple-element.46, bf16[1536,768]{1,0:T(8,128)(2,1)S(1)} %get-tuple-element.45), kind=kOutput, calls=%fused_computation.1 | convolution fusion | flops 9676259328 | bytes 17301504 | tf_op jit(solution)/shard_map/dot_general | solution.py:42
  247.6 0.0 copy-start.7
  247.6 2.6 pad_maximum_fusion.dpair_ref
  250.1 0.0 copy-done.7
  250.1 7.0 %convolution_convert_fusion.party_ref = bf16[1536,2048]{1,0:T(8,128)(2,1)} fusion(bf16[1536,768]{1,0:T(8,128)(2,1)S(1)} %copy-done.7, bf16[2048,768]{1,0:T(8,128)(2,1)S(1)} %copy-done.6), kind=kOutput, calls=%fused_computation | convolution fusion | flops 4834983936 | bytes 11796480 | tf_op jit(solution)/shard_map/dot_general | solution.py:42
  257.2 362.4 %back.1 = (bf16[192,2048]{1,0:T(8,128)(2,1)}, bf16[192,2048]{1,0:T(8,128)(2,1)}, f32[8,2048]{1,0:T(8,128)}, bf16[3,256,6144]{2,1,0:T(8,128)(2,1)}, bf16[256,6144...) custom-call(bf16[1536,2048]{1,0:T(8,128)(2,1)} %convolution_convert_fusion.1.p, ...), custom_call_target="tpu_custom_call" | custom-call | tf_op jit(solution)/shard_map/back/pallas_call | solution.py:1046
  619.6 0.0 copy-start.1
  619.6 1.3 slice_bitcast_fusion
  620.9 1.5 fusion.1
  622.5 2.8 slice_convert_fusion
  625.2 0.0 copy-done.1
  625.3 0.0 copy-start
  626.0 2.6 concatenate.12
  628.6 1.9 copy-done
  630.5 0.0 copy-start.3
  630.5 0.0 copy-start.2
  630.5 6.9 %bitcast_convert_fusion = (f32[256,6144]{1,0:T(8,128)}, f32[256,6144]{1,0:T(8,128)}, f32[256,6144]{1,0:T(8,128)}) fusion(bf16[3,256,6144]{2,1,0:T(8,128)(2,1)S(1)} %copy-done), kind=kLoop, calls=%fused_computation.9 | loop fusion | flops 4718592 | bytes 28311552 | tf_op jit(solution)/shard_map/convert_element_type | solution.py:1134
  637.4 0.0 copy-done.3
  637.4 0.9 copy.60
  638.3 0.0 copy-done.2
  638.3 0.9 copy.61
  (26 shorter events, 0.7 us)
Async XLA Ops:
  205.2 14.3 %copy-start.5 = (bf16[1536,2048]{1,0:T(8,128)(2,1)S(1)}, bf16[1536,2048]{1,0:T(8,128)(2,1)}, u32[]{:S(2)}) copy-start(bf16[1536,2048]{1,0:T(8,128)(2,1)} %get-tuple-element.28) | copy-start | bytes 18874372
  205.3 14.3 %copy-start.6 = (bf16[2048,768]{1,0:T(8,128)(2,1)S(1)}, bf16[2048,768]{1,0:T(8,128)(2,1)}, u32[]{:S(2)}) copy-start(bf16[2048,768]{1,0:T(8,128)(2,1)} %get-tuple-element.29) | copy-start | bytes 9437188
  227.3 8.4 %copy-start.4 = (bf16[2048,1536]{1,0:T(8,128)(2,1)S(1)}, bf16[2048,1536]{1,0:T(8,128)(2,1)}, u32[]{:S(2)}) copy-start(bf16[2048,1536]{1,0:T(8,128)(2,1)} %get-tuple-element.31) | copy-start | bytes 18874372
  247.6 2.6 copy-start.7
  619.6 5.7 copy-start.1
  625.3 5.2 copy-start
  630.5 6.9 %copy-start.3 = (bf16[192,2048]{1,0:T(8,128)(2,1)S(1)}, bf16[192,2048]{1,0:T(8,128)(2,1)}, u32[]{:S(2)}) copy-start(bf16[192,2048]{1,0:T(8,128)(2,1)} %get-tuple-element.66) | copy-start | bytes 2359300
  630.5 7.8 %copy-start.2 = (bf16[192,2048]{1,0:T(8,128)(2,1)S(1)}, bf16[192,2048]{1,0:T(8,128)(2,1)}, u32[]{:S(2)}) copy-start(bf16[192,2048]{1,0:T(8,128)(2,1)} %get-tuple-element.67) | copy-start | bytes 2359300

commit v9 on v8

--- a/solution.py
+++ b/solution.py
@@ -716,7 +716,7 @@
 
 
 def back_kernel(n, n_z, part_ref, party_ref, x_ref, h_ref, g_ref, gain1_ref, gain2_ref, gainq_ref, gaink_ref,
-                down_ref, n2_ref, dpair_ref, wout_ref, wqkv_ref, q_ref, kv_ref, ctx_ref, proj_ref, table_ref, place_ref,
+                down_ref, n2_ref, dgate_ref, dup_ref, wout_ref, wqkv_ref, q_ref, kv_ref, ctx_ref, proj_ref, table_ref, place_ref,
                 n1_ref,
                 dx_ref, y_ref, gains_ref, gmlp_ref, gqkv_ref, dhall_ref, gate_ref, up_ref,
                 near, mine, far, stage, dh, plane_gain, all_gain,
@@ -748,10 +748,10 @@
         LineSum(at, chunk, ring, r_c, s_z, r_z, credit.at[0], mlp_place, s_o, 0, feed.start),
         LineSum(at, chunk2, ring2, r_c2, s_z2, r_z2, credit.at[1], attn_place, s_o2, outs))
     sum_n2 = ScatterSum(at, part_ref, near, mine, far, s_r.at[0])
+    sum_n2.start()
     for c in range(LEAD):
         feed.start(jnp.int32(c))
-    sum_n2.start()
-    load = pltpu.make_async_copy(dpair_ref.at[:, pl.ds(0, share)], d_in, s_e.at[0])
+    load = pltpu.make_async_copy(dgate_ref, d_in, s_e.at[0])
     load.start()
     lines.run(1)
     sum_n2.forward()
@@ -801,7 +801,7 @@
     body, end = tiles(gate_ref, per_tile)
     lines.run(3, body)
     end()
-    load = pltpu.make_async_copy(dpair_ref.at[:, pl.ds(share, share)], d_in, s_e.at[0])
+    load = pltpu.make_async_copy(dup_ref, d_in, s_e.at[0])
     load.start()
     lines.run(n - 8)
     sum_n2.wait()
@@ -1034,7 +1034,7 @@
     )(x, gain1, gain2, gain_q, gain_k, place, table, w_out, w_qkv, g, gate, up, down)
 
 
-def back(n, n_z, part, part_y, x, h, g, gain1, gain2, gain_q, gain_k, down, n2, d_pair, w_out, w_qkv, q, kv, ctx, proj,
+def back(n, n_z, part, part_y, x, h, g, gain1, gain2, gain_q, gain_k, down, n2, d_gate, d_up, w_out, w_qkv, q, kv, ctx, proj,
          table, places, n1):
     rows, width = x.shape
     chips, share, wide, depth = n // 2, down.shape[1], w_qkv.shape[1], width // n
@@ -1055,7 +1055,7 @@
             jax.ShapeDtypeStruct((width, share), BF),
             jax.ShapeDtypeStruct((width, share), BF),
         ),
-        in_specs=[ANY, ANY] + [VMEM] * 7 + [ANY] * 3 + [VMEM] * 8 + [ANY],
+        in_specs=[ANY, ANY] + [VMEM] * 7 + [ANY] * 4 + [VMEM] * 8 + [ANY],
         out_specs=(VMEM, VMEM, VMEM, ANY, ANY, ANY, ANY, ANY),
         scratch_shapes=[
             block((chips, rows, width)), block((chips, rows, width)), block((chips - 1, rows, width)),
@@ -1073,7 +1073,7 @@
             pltpu.SemaphoreType.REGULAR((2,)), pltpu.SemaphoreType.REGULAR, DMA((1,)), DMA((2,)), DMA((2,)), DMA((1,)), DMA((2,))],
         compiler_params=pltpu.CompilerParams(collective_id=2, has_side_effects=True, vmem_limit_bytes=511 << 17),
         name="back",
-    )(part, part_y, x, h, g, gain1, gain2, gain_q, gain_k, down, n2, d_pair, w_out, w_qkv, q, kv, ctx, proj, table, places, n1)
+    )(part, part_y, x, h, g, gain1, gain2, gain_q, gain_k, down, n2, d_gate, d_up, w_out, w_qkv, q, kv, ctx, proj, table, places, n1)
 
 
 def row_positions(flat_lens, ranks, first_row, count):
@@ -1114,11 +1114,13 @@
     part_y = dot_cols(act, down_c).astype(BF)
 
     d_act = dot(g_all, down_c)
-    d_pair = jnp.concatenate([d_act * up * sg * (1.0 + gate * (1.0 - sg)), d_act * silu], axis=1).astype(BF)
+    d_gate = (d_act * up * sg * (1.0 + gate * (1.0 - sg))).astype(BF)
+    d_up = (d_act * silu).astype(BF)
+    d_n2 = dot_cols(d_gate, pair_c[:, :share]) + dot_cols(d_up, pair_c[:, share:])
 
     input_grad, output, gain_sums, g_mlp, g_attn, _, _, _ = back(
-        n_fsdp, n_replica, dot_cols(d_pair, pair_c).astype(BF), part_y, tokens, h, cotangent, *gains,
-        dot_rows(g_all, act).astype(BF), n2, d_pair,
+        n_fsdp, n_replica, d_n2.astype(BF), part_y, tokens, h, cotangent, *gains,
+        dot_rows(g_all, act).astype(BF), n2, d_gate, d_up,
         w_out, w_qkv_c, q_low, kv_window, ctx_low, proj, table, places, n1)
     wide = qw + 2 * HEAD_WIDTH
     g_out = g_attn[:, :width]

time: 644 us -> 644 us (level)
    dot_general x2 -> x3, matrix products: 18.9 us -> 19.7 us  [dot_cols(): lax.dot_general(left, right, (((1,), (1,)), ((), ())), preferred_element_...]
where the time goes in v9:
time: 644 us; the launch traced here: 639 us
  Pallas kernels  565 us (88%)
  matrix products  51.2 us (8%)
  other arithmetic  13.2 us (2%)
  local copies, waits for them, and re-layouts  8.69 us (1%)
    pallas_call x1, Pallas kernels, back(): pl.pallas_call(functools.partial(back_kernel, n, n_z), out_shape=(jax.Sha...  362 us
    pallas_call x1, Pallas kernels, front(): pl.pallas_call(functools.partial(front_kernel, n, n_z), out_shape=(shape(...  202 us
    dot_general x2, matrix products, dot(): return jnp.dot(left, right, preferred_element_type=F32)  24.8 us
    dot_general x3, matrix products, dot_cols(): lax.dot_general(left, right, (((1,), (1,)), ((), ())), preferred_element_...  19.7 us

profile of v9, /device:TPU:0, one launch (start us, length us, event | category | flops | bytes accessed | tf_op | source)
XLA Modules:
  0.0 638.8 jit_solution(13166369204290022942)
XLA Ops:
  0.6 0.8 mul.35
  1.4 0.8 select_reduce_fusion.1
  2.2 0.1 select_reduce_fusion
  2.3 0.7 broadcast_in_dim.36.place_ref
  3.1 202.2 %front.1 = (f32[192,2048]{1,0:T(8,128)}, bf16[1536,256]{1,0:T(8,128)(2,1)}, bf16[8,288,256]{2,1,0:T(8,128)(2,1)}, bf16[1536,256]{1,0:T(8,128)(2,1)}, f32[1536,38...) custom-call(bf16[192,2048]{1,0:T(8,128)(2,1)} %x_ref.3, ...), custom_call_target="tpu_custom_call" | custom-call | tf_op jit(solution)/shard_map/front/pallas_call | solution.py:1017
  205.2 0.0 copy-start.6
  205.2 0.0 copy-start.7
  205.2 15.7 %fusion.5 = f32[1536,1536]{1,0:T(8,128)} fusion(bf16[1536,2048]{1,0:T(8,128)(2,1)} %get-tuple-element.30.n2_ref, bf16[2048,1536]{1,0:T(8,128)(2,1)} %get-tuple-element.31), kind=kOutput, calls=%fused_computation.46 | convolution fusion | flops 9663676416 | bytes 22020096 | tf_op jit(solution)/shard_map/dot_general | solution.py:34
  220.9 0.0 copy-done.6
  220.9 0.0 copy-done.7
  221.0 0.0 slice-start
  221.0 9.1 %multiply_convert_fusion.1 = (bf16[1536,768]{1,0:T(8,128)(2,1)S(1)}, bf16[1536,768]{1,0:T(8,128)(2,1)S(1)}, bf16[1536,768]{1,0:T(8,128)(2,1)S(1)}) fusion(f32[1536,1536]{1,0:T(8,128)} %fusion.5, bf16[1536,2048]{1,0:T(8,128)(2,1)S(1)} %copy-done.6, bf16[2048,768]{1,0:T(8,128)(2,1)S(1)} %copy-done.7), kind=kOutput, calls=%fused_computation.3 | convolution fusion | flops 4849532928 | bytes 25952256 | tf_op jit(solution)/shard_map/dot_general | solution.py:34
  230.1 0.0 copy-start.3
  230.1 0.0 copy-start.2
  230.1 0.0 slice-start.1
  230.1 6.7 %convolution_convert_fusion.1.down_ref = bf16[2048,768]{1,0:T(8,128)(2,1)} fusion(bf16[1536,2048]{1,0:T(8,128)(2,1)S(1)} %copy-done.6, bf16[1536,768]{1,0:T(8,128)(2,1)S(1)} %get-tuple-element.50), kind=kOutput, calls=%fused_computation.7 | convolution fusion | flops 4833411072 | bytes 11796480 | tf_op jit(solution)/shard_map/dot_general | solution.py:38
  236.8 7.1 %convolution_convert_fusion.party_ref = bf16[1536,2048]{1,0:T(8,128)(2,1)} fusion(bf16[1536,768]{1,0:T(8,128)(2,1)S(1)} %get-tuple-element.50, bf16[2048,768]{1,0:T(8,128)(2,1)S(1)} %copy-done.7), kind=kOutput, calls=%fused_computation.1 | convolution fusion | flops 4834983936 | bytes 11796480 | tf_op jit(solution)/shard_map/dot_general | solution.py:42
  243.9 0.0 copy-done.3
  243.9 0.0 slice-done
  244.0 0.0 slice-done.1
  244.0 5.2 fusion.2
  249.2 0.0 copy-done.2
  249.2 7.4 %add_convert_fusion.part_ref = bf16[1536,2048]{1,0:T(8,128)(2,1)} fusion(f32[1536,2048]{1,0:T(8,128)S(1)} %fusion.2, bf16[1536,768]{1,0:T(8,128)(2,1)S(1)} %get-tuple-element.45.dup_ref, bf16[2048,1536]{1,0:T(8,128)(2,1)S(1)} %bitcast.42), kind=kOutput, calls=%fused_computation | convolution fusion | flops 4838129664 | bytes 24379392 | tf_op jit(solution)/shard_map/dot_general | solution.py:42
  256.5 362.4 %back.1 = (bf16[192,2048]{1,0:T(8,128)(2,1)}, bf16[192,2048]{1,0:T(8,128)(2,1)}, f32[8,2048]{1,0:T(8,128)}, bf16[3,256,6144]{2,1,0:T(8,128)(2,1)}, bf16[256,6144...) custom-call(bf16[1536,2048]{1,0:T(8,128)(2,1)} %add_convert_fusion.part_ref, ...), custom_call_target="tpu_custom_call" | custom-call | tf_op jit(solution)/shard_map/back/pallas_call | solution.py:1046
  618.9 0.0 copy-start.1
  618.9 1.4 slice_bitcast_fusion
  620.2 1.5 fusion.4
  621.8 2.8 slice_convert_fusion
  624.6 0.0 copy-done.1
  624.6 0.0 copy-start
  625.3 2.6 concatenate.7
  627.9 1.9 copy-done
  629.8 0.0 copy-start.5
  629.8 0.0 copy-start.4
  629.8 6.9 %bitcast_convert_fusion = (f32[256,6144]{1,0:T(8,128)}, f32[256,6144]{1,0:T(8,128)}, f32[256,6144]{1,0:T(8,128)}) fusion(bf16[3,256,6144]{2,1,0:T(8,128)(2,1)S(1)} %copy-done), kind=kLoop, calls=%fused_computation.8 | loop fusion | flops 4718592 | bytes 28311552 | tf_op jit(solution)/shard_map/convert_element_type | solution.py:1136
  636.7 0.0 copy-done.5
  636.7 0.9 copy.50
  637.6 0.0 copy-done.4
  637.6 0.9 copy.51
  (27 shorter events, 0.7 us)
Async XLA Ops:
  205.2 15.7 %copy-start.6 = (bf16[1536,2048]{1,0:T(8,128)(2,1)S(1)}, bf16[1536,2048]{1,0:T(8,128)(2,1)}, u32[]{:S(2)}) copy-start(bf16[1536,2048]{1,0:T(8,128)(2,1)} %get-tuple-element.28) | copy-start | bytes 18874372
  205.2 15.7 %copy-start.7 = (bf16[2048,768]{1,0:T(8,128)(2,1)S(1)}, bf16[2048,768]{1,0:T(8,128)(2,1)}, u32[]{:S(2)}) copy-start(bf16[2048,768]{1,0:T(8,128)(2,1)} %get-tuple-element.29) | copy-start | bytes 9437188
  221.0 23.0 %slice-start = ((s8[6291456]{0:T(1024)(128)(4,1)}), s8[4194304]{0:T(1024)(128)(4,1)S(1)}, s32[]{:S(2)}) async-start(s8[6291456]{0:T(1024)(128)(4,1)} %bitcast.41), calls=%async_computation | async-start | bytes 8388608
  230.1 13.8 %copy-start.3 = (bf16[1536,768]{1,0:T(8,128)(2,1)}, bf16[1536,768]{1,0:T(8,128)(2,1)S(1)}, u32[]{:S(2)}) copy-start(bf16[1536,768]{1,0:T(8,128)(2,1)S(1)} %get-tuple-element.46.dgate_ref) | copy-start | bytes 7077892
  230.1 19.0 %copy-start.2 = (bf16[1536,768]{1,0:T(8,128)(2,1)}, bf16[1536,768]{1,0:T(8,128)(2,1)S(1)}, u32[]{:S(2)}) copy-start(bf16[1536,768]{1,0:T(8,128)(2,1)S(1)} %get-tuple-element.45.dup_ref) | copy-start | bytes 7077892
  230.1 13.8 %slice-start.1 = ((s8[6291456]{0:T(1024)(128)(4,1)}), s8[2097152]{0:T(1024)(128)(4,1)S(1)}, s32[]{:S(2)}) async-start(s8[6291456]{0:T(1024)(128)(4,1)} %bitcast.41), calls=%async_computation.1 | async-start | bytes 4194304
  618.9 5.7 copy-start.1
  624.6 5.2 copy-start
  629.8 6.9 %copy-start.5 = (bf16[192,2048]{1,0:T(8,128)(2,1)S(1)}, bf16[192,2048]{1,0:T(8,128)(2,1)}, u32[]{:S(2)}) copy-start(bf16[192,2048]{1,0:T(8,128)(2,1)} %get-tuple-element.66) | copy-start | bytes 2359300
  629.8 7.8 %copy-start.4 = (bf16[192,2048]{1,0:T(8,128)(2,1)S(1)}, bf16[192,2048]{1,0:T(8,128)(2,1)}, u32[]{:S(2)}) copy-start(bf16[192,2048]{1,0:T(8,128)(2,1)} %get-tuple-element.67) | copy-start | bytes 2359300
